TPU v7x, 256 devices: a whole 4x4x8 slice. The times are simulated.
256 devices in a mesh: tensor: 8 (over z_hi, y), seq: 32 (over x, z_lo, core).
Axes of the slice: x: 4, y: 4, z: 8 (z_hi: 2, z_lo: 4; z = z_hi * 4 + z_lo), core: 2. Of those that a mesh axis runs over, the one named last changes fastest.
Arguments:
- queries: bfloat16 [16, 524288], P('tensor', 'seq'), may hold values from -6 to 6
- key_feats: bfloat16 [16, 524288], P('tensor', 'seq'), may hold values from -6 to 6
- value_feats: bfloat16 [16, 524288], P('tensor', 'seq'), may hold values from -6 to 6
- filter_taps: bfloat16 [16, 524288], P('tensor', 'seq'), may hold values from -1 to 1
- skip_gain: float32 [16], P('tensor'), may hold values from -4 to 4
- out_weight: bfloat16 [16, 16], replicated, may hold values from -1.5 to 1.5
- out_grad: bfloat16 [16, 524288], P('tensor', 'seq'), may hold values from -6 to 6
Outputs:
- output: bfloat16 [16, 524288], P('tensor', 'seq')
- grad_queries: bfloat16 [16, 524288], P('tensor', 'seq')
- grad_keys: bfloat16 [16, 524288], P('tensor', 'seq')
- grad_values: bfloat16 [16, 524288], P('tensor', 'seq')
- grad_taps: float32 [16, 524288], P('tensor', 'seq')
All inputs are finite; a program needn't handle non-finite values.
Results may differ from a plain program's by a relative error of at most 0.015.
Values may be sent and summed in bfloat16 or wider, within the bound.
No kernel may reach another device: no remote copies, remote signals or barrier semaphores. Data moves between devices by JAX's collectives and lax.ppermute only.
A program may use at most 128 MiB of HBM per device.

v0:
```python
import math

import jax
import jax.numpy as jnp
from jax import lax
from jax.sharding import PartitionSpec as P

COLS = 1024


def angle_tables(first_ids, second_ids, period):
    product = first_ids[:, None] * second_ids[None, :] % period
    angles = product.astype(jnp.float32) * (2.0 * math.pi / period)
    return (jnp.cos(angles), jnp.sin(angles))


def split_table(table):
    upper = table.astype(jnp.bfloat16)
    rest = table - upper.astype(jnp.float32)
    middle = rest.astype(jnp.bfloat16)
    lowest = (rest - middle.astype(jnp.float32)).astype(jnp.bfloat16)
    return jnp.stack([upper, middle, lowest])


def first_section(columns, pieces):
    terms = jnp.einsum("scab,pak->pscbk", columns, pieces, preferred_element_type=jnp.float32)
    return terms[0] + terms[1] + terms[2]


def body(queries, key_feats, value_feats, filter_taps, skip_gain, out_weight, out_grad):
    f32 = jnp.float32
    chan_count, tok_count = queries.shape
    seq_count = lax.axis_size("seq")
    seq_pos = lax.axis_index("seq")
    rows_dev = tok_count // COLS
    half_rows = rows_dev * seq_count
    rows_all = 2 * half_rows
    cols_dev = COLS // seq_count
    freq_dev = 2 * rows_dev
    period = rows_all * COLS
    highest = lax.Precision.HIGHEST
    row_ids = jnp.arange(rows_all, dtype=jnp.int32)
    col_ids = jnp.arange(COLS, dtype=jnp.int32)
    owner_block = row_ids // freq_dev
    owner_rest = row_ids % freq_dev
    lower_ids = owner_block * rows_dev + owner_rest % rows_dev
    freq_order = jnp.where(
        owner_rest < rows_dev, lower_ids, jnp.where(lower_ids > 0, rows_all - lower_ids, half_rows)
    )
    cos_first, sin_first = angle_tables(row_ids[:half_rows], freq_order, rows_all)
    cos_split = split_table(cos_first)
    sin_split = split_table(sin_first)
    cos_second, sin_second = angle_tables(col_ids, col_ids, COLS)
    my_cols = seq_pos * cols_dev + jnp.arange(cols_dev, dtype=jnp.int32)
    cos_fwd, sin_fwd = angle_tables(my_cols, freq_order, period)
    my_freq = lax.dynamic_slice_in_dim(freq_order, seq_pos * freq_dev, freq_dev, 0)
    cos_inv, sin_inv = angle_tables(my_freq, col_ids, period)

    def contract(form, left, right):
        return jnp.einsum(form, left, right, precision=highest, preferred_element_type=f32)

    def transform(signal):
        stacked = signal.shape[0]
        blocks = signal.reshape(stacked, chan_count, rows_dev, COLS)
        columns = lax.all_to_all(blocks, "seq", split_axis=3, concat_axis=2, tiled=True)
        first_re = first_section(columns, cos_split)
        first_im = -first_section(columns, sin_split)
        turned_re = first_re * cos_fwd + first_im * sin_fwd
        turned_im = first_im * cos_fwd - first_re * sin_fwd
        mid_re, mid_im = (
            lax.all_to_all(
                turned_re.astype(jnp.bfloat16), "seq", split_axis=3, concat_axis=2, tiled=True
            ).astype(turned_re.dtype),
            lax.all_to_all(
                turned_im.astype(jnp.bfloat16), "seq", split_axis=3, concat_axis=2, tiled=True
            ).astype(turned_im.dtype),
        )
        spec_re = contract("scbk,bq->sckq", mid_re, cos_second) + contract(
            "scbk,bq->sckq", mid_im, sin_second
        )
        spec_im = contract("scbk,bq->sckq", mid_im, cos_second) - contract(
            "scbk,bq->sckq", mid_re, sin_second
        )
        return (spec_re, spec_im)

    def invert(spec_re, spec_im):
        back_re = contract("sckq,bq->sckb", spec_re, cos_second) - contract(
            "sckq,bq->sckb", spec_im, sin_second
        )
        back_im = contract("sckq,bq->sckb", spec_im, cos_second) + contract(
            "sckq,bq->sckb", spec_re, sin_second
        )
        turned_re = back_re * cos_inv - back_im * sin_inv
        turned_im = back_im * cos_inv + back_re * sin_inv
        full_re, full_im = (
            lax.all_to_all(
                turned_re.astype(jnp.bfloat16), "seq", split_axis=3, concat_axis=2, tiled=True
            ).astype(turned_re.dtype),
            lax.all_to_all(
                turned_im.astype(jnp.bfloat16), "seq", split_axis=3, concat_axis=2, tiled=True
            ).astype(turned_im.dtype),
        )
        inv_scale = 1.0 / period
        real_part = (
            contract("sckb,ak->scab", full_re, cos_first)
            - contract("sckb,ak->scab", full_im, sin_first)
        ) * inv_scale
        row_blocks = lax.all_to_all(
            real_part.astype(jnp.bfloat16), "seq", split_axis=2, concat_axis=3, tiled=True
        ).astype(real_part.dtype)
        return row_blocks.reshape(row_blocks.shape[0], chan_count, tok_count)

    tensor_pos = lax.axis_index("tensor")
    weight_rows = lax.dynamic_slice_in_dim(out_weight, tensor_pos * chan_count, chan_count, 0)
    weight_cols = lax.dynamic_slice_in_dim(out_weight, tensor_pos * chan_count, chan_count, 1)

    def channel_mix(local_part, by_source):
        return jnp.dot(
            by_source.T,
            lax.all_gather(local_part, "tensor", axis=0, tiled=True),
            preferred_element_type=f32,
        )

    key_float = key_feats.astype(f32)
    value_float = value_feats.astype(f32)
    query_float = queries.astype(f32)
    key_value = (key_float * value_float).astype(jnp.bfloat16)
    spec_re, spec_im = transform(jnp.stack([key_value, filter_taps]))
    source_re, source_im = (spec_re[0], spec_im[0])
    taps_re, taps_im = (spec_re[1], spec_im[1])
    product_re = source_re * taps_re - source_im * taps_im
    product_im = source_re * taps_im + source_im * taps_re
    convolved = invert(product_re[None], product_im[None])[0]
    source_float = key_value.astype(f32)
    inner_sum = convolved + skip_gain[:, None] * source_float
    gated_out = (query_float * inner_sum).astype(jnp.bfloat16)
    output = channel_mix(gated_out, weight_cols).astype(jnp.bfloat16)
    grad_gated = channel_mix(out_grad, weight_rows.T)
    grad_queries = (grad_gated * inner_sum).astype(jnp.bfloat16)
    grad_inner = (grad_gated * query_float).astype(jnp.bfloat16)
    grad_re, grad_im = transform(grad_inner[None])
    grad_re, grad_im = (grad_re[0], grad_im[0])
    corr_re = grad_re * taps_re + grad_im * taps_im
    corr_im = grad_im * taps_re - grad_re * taps_im
    cross_re = grad_re * source_re + grad_im * source_im
    cross_im = grad_im * source_re - grad_re * source_im
    inverses = invert(jnp.stack([corr_re, cross_re]), jnp.stack([corr_im, cross_im]))
    grad_source = inverses[0] + skip_gain[:, None] * grad_inner.astype(f32)
    grad_taps = inverses[1] * (tok_count * seq_count) ** (-0.5)
    grad_keys = (grad_source * value_float).astype(jnp.bfloat16)
    grad_values = (grad_source * key_float).astype(jnp.bfloat16)
    return (output, grad_queries, grad_keys, grad_values, grad_taps)


def solution(mesh):
    placed = (
        P("tensor", "seq"),
        P("tensor", "seq"),
        P("tensor", "seq"),
        P("tensor", "seq"),
        P("tensor"),
        P(),
        P("tensor", "seq"),
    )
    return jax.shard_map(
        body,
        mesh=mesh,
        in_specs=placed,
        out_specs=(
            P("tensor", "seq"),
            P("tensor", "seq"),
            P("tensor", "seq"),
            P("tensor", "seq"),
            P("tensor", "seq"),
        ),
        check_vma=False,
    )
```

profile of v0, /device:TPU:24, one launch (start us, length us, event | category | flops | bytes accessed | tf_op | source)
XLA Modules:
  0.0 607.1 jit_solution(10300484255184439947)
XLA Ops:
  0.7 45.4 %all-gather.1 = bf16[8,2,16384]{2,1,0:T(2,128)(2,1)S(1)} all-gather(bf16[1,2,16384]{2,1,0:T(2,128)(2,1)} %bitcast.378), channel_id=1, replica_groups=mesh['tensor'=8,'seq'=32] {'tensor'}, dimensions={0}, use_global_device_ids=true | all-gather | bytes 589824 | tf_op jit(solution)/shard_map/all_gather | solution.py:120
  48.8 8.7 %all-to-all-start.6 = ((bf16[32,2,512]{2,1,0:T(2,128)(2,1)}), bf16[32,2,512]{2,1,0:T(2,128)(2,1)}, u32[]{:S(2)}, u32[]{:S(2)}) async-start(bf16[32,2,512]{2,1,0:T(2,128)(2,1)} %reshape.699), calls=%async_computation.6 | async-start | bytes 131072 | tf_op jit(solution)/shard_map/all_to_all | solution.py:65
  58.2 11.2 %fusion.133 = (bf16[1,512,1024]{2,1,0:T(8,128)(2,1)S(1)}, bf16[1,512,1024]{2,1,0:T(8,128)(2,1)S(1)}, bf16[1,512,1024]{2,1,0:T(8,128)(2,1)}, bf16[1,512,1024]{2,1...) fusion(s32[1024]{0:T(1024)S(1)} %select_select_fusion, s32[512]{0:T(512)S(1)} %slice.79), kind=kLoop, calls=%fused_computation.106 | loop fusion | flops 14680064 | bytes 6297600 | tf_op jit(solution)/shard_map/convert_element_type | solution.py:18
  92.6 8.1 %all-to-all-start.8 = ((bf16[32,2,1024]{2,1,0:T(2,128)(2,1)}), bf16[32,2,1024]{2,1,0:T(2,128)(2,1)}, u32[]{:S(2)}, u32[]{:S(2)}) async-start(bf16[32,2,1024]{2,1,0:T(2,128)(2,1)} %reshape.701), calls=%async_computation.8 | async-start | bytes 262144 | tf_op jit(solution)/shard_map/all_to_all | solution.py:74
  126.4 17.8 %fusion.5 = f32[2,32,1024]{2,1,0:T(8,128)S(1)} fusion(bf16[2,1024,32]{1,2,0:T(8,128)(2,1)S(1)} %reshape.661), kind=kOutput, calls=%fused_computation.9 | convolution fusion | flops 819986432 | bytes 393216 | tf_op jit(solution)/shard_map/scbk,bq->sckq/dot_general | solution.py:60
  144.1 7.9 %all-to-all-start.1 = ((bf16[32,2,2048]{2,1,0:T(2,128)(2,1)}), bf16[32,2,2048]{2,1,0:T(2,128)(2,1)S(1)}, u32[]{:S(2)}, u32[]{:S(2)}) async-start(bf16[32,2,2048]{2,1,0:T(2,128)(2,1)} %reshape.689), calls=%async_computation.1 | async-start | bytes 524288 | tf_op jit(solution)/shard_map/all_to_all | solution.py:71
  153.2 18.1 %fusion.115 = f32[1,2,32,1024]{3,2,1,0:T(8,128)} fusion(f32[2,32,1024]{2,1,0:T(8,128)S(1)} %fusion.5, bf16[2,1024,32]{1,2,0:T(8,128)(2,1)S(1)} %reshape.660), kind=kOutput, calls=%fused_computation.93 | convolution fusion | flops 820051968 | bytes 655360 | tf_op jit(solution)/shard_map/scbk,bq->sckq/dot_general | solution.py:60
  171.3 18.2 %fusion.3 = f32[2,32,1024]{2,1,0:T(8,128)} fusion(bf16[2,1024,32]{1,2,0:T(8,128)(2,1)S(1)} %reshape.660), kind=kOutput, calls=%fused_computation.7 | convolution fusion | flops 819986432 | bytes 393216 | tf_op jit(solution)/shard_map/scbk,bq->sckq/dot_general | solution.py:60
  189.6 8.0 %all-to-all-start.2 = ((bf16[32,2,2048]{2,1,0:T(2,128)(2,1)}), bf16[32,2,2048]{2,1,0:T(2,128)(2,1)S(1)}, u32[]{:S(2)}, u32[]{:S(2)}) async-start(bf16[32,2,2048]{2,1,0:T(2,128)(2,1)} %reshape.691), calls=%async_computation.2 | async-start | bytes 524288 | tf_op jit(solution)/shard_map/all_to_all | solution.py:74
  199.9 18.3 %fusion.23 = f32[2,2,32,1024]{3,2,1,0:T(8,128)} fusion(bf16[2,2,1024,32]{2,3,1,0:T(8,128)(2,1)S(1)} %all_to_all.141), kind=kOutput, calls=%fused_computation.27 | convolution fusion | flops 1625292800 | bytes 786432 | tf_op jit(solution)/shard_map/scbk,bq->sckq/dot_general | solution.py:60
  220.6 18.2 %fusion.25 = f32[2,2,32,1024]{3,2,1,0:T(8,128)S(1)} fusion(bf16[2,2,1024,32]{2,3,1,0:T(8,128)(2,1)S(1)} %all_to_all.145), kind=kOutput, calls=%fused_computation.29 | convolution fusion | flops 1625292800 | bytes 786432 | tf_op jit(solution)/shard_map/scbk,bq->sckq/dot_general | solution.py:60
  238.8 17.6 %fusion.91 = f32[2,2,32,1024]{3,2,1,0:T(8,128)S(1)} fusion(f32[2,2,32,1024]{3,2,1,0:T(8,128)S(1)} %copy-done.16, bf16[2,2,1024,32]{2,3,1,0:T(8,128)(2,1)S(1)} %all_to_all.145), kind=kOutput, calls=%fused_computation.85 | convolution fusion | flops 1625423872 | bytes 1310720 | tf_op jit(solution)/shard_map/scbk,bq->sckq/dot_general | solution.py:60
  256.5 17.8 %fusion.88 = f32[2,2,32,1024]{3,2,1,0:T(8,128)S(1)} fusion(f32[2,2,32,1024]{3,2,1,0:T(8,128)S(1)} %fusion.25, bf16[2,2,1024,32]{2,3,1,0:T(8,128)(2,1)S(1)} %all_to_all.141), kind=kOutput, calls=%fused_computation.84 | convolution fusion | flops 1625423872 | bytes 1310720 | tf_op jit(solution)/shard_map/scbk,bq->sckq/dot_general | solution.py:60
  274.3 18.3 %multiply_add_fusion.1 = (f32[1,2,32,1024]{3,2,1,0:T(8,128)}, f32[1,2,32,1024]{3,2,1,0:T(8,128)S(1)}, f32[1,2,32,1024]{3,2,1,0:T(8,128)S(1)}, f32[1,2,32,1024]{3...) fusion(f32[1,2,32,1024]{3,2,1,0:T(8,128)S(1)} %copy-done.19, ...), kind=kOutput, calls=%fused_computation.144 | convolution fusion | flops 821231616 | bytes 3276800 | tf_op jit(solution)/shard_map/scbk,bq->sckq/dot_general | solution.py:60
  292.6 19.6 %fusion.9 = f32[2,32,1024]{2,1,0:T(8,128)S(1)} fusion(f32[1,2,32,1024]{3,2,1,0:T(8,128)S(1)} %get-tuple-element.17), kind=kOutput, calls=%fused_computation.13 | convolution fusion | flops 819986432 | bytes 524288 | tf_op jit(solution)/shard_map/sckq,bq->sckb/dot_general | solution.py:60
  312.2 19.4 %fusion.7 = f32[2,32,1024]{2,1,0:T(8,128)S(1)} fusion(f32[1,2,32,1024]{3,2,1,0:T(8,128)S(1)} %get-tuple-element.18), kind=kOutput, calls=%fused_computation.11 | convolution fusion | flops 819986432 | bytes 524288 | tf_op jit(solution)/shard_map/sckq,bq->sckb/dot_general | solution.py:60
  331.6 19.7 %fusion.106 = f32[2,32,1024]{2,1,0:T(8,128)S(1)} fusion(f32[2,32,1024]{2,1,0:T(8,128)S(1)} %fusion.9, f32[1,2,32,1024]{3,2,1,0:T(8,128)S(1)} %get-tuple-element.18), kind=kOutput, calls=%fused_computation.90 | convolution fusion | flops 820051968 | bytes 786432 | tf_op jit(solution)/shard_map/sckq,bq->sckb/dot_general | solution.py:60
  351.3 19.2 %fusion.164 = (bf16[1,2,32,1024]{3,2,1,0:T(8,128)(2,1)S(1)}, bf16[1,2,32,1024]{3,2,1,0:T(8,128)(2,1)S(1)}) fusion(f32[2,32,1024]{2,1,0:T(8,128)S(1)} %fusion.106, f32[32,1024]{1,0:T(8,128)S(1)} %copy-done.13, f32[32,1024]{1,0:T(8,128)S(1)} %copy-done.12, f32[2,32,1024]{2,1,0:T(8,128)S(1)} %fusion.7, f32[1,2,32,1024]{3,2,1,0:T(8,128)S(1)} %get-tuple-element.17), kind=kOutput, calls=%fused_computation.176 | convolution fusion | flops 820576256 | bytes 1310720 | tf_op jit(solution)/shard_map/sckq,bq->sckb/dot_general | solution.py:60
  381.7 19.1 %fusion.21 = f32[2,2,32,1024]{3,2,1,0:T(8,128)S(1)} fusion(f32[1,2,32,1024]{3,2,1,0:T(8,128)S(1)} %get-tuple-element.10, f32[1,2,32,1024]{3,2,1,0:T(8,128)S(1)} %get-tuple-element.11), kind=kOutput, calls=%fused_computation.25 | convolution fusion | flops 1625423872 | bytes 1048576 | tf_op jit(solution)/shard_map/sckq,bq->sckb/dot_general | solution.py:60
  400.8 19.3 %fusion.94 = f32[2,2,32,1024]{3,2,1,0:T(8,128)S(1)} fusion(f32[2,2,32,1024]{3,2,1,0:T(8,128)S(1)} %fusion.21, f32[1,2,32,1024]{3,2,1,0:T(8,128)S(1)} %copy-done.22, f32[1,2,32,1024]{3,2,1,0:T(8,128)S(1)} %copy-done.21), kind=kOutput, calls=%fused_computation.86 | convolution fusion | flops 1625554944 | bytes 1572864 | tf_op jit(solution)/shard_map/sckq,bq->sckb/dot_general | solution.py:60
  420.2 19.1 %fusion.19 = f32[2,2,32,1024]{3,2,1,0:T(8,128)S(1)} fusion(f32[1,2,32,1024]{3,2,1,0:T(8,128)S(1)} %copy-done.22, f32[1,2,32,1024]{3,2,1,0:T(8,128)S(1)} %copy-done.21), kind=kOutput, calls=%fused_computation.23 | convolution fusion | flops 1625423872 | bytes 1048576 | tf_op jit(solution)/shard_map/sckq,bq->sckb/dot_general | solution.py:60
  439.3 8.1 %all-to-all-start.4 = ((bf16[32,2,1024]{2,1,0:T(2,128)(2,1)}), bf16[32,2,1024]{2,1,0:T(2,128)(2,1)S(1)}, u32[]{:S(2)}, u32[]{:S(2)}) async-start(bf16[32,2,1024]{2,1,0:T(2,128)(2,1)} %reshape.695), calls=%async_computation.4 | async-start | bytes 262144 | tf_op jit(solution)/shard_map/all_to_all | solution.py:99
  447.4 19.0 %subtract_convert_fusion.2 = (bf16[2,2,32,1024]{3,2,1,0:T(8,128)(2,1)S(1)}, bf16[2,2,32,1024]{3,2,1,0:T(8,128)(2,1)S(1)}) fusion(f32[2,2,32,1024]{3,2,1,0:T(8,128)S(1)} %fusion.94, f32[32,1024]{1,0:T(8,128)S(1)} %copy-done.13, f32[32,1024]{1,0:T(8,128)S(1)} %copy-done.12, f32[2,2,32,1024]{3,2,1,0:T(8,128)S(1)} %fusion.19, ...), kind=kOutput, calls=%fused_computation.127 | convolution fusion | flops 1626603520 | bytes 2359296 | tf_op jit(solution)/shard_map/sckq,bq->sckb/dot_general | solution.py:60
  472.6 7.9 %all-to-all-start.10 = ((bf16[32,2,2048]{2,1,0:T(2,128)(2,1)}), bf16[32,2,2048]{2,1,0:T(2,128)(2,1)S(1)}, u32[]{:S(2)}, u32[]{:S(2)}) async-start(bf16[32,2,2048]{2,1,0:T(2,128)(2,1)} %reshape.705), calls=%async_computation.10 | async-start | bytes 524288 | tf_op jit(solution)/shard_map/all_to_all | solution.py:99
  481.6 8.7 %fusion.137 = f32[512,64]{0,1:S(1)} fusion(bf16[1024,64]{0,1:T(8,128)(2,1)S(1)} %bitcast.374, s32[1024]{0:T(1024)S(1)} %select_select_fusion, s32[512]{0:T(512)S(1)} %slice.79), kind=kOutput, calls=%fused_computation.109 | convolution fusion | flops 409993216 | bytes 268288
  490.4 9.2 %fusion.140 = f32[512,64]{0,1:S(1)} fusion(bf16[1024,64]{0,1:T(8,128)(2,1)S(1)} %bitcast.375, s32[1024]{0:T(1024)S(1)} %select_select_fusion, s32[512]{0:T(512)S(1)} %slice.79), kind=kOutput, calls=%fused_computation.110 | convolution fusion | flops 409993216 | bytes 268288
  499.6 7.9 %all-to-all-start.9 = ((bf16[32,2,2048]{2,1,0:T(2,128)(2,1)}), bf16[32,2,2048]{2,1,0:T(2,128)(2,1)S(1)}, u32[]{:S(2)}, u32[]{:S(2)}) async-start(bf16[32,2,2048]{2,1,0:T(2,128)(2,1)} %reshape.707), calls=%async_computation.9 | async-start | bytes 524288 | tf_op jit(solution)/shard_map/all_to_all | solution.py:96
  510.9 8.8 %fusion.52 = f32[512,2,2,32]{0,3,2,1:T(8,128)S(1)} fusion(bf16[2,2,1024,32]{2,3,1,0:T(8,128)(2,1)S(1)} %all_to_all.169, s32[1024]{0:T(1024)S(1)} %select_select_fusion, s32[512]{0:T(512)S(1)} %slice.79), kind=kOutput, calls=%fused_computation.68 | convolution fusion | flops 812646400 | bytes 530432 | tf_op jit(solution)/shard_map/sckb,ak->scab/dot_general | solution.py:60
  519.7 8.0 %all-to-all-start.5 = ((bf16[32,2,512]{2,1,0:T(2,128)(2,1)}), bf16[32,2,512]{2,1,0:T(2,128)(2,1)S(1)}, u32[]{:S(2)}, u32[]{:S(2)}) async-start(bf16[32,2,512]{2,1,0:T(2,128)(2,1)} %reshape.697), calls=%async_computation.5 | async-start | bytes 131072 | tf_op jit(solution)/shard_map/all_to_all | solution.py:108
  530.1 9.1 %fusion.127 = bf16[2,2,512,32]{2,3,1,0:T(8,128)(2,1)S(1)} fusion(f32[512,2,2,32]{0,3,2,1:T(8,128)S(1)} %fusion.52, bf16[2,2,1024,32]{2,3,1,0:T(8,128)(2,1)S(1)} %all_to_all.165, s32[1024]{0:T(1024)S(1)} %select_select_fusion, s32[512]{0:T(512)S(1)} %slice.79), kind=kOutput, calls=%fused_computation.97 | convolution fusion | flops 812843008 | bytes 661504 | tf_op jit(solution)/shard_map/sckb,ak->scab/dot_general | solution.py:60
  549.0 8.1 %all-to-all-done.11 = bf16[32,2,1024]{2,1,0:T(2,128)(2,1)S(1)} async-done(((bf16[32,2,1024]{2,1,0:T(2,128)(2,1)}), bf16[32,2,1024]{2,1,0:T(2,128)(2,1)S(1)}, u32[]{:S(2)}, u32[]{:S(2)}) %all-to-all-start.11) | async-done | bytes 131104 | tf_op jit(solution)/shard_map/all_to_all | solution.py:108
  559.6 44.9 %all-gather = bf16[8,2,16384]{2,1,0:T(2,128)(2,1)S(1)} all-gather(bf16[1,2,16384]{2,1,0:T(2,128)(2,1)S(1)} %get-tuple-element.33), channel_id=1, replica_groups=mesh['tensor'=8,'seq'=32] {'tensor'}, dimensions={0}, use_global_device_ids=true | all-gather | bytes 589824 | tf_op jit(solution)/shard_map/all_gather | solution.py:120
  (149 shorter events, 96.4 us)
Async XLA Ops:
  0.6 45.6 %copy-start = (bf16[16,16]{1,0:T(8,128)(2,1)S(1)}, bf16[16,16]{1,0:T(8,128)(2,1)}, u32[]{:S(2)}) copy-start(bf16[16,16]{1,0:T(8,128)(2,1)} %param.12) | copy-start | bytes 1540
  0.6 45.6 %copy-start.8 = (bf16[2,16384]{1,0:T(2,128)(2,1)S(1)}, bf16[2,16384]{1,0:T(2,128)(2,1)}, u32[]{:S(2)}) copy-start(bf16[2,16384]{1,0:T(2,128)(2,1)} %param.7) | copy-start | bytes 196612
  48.8 26.7 %all-to-all-start.6 = ((bf16[32,2,512]{2,1,0:T(2,128)(2,1)}), bf16[32,2,512]{2,1,0:T(2,128)(2,1)}, u32[]{:S(2)}, u32[]{:S(2)}) async-start(bf16[32,2,512]{2,1,0:T(2,128)(2,1)} %reshape.699), calls=%async_computation.6 | async-start | bytes 131072 | tf_op jit(solution)/shard_map/all_to_all | solution.py:65
  58.2 11.2 %copy-start.6 = (bf16[2,16384]{1,0:T(2,128)(2,1)S(1)}, bf16[2,16384]{1,0:T(2,128)(2,1)}, u32[]{:S(2)}) copy-start(bf16[2,16384]{1,0:T(2,128)(2,1)} %param.8) | copy-start | bytes 196612
  58.2 11.2 %copy-start.10 = (bf16[2,16384]{1,0:T(2,128)(2,1)S(1)}, bf16[2,16384]{1,0:T(2,128)(2,1)}, u32[]{:S(2)}) copy-start(bf16[2,16384]{1,0:T(2,128)(2,1)} %param.9) | copy-start | bytes 196612
  58.2 11.3 %copy-start.14 = (bf16[2,16384]{1,0:T(2,128)(2,1)S(1)}, bf16[2,16384]{1,0:T(2,128)(2,1)}, u32[]{:S(2)}) copy-start(bf16[2,16384]{1,0:T(2,128)(2,1)} %param.10) | copy-start | bytes 196612
  75.5 16.5 %all-to-all-start = ((bf16[32,2,1024]{2,1,0:T(2,128)(2,1)}), bf16[32,2,1024]{2,1,0:T(2,128)(2,1)S(1)}, u32[]{:S(2)}, u32[]{:S(2)}) async-start(bf16[32,2,1024]{2,1,0:T(2,128)(2,1)} %reshape.687), calls=%async_computation | async-start | bytes 262144 | tf_op jit(solution)/shard_map/all_to_all | solution.py:65
  84.8 2.7 copy-start.1
  92.6 23.8 %all-to-all-start.8 = ((bf16[32,2,1024]{2,1,0:T(2,128)(2,1)}), bf16[32,2,1024]{2,1,0:T(2,128)(2,1)}, u32[]{:S(2)}, u32[]{:S(2)}) async-start(bf16[32,2,1024]{2,1,0:T(2,128)(2,1)} %reshape.701), calls=%async_computation.8 | async-start | bytes 262144 | tf_op jit(solution)/shard_map/all_to_all | solution.py:74
  107.1 2.8 copy-start.2
  107.1 2.8 copy-start.3
  116.4 27.7 %all-to-all-start.7 = ((bf16[32,2,1024]{2,1,0:T(2,128)(2,1)}), bf16[32,2,1024]{2,1,0:T(2,128)(2,1)S(1)}, u32[]{:S(2)}, u32[]{:S(2)}) async-start(bf16[32,2,1024]{2,1,0:T(2,128)(2,1)} %reshape.703), calls=%async_computation.7 | async-start | bytes 262144 | tf_op jit(solution)/shard_map/all_to_all | solution.py:71
  144.1 45.4 %all-to-all-start.1 = ((bf16[32,2,2048]{2,1,0:T(2,128)(2,1)}), bf16[32,2,2048]{2,1,0:T(2,128)(2,1)S(1)}, u32[]{:S(2)}, u32[]{:S(2)}) async-start(bf16[32,2,2048]{2,1,0:T(2,128)(2,1)} %reshape.689), calls=%async_computation.1 | async-start | bytes 524288 | tf_op jit(solution)/shard_map/all_to_all | solution.py:71
  189.6 28.6 %all-to-all-start.2 = ((bf16[32,2,2048]{2,1,0:T(2,128)(2,1)}), bf16[32,2,2048]{2,1,0:T(2,128)(2,1)S(1)}, u32[]{:S(2)}, u32[]{:S(2)}) async-start(bf16[32,2,2048]{2,1,0:T(2,128)(2,1)} %reshape.691), calls=%async_computation.2 | async-start | bytes 524288 | tf_op jit(solution)/shard_map/all_to_all | solution.py:74
  220.6 18.3 %copy-start.16 = (f32[2,2,32,1024]{3,2,1,0:T(8,128)S(1)}, f32[2,2,32,1024]{3,2,1,0:T(8,128)}, u32[]{:S(2)}) copy-start(f32[2,2,32,1024]{3,2,1,0:T(8,128)} %fusion.23) | copy-start | bytes 1572868
  256.5 17.8 %copy-start.19 = (f32[1,2,32,1024]{3,2,1,0:T(8,128)S(1)}, f32[1,2,32,1024]{3,2,1,0:T(8,128)}, u32[]{:S(2)}) copy-start(f32[1,2,32,1024]{3,2,1,0:T(8,128)} %fusion.115) | copy-start | bytes 786436
  256.5 17.8 %copy-start.20 = (f32[2,32,1024]{2,1,0:T(8,128)S(1)}, f32[2,32,1024]{2,1,0:T(8,128)}, u32[]{:S(2)}) copy-start(f32[2,32,1024]{2,1,0:T(8,128)} %fusion.3) | copy-start | bytes 786436
  292.6 89.2 %copy-start.17 = (f32[1,2,32,1024]{3,2,1,0:T(8,128)}, f32[1,2,32,1024]{3,2,1,0:T(8,128)S(1)}, u32[]{:S(2)}) copy-start(f32[1,2,32,1024]{3,2,1,0:T(8,128)S(1)} %get-tuple-element.11) | copy-start | bytes 786436
  331.6 19.7 %copy-start.12 = (f32[32,1024]{1,0:T(8,128)S(1)}, f32[32,1024]{1,0:T(8,128)}, u32[]{:S(2)}) copy-start(f32[32,1024]{1,0:T(8,128)} %get-tuple-element.35) | copy-start | bytes 393220
  331.6 19.7 %copy-start.13 = (f32[32,1024]{1,0:T(8,128)S(1)}, f32[32,1024]{1,0:T(8,128)}, u32[]{:S(2)}) copy-start(f32[32,1024]{1,0:T(8,128)} %get-tuple-element.36) | copy-start | bytes 393220
  372.2 67.1 %all-to-all-start.3 = ((bf16[32,2,1024]{2,1,0:T(2,128)(2,1)}), bf16[32,2,1024]{2,1,0:T(2,128)(2,1)S(1)}, u32[]{:S(2)}, u32[]{:S(2)}) async-start(bf16[32,2,1024]{2,1,0:T(2,128)(2,1)} %reshape.693), calls=%async_computation.3 | async-start | bytes 262144 | tf_op jit(solution)/shard_map/all_to_all | solution.py:96
  381.7 19.1 %copy-start.21 = (f32[1,2,32,1024]{3,2,1,0:T(8,128)S(1)}, f32[1,2,32,1024]{3,2,1,0:T(8,128)}, u32[]{:S(2)}) copy-start(f32[1,2,32,1024]{3,2,1,0:T(8,128)} %get-tuple-element.9) | copy-start | bytes 786436
  381.7 19.1 %copy-start.22 = (f32[1,2,32,1024]{3,2,1,0:T(8,128)S(1)}, f32[1,2,32,1024]{3,2,1,0:T(8,128)}, u32[]{:S(2)}) copy-start(f32[1,2,32,1024]{3,2,1,0:T(8,128)} %get-tuple-element.12) | copy-start | bytes 786436
  420.2 27.2 %copy-start.18 = (f32[1,2,32,1024]{3,2,1,0:T(8,128)S(1)}, f32[1,2,32,1024]{3,2,1,0:T(8,128)}, u32[]{:S(2)}) copy-start(f32[1,2,32,1024]{3,2,1,0:T(8,128)} %copy-done.17) | copy-start | bytes 786436
  439.3 33.3 %all-to-all-start.4 = ((bf16[32,2,1024]{2,1,0:T(2,128)(2,1)}), bf16[32,2,1024]{2,1,0:T(2,128)(2,1)S(1)}, u32[]{:S(2)}, u32[]{:S(2)}) async-start(bf16[32,2,1024]{2,1,0:T(2,128)(2,1)} %reshape.695), calls=%async_computation.4 | async-start | bytes 262144 | tf_op jit(solution)/shard_map/all_to_all | solution.py:99
  472.6 27.0 %all-to-all-start.10 = ((bf16[32,2,2048]{2,1,0:T(2,128)(2,1)}), bf16[32,2,2048]{2,1,0:T(2,128)(2,1)S(1)}, u32[]{:S(2)}, u32[]{:S(2)}) async-start(bf16[32,2,2048]{2,1,0:T(2,128)(2,1)} %reshape.705), calls=%async_computation.10 | async-start | bytes 524288 | tf_op jit(solution)/shard_map/all_to_all | solution.py:99
  499.6 20.1 %all-to-all-start.9 = ((bf16[32,2,2048]{2,1,0:T(2,128)(2,1)}), bf16[32,2,2048]{2,1,0:T(2,128)(2,1)S(1)}, u32[]{:S(2)}, u32[]{:S(2)}) async-start(bf16[32,2,2048]{2,1,0:T(2,128)(2,1)} %reshape.707), calls=%async_computation.9 | async-start | bytes 524288 | tf_op jit(solution)/shard_map/all_to_all | solution.py:96
  519.7 21.1 %all-to-all-start.5 = ((bf16[32,2,512]{2,1,0:T(2,128)(2,1)}), bf16[32,2,512]{2,1,0:T(2,128)(2,1)S(1)}, u32[]{:S(2)}, u32[]{:S(2)}) async-start(bf16[32,2,512]{2,1,0:T(2,128)(2,1)} %reshape.697), calls=%async_computation.5 | async-start | bytes 131072 | tf_op jit(solution)/shard_map/all_to_all | solution.py:108
  540.8 16.4 %all-to-all-start.11 = ((bf16[32,2,1024]{2,1,0:T(2,128)(2,1)}), bf16[32,2,1024]{2,1,0:T(2,128)(2,1)S(1)}, u32[]{:S(2)}, u32[]{:S(2)}) async-start(bf16[32,2,1024]{2,1,0:T(2,128)(2,1)} %reshape.709), calls=%async_computation.11 | async-start | bytes 262144 | tf_op jit(solution)/shard_map/all_to_all | solution.py:108
  557.6 0.9 copy-start.9
  557.6 0.9 copy-start.11
  557.6 0.9 copy-start.15
  (3 other events, 2.5 us)
where the time goes:
time: 615 us; the launch traced here: 607 us
  matrix products  344 us (56%)
  starting transfers between devices  95.3 us (15%)
  blocking collectives  90.3 us (15%)
  local copies, waits for them, and re-layouts  51.6 us (8%)
  other arithmetic  15.7 us (3%)
  waiting for transfers between devices  8.35 us (1%)
    dot_general x18, matrix products, contract(): jnp.einsum(form, left, right, precision=highest, preferred_element_type=f32)  317 us
    all_gather x2, blocking collectives, channel_mix(): lax.all_gather(local_part, 'tensor', axis=0, tiled=True)  90.3 us
    unnamed x73, local copies, waits for them, and re-layouts  28 us
    unnamed x2, matrix products  17.9 us
    all_to_all x2, starting transfers between devices, transform(): lax.all_to_all(blocks, 'seq', split_axis=3, concat_axis=2, tiled=True)  16.3 us
    all_to_all x2, starting transfers between devices, transform(): lax.all_to_all(turned_im.astype(jnp.bfloat16), 'seq', split_axis=3, conca...  16.1 us
    all_to_all x2, starting transfers between devices, invert(): lax.all_to_all(turned_im.astype(jnp.bfloat16), 'seq', split_axis=3, conca...  16 us
    all_to_all x2, starting transfers between devices, transform(): lax.all_to_all(turned_re.astype(jnp.bfloat16), 'seq', split_axis=3, conca...  15.7 us
  transfers between devices with their start and end apart: 12, of which 2 were waited for; matrix products, arithmetic and copies ran while one was open for 40% of the time, Pallas kernels for 0%

commit v1 on v0

v1 whole, which is shorter than its diff:
```python
import math

import jax
import jax.numpy as jnp
import numpy as np
from jax import lax
from jax.experimental import pallas as pl
from jax.experimental.pallas import tpu as pltpu
from jax.sharding import PartitionSpec as P

F32 = jnp.float32
BF16 = jnp.bfloat16
CH = 2
GROUP = 8
BLOCKS = 32
SIDE = 128
ROWS = CH * SIDE
BLOCK = SIDE * SIDE
LENGTH = 2 * BLOCK
FREQ_ROWS = SIDE // BLOCKS
PIECE = CH * FREQ_ROWS
VMEM = pl.BlockSpec(memory_space=pltpu.VMEM)
SMEM = pl.BlockSpec(memory_space=pltpu.SMEM)
PARAMS = pltpu.CompilerParams(vmem_limit_bytes=48 * 1024 * 1024)


def tables():
    side = np.arange(SIDE)
    k1 = np.arange(BLOCKS)[:, None, None] * FREQ_ROWS + np.arange(FREQ_ROWS)[None, None, :]
    k1 = np.broadcast_to(k1, (BLOCKS, CH, FREQ_ROWS)).reshape(-1)
    chan = np.broadcast_to(np.arange(CH)[None, :, None], (BLOCKS, CH, FREQ_ROWS)).reshape(-1)
    angle = 2 * np.pi * (k1[:, None] + 0.5) * side[None, :] / (2 * SIDE)
    first = np.zeros((2, ROWS, CH, SIDE))
    for c in range(CH):
        mine = (chan == c)[:, None]
        first[0, :, c] = np.where(mine, np.cos(angle), 0)
        first[1, :, c] = np.where(mine, -np.sin(angle), 0)
    first = first.reshape(2 * ROWS, ROWS)
    turn = 2 * np.pi * (k1[:, None] + 0.5) * side[None, :] / LENGTH
    turn = np.stack([np.cos(turn), np.sin(turn)])
    phase = 2 * np.pi * side[:, None] * side[None, :] / SIDE
    second = np.block([[np.cos(phase), -np.sin(phase)], [np.sin(phase), np.cos(phase)]])
    return (
        jnp.asarray(first, BF16),
        jnp.asarray(first.T, BF16),
        jnp.asarray(turn, F32),
        jnp.asarray(second, BF16),
        jnp.asarray(second.T, BF16),
    )


def square(ref):
    return ref[...].astype(F32).reshape(ROWS, SIDE)


def forward(signal, first, turn, second):
    stage = jnp.dot(first, signal, preferred_element_type=F32)
    real, imag = stage[:ROWS], stage[ROWS:]
    cos, sin = turn[0], turn[1]
    turned = jnp.concatenate(
        [(real * cos + imag * sin).astype(BF16), (imag * cos - real * sin).astype(BF16)], axis=1
    )
    spec = jnp.dot(turned, second, preferred_element_type=F32)
    return spec[:, :SIDE], spec[:, SIDE:]


def pack(real, imag):
    both = jnp.concatenate(
        [real.reshape(BLOCKS, PIECE, SIDE), imag.reshape(BLOCKS, PIECE, SIDE)], axis=1
    )
    return both.astype(BF16)


def inverse(rows, first_t, turn, second_t):
    rows = rows.astype(F32)
    real = rows[:, :PIECE].reshape(ROWS, SIDE)
    imag = rows[:, PIECE:].reshape(ROWS, SIDE)
    spec = jnp.concatenate([real.astype(BF16), imag.astype(BF16)], axis=1)
    stage = jnp.dot(spec, second_t, preferred_element_type=F32)
    real, imag = stage[:, :SIDE], stage[:, SIDE:]
    cos, sin = turn[0], turn[1]
    turned = jnp.concatenate(
        [(real * cos - imag * sin).astype(BF16), (imag * cos + real * sin).astype(BF16)], axis=0
    )
    return jnp.dot(first_t, turned, preferred_element_type=F32) * (2.0 / LENGTH)


def spread_kernel(grad_ref, out_ref):
    rows = square(grad_ref).astype(BF16)
    for peer in range(GROUP):
        out_ref[peer] = rows


def source_kernel(key_ref, value_ref, taps_ref, first_ref, turn_ref, second_ref, kv_ref, spec_ref):
    tables_in = (first_ref[...], turn_ref[...], second_ref[...])
    key_value = (square(key_ref) * square(value_ref)).astype(BF16)
    kv_ref[...] = key_value
    spec_ref[:, :16, :] = pack(*forward(key_value, *tables_in))
    spec_ref[:, 16:, :] = pack(*forward(square(taps_ref).astype(BF16), *tables_in))


def mix(weight_ref, all_ref, chan):
    total = None
    for peer in range(GROUP):
        for c in range(CH):
            part = weight_ref[chan, peer * CH + c] * all_ref[
                peer, c * SIDE : (c + 1) * SIDE, :
            ].astype(F32)
            total = part if total is None else total + part
    return total


def grad_kernel(
    weight_ref, grads_ref, query_ref, spec_ref, first_ref, turn_ref, second_ref,
    gated_ref, inner_ref, out_ref,
):
    grad_gated = jnp.concatenate([mix(weight_ref, grads_ref, c) for c in range(CH)], axis=0)
    gated_ref[...] = grad_gated
    grad_inner = (grad_gated * square(query_ref)).astype(BF16)
    inner_ref[...] = grad_inner
    out_ref[:, :32, :] = spec_ref[...]
    out_ref[:, 32:, :] = pack(
        *forward(grad_inner, first_ref[...], turn_ref[...], second_ref[...])
    )


def block_kernel(spec_ref, out_ref, buf_ref):
    for sig in range(3):
        both = spec_ref[:, 16 * sig : 16 * sig + 16, :].astype(F32)
        buf_ref[sig, 0] = both[:, :PIECE]
        buf_ref[sig, 1] = both[:, PIECE:]
    row = lax.broadcasted_iota(jnp.int32, (PIECE, SIDE), 0)
    sign = jnp.where(row % 2 == 0, 1.0, -1.0).astype(F32)
    source, taps, grad = 0, 1, 2
    tile = 4

    def at(sig, blk):
        return buf_ref[sig, 0, blk], buf_ref[sig, 1, blk]

    def put(sig, blk, real, imag):
        out_ref[blk, 16 * sig : 16 * sig + 16, :] = jnp.concatenate([real, imag], axis=0).astype(
            BF16
        )

    def add(total, real, imag):
        return (real, imag) if total is None else (total[0] + real, total[1] + imag)

    last = None
    for base in range(0, BLOCKS, tile):
        sums = [None] * tile
        window = {}
        for j in range(base + tile):
            hr, hi = at(taps, j)
            for o in range(tile):
                blk = base + o - j
                if blk < 0:
                    continue
                if blk not in window:
                    window[blk] = at(source, blk)
                xr, xi = window[blk]
                sums[o] = add(sums[o], hr * xr - hi * xi, hr * xi + hi * xr)
        for o in range(tile):
            real, imag = sums[o]
            if last is not None:
                real, imag = real - sign * last[1], imag + sign * last[0]
            put(0, base + o, real, imag)
            last = sums[o]

    for slot, other in ((1, taps), (2, source)):
        after = None
        for base in range(BLOCKS - tile, -1, -tile):
            sums = [None] * tile
            window = {}
            for j in range(BLOCKS - base):
                hr, hi = at(other, j)
                for o in range(tile):
                    blk = base + o + j
                    if blk >= BLOCKS:
                        continue
                    if blk not in window:
                        window[blk] = at(grad, blk)
                    gr, gi = window[blk]
                    sums[o] = add(sums[o], gr * hr + gi * hi, gi * hr - gr * hi)
            for o in range(tile - 1, -1, -1):
                real, imag = sums[o]
                if after is not None:
                    real, imag = real + sign * after[1], imag - sign * after[0]
                put(slot, base + o, real, imag)
                after = sums[o]


def gate_kernel(
    skip_ref, rows_ref, kv_ref, query_ref, gated_ref, first_ref, turn_ref, second_ref,
    spread_ref, grad_query_ref,
):
    convolved = inverse(rows_ref[:, :16, :], first_ref[...], turn_ref[...], second_ref[...])
    inner_sum = convolved + skip_rows(skip_ref) * kv_ref[...].astype(F32)
    gated = (square(query_ref) * inner_sum).astype(BF16)
    for peer in range(GROUP):
        spread_ref[peer] = gated
    grad_query_ref[...] = (gated_ref[...] * inner_sum).reshape(CH, BLOCK).astype(BF16)


def skip_rows(skip_ref):
    row = lax.broadcasted_iota(jnp.int32, (ROWS, SIDE), 0)
    return jnp.where(row < SIDE, skip_ref[0], skip_ref[1])


def grads_kernel(
    skip_ref, rows_ref, inner_ref, key_ref, value_ref, first_ref, turn_ref, second_ref,
    grad_key_ref, grad_value_ref, grad_taps_ref, *, scale,
):
    tables_in = (first_ref[...], turn_ref[...], second_ref[...])
    source = inverse(rows_ref[:, 16:32, :], *tables_in)
    source = source + skip_rows(skip_ref) * inner_ref[...].astype(F32)
    source = source.reshape(CH, BLOCK)
    grad_key_ref[...] = (source * value_ref[...].astype(F32)).astype(BF16)
    grad_value_ref[...] = (source * key_ref[...].astype(F32)).astype(BF16)
    taps = inverse(rows_ref[:, 32:, :], *tables_in) * scale
    grad_taps_ref[...] = taps.reshape(CH, BLOCK)


def output_kernel(weight_ref, all_ref, out_ref):
    both = jnp.concatenate([mix(weight_ref, all_ref, c) for c in range(CH)], axis=0)
    out_ref[...] = both.reshape(CH, BLOCK).astype(BF16)


def call(kernel, outs, operands, smem=0, scratch=()):
    return pl.pallas_call(
        kernel,
        out_shape=[jax.ShapeDtypeStruct(shape, dtype) for shape, dtype in outs],
        in_specs=[SMEM] * smem + [VMEM] * (len(operands) - smem),
        out_specs=[VMEM] * len(outs),
        scratch_shapes=list(scratch),
        compiler_params=PARAMS,
    )(*operands)


def exchange(blocks, axis):
    return lax.all_to_all(blocks, axis, split_axis=0, concat_axis=0, tiled=True)


def body(queries, key_feats, value_feats, filter_taps, skip_gain, out_weight, out_grad):
    first, first_t, turn, second, second_t = tables()
    forward_tables = (first, turn, second)
    inverse_tables = (first_t, turn, second_t)
    start = lax.axis_index("tensor") * CH
    weight = out_weight.astype(F32)
    weight_rows = lax.dynamic_slice_in_dim(weight, start, CH, 0)
    weight_cols = lax.dynamic_slice_in_dim(weight, start, CH, 1).T
    square_shape = (ROWS, SIDE)
    spread_shape = (GROUP, ROWS, SIDE)
    tokens = (CH, BLOCK)

    (spread,) = call(spread_kernel, [(spread_shape, BF16)], (out_grad,))
    all_grads = exchange(spread, "tensor")
    key_value, spec = call(
        source_kernel,
        [(square_shape, BF16), ((BLOCKS, 32, SIDE), BF16)],
        (key_feats, value_feats, filter_taps, *forward_tables),
    )
    grad_gated, grad_inner, spec = call(
        grad_kernel,
        [(square_shape, F32), (square_shape, BF16), ((BLOCKS, 48, SIDE), BF16)],
        (weight_rows, all_grads, queries, spec, *forward_tables),
        smem=1,
    )
    spec = exchange(spec, "seq")
    (rows,) = call(
        block_kernel,
        [((BLOCKS, 48, SIDE), BF16)],
        (spec,),
        scratch=[pltpu.VMEM((3, 2, BLOCKS, PIECE, SIDE), F32)],
    )
    rows = exchange(rows, "seq")
    spread, grad_queries = call(
        gate_kernel,
        [(spread_shape, BF16), (tokens, BF16)],
        (skip_gain, rows, key_value, queries, grad_gated, *inverse_tables),
        smem=1,
    )
    all_gated = exchange(spread, "tensor")

    def grads(*refs):
        grads_kernel(*refs, scale=(BLOCKS * BLOCK) ** -0.5)

    grad_keys, grad_values, grad_taps = call(
        grads,
        [(tokens, BF16), (tokens, BF16), (tokens, F32)],
        (skip_gain, rows, grad_inner, key_feats, value_feats, *inverse_tables),
        smem=1,
    )
    (output,) = call(output_kernel, [(tokens, BF16)], (weight_cols, all_gated), smem=1)
    return (output, grad_queries, grad_keys, grad_values, grad_taps)


def solution(mesh):
    assert dict(mesh.shape) == {"tensor": GROUP, "seq": BLOCKS}
    placed = P("tensor", "seq")
    return jax.shard_map(
        body,
        mesh=mesh,
        in_specs=(placed, placed, placed, placed, P("tensor"), P(), placed),
        out_specs=(placed,) * 5,
        check_vma=False,
    )
```

time: 615 us -> 97.8 us (0.16)
  the two profiles are of different devices: /device:TPU:24 before, /device:TPU:1 now
where the time goes in v1:
time: 97.8 us; the launch traced here: 96.7 us
  blocking collectives  45.1 us (46%)
  waiting for transfers between devices  23.5 us (24%)
  starting transfers between devices  15.3 us (16%)
  Pallas kernels  9.56 us (10%)
  local copies, waits for them, and re-layouts  2.46 us (3%)
    all_to_all x2, blocking collectives, exchange(): return lax.all_to_all(blocks, axis, split_axis=0, concat_axis=0, tiled=True)  45.1 us
    all_to_all x2, waiting for transfers between devices, exchange(): return lax.all_to_all(blocks, axis, split_axis=0, concat_axis=0, tiled=True)  23.5 us
    all_to_all x2, starting transfers between devices, exchange(): return lax.all_to_all(blocks, axis, split_axis=0, concat_axis=0, tiled=True)  15.3 us
    pallas_call x7, Pallas kernels, call(): pl.pallas_call(kernel, out_shape=[jax.ShapeDtypeStruct(shape, dtype) for...  9.56 us
    unnamed x25, local copies, waits for them, and re-layouts  2.29 us
  transfers between devices with their start and end apart: 2, of which 2 were waited for; matrix products, arithmetic and copies ran while one was open for 0% of the time, Pallas kernels for 3%

profile of v1, /device:TPU:1, one launch (start us, length us, event | category | flops | bytes accessed | tf_op | source)
XLA Modules:
  0.0 96.7 jit_solution(5939854062517149648)
XLA Ops:
  0.6 0.0 copy-start.8
  0.6 0.8 copy-done.8
  1.5 0.8 shard_map.155
  2.3 0.0 copy-start.7
  2.3 0.0 copy-start.9
  2.3 11.8 %all-to-all-start = ((bf16[8,256,128]{2,1,0:T(8,128)(2,1)}), bf16[8,256,128]{2,1,0:T(8,128)(2,1)S(1)}, u32[]{:S(2)}, u32[]{:S(2)}) async-start(bf16[8,256,128]{2,1,0:T(8,128)(2,1)} %shard_map.155), calls=%async_computation | async-start | bytes 1048576 | tf_op jit(solution)/shard_map/all_to_all | solution.py:240
  14.1 0.7 copy-done.11
  14.8 0.1 copy.17
  14.9 0.1 constant_dynamic-slice_fusion
  15.0 0.1 copy.18.weight_ref
  15.1 0.0 copy-done
  15.1 0.0 copy-done.1
  15.1 0.0 copy-done.4
  15.1 0.0 copy-done.6
  15.1 0.0 copy-done.7
  15.1 0.0 copy-done.9
  15.1 0.0 copy-start.5
  15.1 0.7 shard_map.156
  15.8 9.9 %all-to-all-done.grads_ref = bf16[8,256,128]{2,1,0:T(8,128)(2,1)S(1)} async-done(((bf16[8,256,128]{2,1,0:T(8,128)(2,1)}), bf16[8,256,128]{2,1,0:T(8,128)(2,1)S(1)}, u32[]{:S(2)}, u32[]{:S(2)}) %all-to-all-start) | async-done | bytes 524320 | tf_op jit(solution)/shard_map/all_to_all | solution.py:240
  25.7 0.0 copy-done.5
  25.7 1.2 %shard_map.157 = (f32[256,128]{1,0:T(8,128)S(1)}, bf16[256,128]{1,0:T(8,128)(2,1)S(1)}, bf16[32,48,128]{2,1,0:T(8,128)(2,1)S(1)}) custom-call(f32[2,16]{1,0:T(2,128)S(1)} %copy.18.weight_ref, bf16[8,256,128]{2,1,0:T(8,128)(2,1)S(1)} %all-to-all-done.grads_ref, bf16[2,16384]{1,0:T(2,128)(2,1)S(1)} %copy-done.5, ...), custom_call_target="tpu_custom_call" | custom-call | tf_op jit(solution)/shard_map/pallas_call | solution.py:229
  26.9 27.5 %all_to_all.20.spec_ref = bf16[32,48,128]{2,1,0:T(8,128)(2,1)S(1)} all-to-all(bf16[32,48,128]{2,1,0:T(8,128)(2,1)S(1)} %get-tuple-element.16), channel_id=1, replica_groups=mesh['tensor'=8,'seq'=32] {'seq'}, dimensions={0} | all-to-all | bytes 786432 | tf_op jit(solution)/shard_map/all_to_all | solution.py:240
  54.4 1.7 %shard_map.158 = bf16[32,48,128]{2,1,0:T(8,128)(2,1)S(1)} custom-call(bf16[32,48,128]{2,1,0:T(8,128)(2,1)S(1)} %all_to_all.20.spec_ref), custom_call_target="tpu_custom_call" | custom-call | tf_op jit(solution)/shard_map/pallas_call | solution.py:229
  56.1 0.0 copy-start.2
  56.2 0.0 copy-start.3
  56.2 17.6 %all_to_all.21.rows_ref.refs_1_ = bf16[32,48,128]{2,1,0:T(8,128)(2,1)S(1)} all-to-all(bf16[32,48,128]{2,1,0:T(8,128)(2,1)S(1)} %shard_map.158), channel_id=1, replica_groups=mesh['tensor'=8,'seq'=32] {'seq'}, dimensions={0} | all-to-all | bytes 786432 | tf_op jit(solution)/shard_map/all_to_all | solution.py:240
  73.8 0.6 copy-done.10
  74.4 1.8 %shard_map.159 = (bf16[8,256,128]{2,1,0:T(8,128)(2,1)}, bf16[2,16384]{1,0:T(2,128)(2,1)}) custom-call(f32[2]{0:T(128)S(1)} %copy-done.10, bf16[32,48,128]{2,1,0:T(8,128)(2,1)S(1)} %all_to_all.21.rows_ref.refs_1_, bf16[256,128]{1,0:T(8,128)(2,1)S(1)} %get-tuple-element.17.kv_ref, bf16[2,16384]{1,0:T(2,128)(2,1)S(1)} %copy-done.5, ...), custom_call_target="tpu_custom_call" | custom-call | tf_op jit(solution)/shard_map/pallas_call | solution.py:229
  76.3 3.5 %all-to-all-start.3 = ((bf16[8,256,128]{2,1,0:T(8,128)(2,1)}), bf16[8,256,128]{2,1,0:T(8,128)(2,1)S(1)}, u32[]{:S(2)}, u32[]{:S(2)}) async-start(bf16[8,256,128]{2,1,0:T(8,128)(2,1)} %get-tuple-element.19), calls=%async_computation.3 | async-start | bytes 1048576 | tf_op jit(solution)/shard_map/all_to_all | solution.py:240
  79.8 1.8 %shard_map.161 = (bf16[2,16384]{1,0:T(2,128)(2,1)}, bf16[2,16384]{1,0:T(2,128)(2,1)}, f32[2,16384]{1,0:T(2,128)}) custom-call(f32[2]{0:T(128)S(1)} %copy-done.10, bf16[32,48,128]{2,1,0:T(8,128)(2,1)S(1)} %all_to_all.21.rows_ref.refs_1_, bf16[256,128]{1,0:T(8,128)(2,1)S(1)} %get-tuple-element.21.refs_2_, bf16[2,16384]{1,0:T(2,128)(2,1)S(1)} %copy-done.6, ...), custom_call_target="tpu_custom_call" | custom-call | tf_op jit(solution)/shard_map/pallas_call | solution.py:229
  81.7 13.6 %all-to-all-done.3.all_ref = bf16[8,256,128]{2,1,0:T(8,128)(2,1)S(1)} async-done(((bf16[8,256,128]{2,1,0:T(8,128)(2,1)}), bf16[8,256,128]{2,1,0:T(8,128)(2,1)S(1)}, u32[]{:S(2)}, u32[]{:S(2)}) %all-to-all-start.3) | async-done | bytes 524320 | tf_op jit(solution)/shard_map/all_to_all | solution.py:240
  95.2 1.4 %shard_map.160 = bf16[2,16384]{1,0:T(2,128)(2,1)} custom-call(f32[2,16]{1,0:T(2,128)S(1)} %dynamic-slice_bitcast_fusion.weight_ref, bf16[8,256,128]{2,1,0:T(8,128)(2,1)S(1)} %all-to-all-done.3.all_ref), custom_call_target="tpu_custom_call" | custom-call | tf_op jit(solution)/shard_map/pallas_call | solution.py:229
  (10 shorter events, 0.0 us)
Async XLA Ops:
  0.6 0.8 copy-start.8
  2.3 12.8 %copy-start = (f32[2,256,128]{2,1,0:T(8,128)S(1)}, f32[2,256,128]{2,1,0:T(8,128)}, u32[]{:S(2)}) copy-start(f32[2,256,128]{2,1,0:T(8,128)} %constant.24.clone.turn_ref.refs_6_) | copy-start | bytes 786436
  2.3 12.8 %copy-start.1 = (bf16[512,256]{1,0:T(8,128)(2,1)S(1)}, bf16[512,256]{1,0:T(8,128)(2,1)}, u32[]{:S(2)}) copy-start(bf16[512,256]{1,0:T(8,128)(2,1)} %constant.22.clone.first_ref) | copy-start | bytes 786436
  2.3 12.8 %copy-start.4 = (bf16[256,256]{1,0:T(8,128)(2,1)S(1)}, bf16[256,256]{1,0:T(8,128)(2,1)}, u32[]{:S(2)}) copy-start(bf16[256,256]{1,0:T(8,128)(2,1)} %constant.25.clone.second_ref) | copy-start | bytes 393220
  2.3 12.8 %copy-start.6 = (bf16[2,16384]{1,0:T(2,128)(2,1)S(1)}, bf16[2,16384]{1,0:T(2,128)(2,1)}, u32[]{:S(2)}) copy-start(bf16[2,16384]{1,0:T(2,128)(2,1)} %refs_3_.1) | copy-start | bytes 196612
  2.3 12.8 %copy-start.7 = (bf16[2,16384]{1,0:T(2,128)(2,1)S(1)}, bf16[2,16384]{1,0:T(2,128)(2,1)}, u32[]{:S(2)}) copy-start(bf16[2,16384]{1,0:T(2,128)(2,1)} %refs_4_.1) | copy-start | bytes 196612
  2.3 12.8 %copy-start.9 = (bf16[2,16384]{1,0:T(2,128)(2,1)S(1)}, bf16[2,16384]{1,0:T(2,128)(2,1)}, u32[]{:S(2)}) copy-start(bf16[2,16384]{1,0:T(2,128)(2,1)} %taps_ref.1) | copy-start | bytes 196612
  2.3 23.4 %all-to-all-start = ((bf16[8,256,128]{2,1,0:T(8,128)(2,1)}), bf16[8,256,128]{2,1,0:T(8,128)(2,1)S(1)}, u32[]{:S(2)}, u32[]{:S(2)}) async-start(bf16[8,256,128]{2,1,0:T(8,128)(2,1)} %shard_map.155), calls=%async_computation | async-start | bytes 1048576 | tf_op jit(solution)/shard_map/all_to_all | solution.py:240
  14.1 0.7 copy-start.11
  15.1 10.6 %copy-start.5 = (bf16[2,16384]{1,0:T(2,128)(2,1)S(1)}, bf16[2,16384]{1,0:T(2,128)(2,1)}, u32[]{:S(2)}) copy-start(bf16[2,16384]{1,0:T(2,128)(2,1)} %query_ref.3) | copy-start | bytes 196612
  56.1 17.7 %copy-start.2 = (bf16[256,512]{1,0:T(8,128)(2,1)S(1)}, bf16[256,512]{1,0:T(8,128)(2,1)}, u32[]{:S(2)}) copy-start(bf16[256,512]{1,0:T(8,128)(2,1)} %constant.23.clone.first_ref.refs_5_) | copy-start | bytes 786436
  56.2 17.6 %copy-start.3 = (bf16[256,256]{1,0:T(8,128)(2,1)S(1)}, bf16[256,256]{1,0:T(8,128)(2,1)}, u32[]{:S(2)}) copy-start(bf16[256,256]{1,0:T(8,128)(2,1)} %constant.26.clone.second_ref.refs_7_) | copy-start | bytes 393220
  73.8 0.7 copy-start.10
  76.3 18.9 %all-to-all-start.3 = ((bf16[8,256,128]{2,1,0:T(8,128)(2,1)}), bf16[8,256,128]{2,1,0:T(8,128)(2,1)S(1)}, u32[]{:S(2)}, u32[]{:S(2)}) async-start(bf16[8,256,128]{2,1,0:T(8,128)(2,1)} %get-tuple-element.19), calls=%async_computation.3 | async-start | bytes 1048576 | tf_op jit(solution)/shard_map/all_to_all | solution.py:240

commit v2 on v1

v2 whole, which is shorter than its diff:
```python
import math

import jax
import jax.numpy as jnp
import numpy as np
from jax import lax
from jax.experimental import pallas as pl
from jax.experimental.pallas import tpu as pltpu
from jax.sharding import PartitionSpec as P

F32 = jnp.float32
BF16 = jnp.bfloat16
CH = 2
GROUP = 8
RING = 4
TILE = 4
BLOCKS = 32
SIDE = 128
ROWS = CH * SIDE
BLOCK = SIDE * SIDE
LENGTH = 2 * BLOCK
FREQ_ROWS = SIDE // BLOCKS
PIECE = CH * FREQ_ROWS
VMEM = pl.BlockSpec(memory_space=pltpu.VMEM)
SMEM = pl.BlockSpec(memory_space=pltpu.SMEM)
HBM = pl.BlockSpec(memory_space=pltpu.HBM)


def tables():
    side = np.arange(SIDE)
    k1 = np.arange(BLOCKS)[:, None, None] * FREQ_ROWS + np.arange(FREQ_ROWS)[None, None, :]
    k1 = np.broadcast_to(k1, (BLOCKS, CH, FREQ_ROWS)).reshape(-1)
    chan = np.broadcast_to(np.arange(CH)[None, :, None], (BLOCKS, CH, FREQ_ROWS)).reshape(-1)
    angle = 2 * np.pi * (k1[:, None] + 0.5) * side[None, :] / (2 * SIDE)
    first = np.zeros((2, ROWS, CH, SIDE))
    for c in range(CH):
        mine = (chan == c)[:, None]
        first[0, :, c] = np.where(mine, np.cos(angle), 0)
        first[1, :, c] = np.where(mine, -np.sin(angle), 0)
    first = first.reshape(2 * ROWS, ROWS)
    turn = 2 * np.pi * (k1[:, None] + 0.5) * side[None, :] / LENGTH
    turn = np.stack([np.cos(turn), np.sin(turn)])
    phase = 2 * np.pi * side[:, None] * side[None, :] / SIDE
    second = np.block([[np.cos(phase), -np.sin(phase)], [np.sin(phase), np.cos(phase)]])
    return (
        jnp.asarray(first, BF16),
        jnp.asarray(first.T, BF16),
        jnp.asarray(turn, F32),
        jnp.asarray(second, BF16),
        jnp.asarray(second.T, BF16),
    )


def square(ref):
    return ref[...].astype(F32).reshape(ROWS, SIDE)


def forward(signal, first, turn, second):
    stage = jnp.dot(first, signal, preferred_element_type=F32)
    real, imag = stage[:ROWS], stage[ROWS:]
    cos, sin = turn[0], turn[1]
    turned = jnp.concatenate(
        [(real * cos + imag * sin).astype(BF16), (imag * cos - real * sin).astype(BF16)], axis=1
    )
    spec = jnp.dot(turned, second, preferred_element_type=F32)
    return spec[:, :SIDE], spec[:, SIDE:]


def pack(real, imag):
    both = jnp.concatenate(
        [real.reshape(BLOCKS, PIECE, SIDE), imag.reshape(BLOCKS, PIECE, SIDE)], axis=1
    )
    return both.astype(BF16)


def inverse(rows, first_t, turn, second_t):
    rows = rows.astype(F32)
    real = rows[:, :PIECE].reshape(ROWS, SIDE)
    imag = rows[:, PIECE:].reshape(ROWS, SIDE)
    spec = jnp.concatenate([real.astype(BF16), imag.astype(BF16)], axis=1)
    stage = jnp.dot(spec, second_t, preferred_element_type=F32)
    real, imag = stage[:, :SIDE], stage[:, SIDE:]
    cos, sin = turn[0], turn[1]
    turned = jnp.concatenate(
        [(real * cos - imag * sin).astype(BF16), (imag * cos + real * sin).astype(BF16)], axis=0
    )
    return jnp.dot(first_t, turned, preferred_element_type=F32) * (2.0 / LENGTH)


def source_kernel(
    key_hbm, value_hbm, taps_hbm, first_hbm, turn_hbm, second_hbm, kv_ref, spec_ref,
    key_ref, value_ref, taps_ref, first_ref, turn_ref, second_ref, sems,
):
    pairs = (
        (key_hbm, key_ref),
        (value_hbm, value_ref),
        (taps_hbm, taps_ref),
        (first_hbm, first_ref),
        (turn_hbm, turn_ref),
        (second_hbm, second_ref),
    )
    copies = [
        pltpu.make_async_copy(src, dst, sems.at[i]) for i, (src, dst) in enumerate(pairs)
    ]
    for copy in copies:
        copy.start()
    for copy in copies:
        copy.wait()
    tables_in = (first_ref[...], turn_ref[...], second_ref[...])
    key_value = (square(key_ref) * square(value_ref)).astype(BF16)
    kv_ref[...] = key_value
    spec_ref[:, :16, :] = pack(*forward(key_value, *tables_in))
    spec_ref[:, 16:, :] = pack(*forward(square(taps_ref).astype(BF16), *tables_in))


def mix_for(weight_ref, pieces, shift, by_row):
    place = lax.axis_index("tensor")
    near, line = place // RING, place % RING
    target = near * RING + (line + shift) % RING
    totals = []
    for c in range(CH):
        total = None
        for half, piece in enumerate(pieces):
            source = (near ^ half) * RING + line
            for i in range(CH):
                to, of = target * CH + c, source * CH + i
                weight = weight_ref[to, of] if by_row else weight_ref[of, to]
                part = weight * piece[i * SIDE : (i + 1) * SIDE]
                total = part if total is None else total + part
        totals.append(total)
    return jnp.concatenate(totals, axis=0)


def mix_parts(weight_ref, pieces, mine_ref, other_refs, by_row):
    mine_ref[...] = mix_for(weight_ref, pieces, 0, by_row)
    for shift, ref in enumerate(other_refs, 1):
        ref[...] = mix_for(weight_ref, pieces, shift, by_row).astype(BF16)


def grad_mix_kernel(weight_ref, near_ref, far_ref, mine_ref, *other_refs):
    mix_parts(weight_ref, [square(near_ref), square(far_ref)], mine_ref, other_refs, True)


def out_mix_kernel(weight_ref, near_ref, far_ref, mine_ref, *other_refs):
    pieces = [near_ref[...].astype(F32), far_ref[...].astype(F32)]
    mix_parts(weight_ref, pieces, mine_ref, other_refs, False)


def total_of(mine_ref, other_refs):
    total = mine_ref[...]
    for ref in other_refs:
        total = total + ref[...].astype(F32)
    return total


def load(spec_ref, sig, buf_ref, slot):
    both = spec_ref[:, 16 * sig : 16 * sig + 16, :].astype(F32)
    buf_ref[slot, 0] = both[:, :PIECE]
    buf_ref[slot, 1] = both[:, PIECE:]


def alternate():
    row = lax.broadcasted_iota(jnp.int32, (PIECE, SIDE), 0)
    return jnp.where(row % 2 == 0, 1.0, -1.0).astype(F32)


def put(out_ref, blk, sig, real, imag):
    both = jnp.concatenate([real, imag], axis=0)
    out_ref[blk, 16 * sig : 16 * sig + 16, :] = both.astype(BF16)


def add(total, real, imag):
    return (real, imag) if total is None else (total[0] + real, total[1] + imag)


def convolve(buf_ref, out_ref, sign):
    def at(slot, blk):
        return buf_ref[slot, 0, blk], buf_ref[slot, 1, blk]

    last = None
    for base in range(0, BLOCKS, TILE):
        sums = [None] * TILE
        window = {}
        for j in range(base + TILE):
            hr, hi = at(1, j)
            for o in range(TILE):
                blk = base + o - j
                if blk < 0:
                    continue
                if blk not in window:
                    window[blk] = at(0, blk)
                xr, xi = window[blk]
                sums[o] = add(sums[o], hr * xr - hi * xi, hr * xi + hi * xr)
        for o in range(TILE):
            real, imag = sums[o]
            if last is not None:
                real, imag = real - sign * last[1], imag + sign * last[0]
            put(out_ref, base + o, 0, real, imag)
            last = sums[o]


def correlate(buf_ref, out_ref, sign, other, sig):
    def at(slot, blk):
        return buf_ref[slot, 0, blk], buf_ref[slot, 1, blk]

    after = None
    for base in range(BLOCKS - TILE, -1, -TILE):
        sums = [None] * TILE
        window = {}
        for j in range(BLOCKS - base):
            hr, hi = at(other, j)
            for o in range(TILE):
                blk = base + o + j
                if blk >= BLOCKS:
                    continue
                if blk not in window:
                    window[blk] = at(2, blk)
                gr, gi = window[blk]
                sums[o] = add(sums[o], gr * hr + gi * hi, gi * hr - gr * hi)
        for o in range(TILE - 1, -1, -1):
            real, imag = sums[o]
            if after is not None:
                real, imag = real + sign * after[1], imag - sign * after[0]
            put(out_ref, base + o, sig, real, imag)
            after = sums[o]


def convolve_kernel(spec_ref, grad_ref, out_ref, buf_ref):
    out_ref[:, 16:, :] = grad_ref[...]
    load(spec_ref, 0, buf_ref, 0)
    load(spec_ref, 1, buf_ref, 1)
    convolve(buf_ref, out_ref, alternate())


def grad_kernel(
    mine_ref, r1_ref, r2_ref, r3_ref, query_ref, first_ref, turn_ref, second_ref,
    gated_ref, inner_ref, out_ref,
):
    grad_gated = total_of(mine_ref, (r1_ref, r2_ref, r3_ref))
    gated_ref[...] = grad_gated
    grad_inner = (grad_gated * square(query_ref)).astype(BF16)
    inner_ref[...] = grad_inner
    out_ref[...] = pack(*forward(grad_inner, first_ref[...], turn_ref[...], second_ref[...]))


def correlate_kernel(spec_ref, rows_ref, out_ref, buf_ref):
    load(spec_ref, 0, buf_ref, 0)
    load(spec_ref, 1, buf_ref, 1)
    load(rows_ref, 1, buf_ref, 2)
    sign = alternate()
    correlate(buf_ref, out_ref, sign, 1, 0)
    correlate(buf_ref, out_ref, sign, 0, 1)


def gate_kernel(
    skip_ref, rows_ref, kv_ref, query_ref, gated_ref, first_ref, turn_ref, second_ref,
    out_ref, grad_query_ref,
):
    convolved = inverse(rows_ref[:, :16, :], first_ref[...], turn_ref[...], second_ref[...])
    inner_sum = convolved + skip_rows(skip_ref) * kv_ref[...].astype(F32)
    out_ref[...] = (square(query_ref) * inner_sum).astype(BF16)
    grad_query_ref[...] = (gated_ref[...] * inner_sum).reshape(CH, BLOCK).astype(BF16)


def skip_rows(skip_ref):
    row = lax.broadcasted_iota(jnp.int32, (ROWS, SIDE), 0)
    return jnp.where(row < SIDE, skip_ref[CH * GROUP, 0], skip_ref[CH * GROUP, 1])


def grads_kernel(
    skip_ref, rows_ref, inner_ref, key_ref, value_ref, first_ref, turn_ref, second_ref,
    grad_key_ref, grad_value_ref, grad_taps_ref, *, scale,
):
    tables_in = (first_ref[...], turn_ref[...], second_ref[...])
    source = inverse(rows_ref[:, :16, :], *tables_in)
    source = source + skip_rows(skip_ref) * inner_ref[...].astype(F32)
    source = source.reshape(CH, BLOCK)
    grad_key_ref[...] = (source * value_ref[...].astype(F32)).astype(BF16)
    grad_value_ref[...] = (source * key_ref[...].astype(F32)).astype(BF16)
    taps = inverse(rows_ref[:, 16:, :], *tables_in) * scale
    grad_taps_ref[...] = taps.reshape(CH, BLOCK)


def output_kernel(mine_ref, r1_ref, r2_ref, r3_ref, out_ref):
    both = total_of(mine_ref, (r1_ref, r2_ref, r3_ref))
    out_ref[...] = both.reshape(CH, BLOCK).astype(BF16)


def call(kernel, outs, operands, smem=0, scratch=(), place=VMEM, limit=48):
    return pl.pallas_call(
        kernel,
        out_shape=[jax.ShapeDtypeStruct(shape, dtype) for shape, dtype in outs],
        in_specs=[SMEM] * smem + [place] * (len(operands) - smem),
        out_specs=[VMEM] * len(outs),
        scratch_shapes=list(scratch),
        compiler_params=pltpu.CompilerParams(vmem_limit_bytes=limit * 1024 * 1024),
    )(*operands)


def exchange(blocks):
    return lax.all_to_all(blocks, "seq", split_axis=0, concat_axis=0, tiled=True)


def along_y(arrays):
    received = []
    for shift, array in enumerate(arrays, 1):
        pairs = [
            (near * RING + line, near * RING + (line + shift) % RING)
            for near in range(GROUP // RING)
            for line in range(RING)
        ]
        received.append(lax.ppermute(array, "tensor", pairs))
    return received


def across(array):
    return lax.ppermute(array, "tensor", [(i, (i + RING) % GROUP) for i in range(GROUP)])


def body(queries, key_feats, value_feats, filter_taps, skip_gain, out_weight, out_grad):
    first, first_t, turn, second, second_t = tables()
    forward_tables = (first, turn, second)
    inverse_tables = (first_t, turn, second_t)
    skip_row = jnp.concatenate([skip_gain, jnp.zeros(2 * CH * GROUP - CH - CH * GROUP, F32)])
    weight = jnp.concatenate([out_weight.astype(F32), skip_row[None]], axis=0)
    square_shape = (ROWS, SIDE)
    tokens = (CH, BLOCK)
    one, two = (BLOCKS, 16, SIDE), (BLOCKS, 32, SIDE)
    parts = [(square_shape, F32)] + [(square_shape, BF16)] * (RING - 1)

    key_value, spec = call(
        source_kernel,
        [(square_shape, BF16), (two, BF16)],
        (key_feats, value_feats, filter_taps, *forward_tables),
        scratch=[
            *[pltpu.VMEM(tokens, BF16)] * 3,
            *[pltpu.VMEM(table.shape, table.dtype) for table in forward_tables],
            pltpu.SemaphoreType.DMA((6,)),
        ],
        place=HBM,
        limit=62,
    )
    spec, far = lax.optimization_barrier((spec, across(out_grad)))
    spec = exchange(spec)
    mine, *others = call(grad_mix_kernel, parts, (weight, out_grad, far), smem=1)
    others = along_y(others)
    grad_gated, grad_inner, grad_spec = call(
        grad_kernel,
        [(square_shape, F32), (square_shape, BF16), (one, BF16)],
        (mine, *others, queries, *forward_tables),
    )
    (rows,) = call(
        convolve_kernel,
        [(two, BF16)],
        (spec, grad_spec),
        scratch=[pltpu.VMEM((2, 2, BLOCKS, PIECE, SIDE), F32)],
    )
    rows = exchange(rows)
    gated, grad_queries = call(
        gate_kernel,
        [(square_shape, BF16), (tokens, BF16)],
        (weight, rows, key_value, queries, grad_gated, *inverse_tables),
        smem=1,
    )
    (corr,) = call(
        correlate_kernel,
        [(two, BF16)],
        (spec, rows),
        scratch=[pltpu.VMEM((3, 2, BLOCKS, PIECE, SIDE), F32)],
    )
    corr, far = lax.optimization_barrier((corr, across(gated)))
    corr = exchange(corr)
    mine, *others = call(out_mix_kernel, parts, (weight, gated, far), smem=1)
    others = along_y(others)

    def grads(*refs):
        grads_kernel(*refs, scale=(BLOCKS * BLOCK) ** -0.5)

    grad_keys, grad_values, grad_taps = call(
        grads,
        [(tokens, BF16), (tokens, BF16), (tokens, F32)],
        (weight, corr, grad_inner, key_feats, value_feats, *inverse_tables),
        smem=1,
    )
    (output,) = call(output_kernel, [(tokens, BF16)], (mine, *others))
    return (output, grad_queries, grad_keys, grad_values, grad_taps)


def solution(mesh):
    assert dict(mesh.shape) == {"tensor": GROUP, "seq": BLOCKS}
    placed = P("tensor", "seq")
    return jax.shard_map(
        body,
        mesh=mesh,
        in_specs=(placed, placed, placed, placed, P("tensor"), P(), placed),
        out_specs=(placed,) * 5,
        check_vma=False,
    )
```

time: 97.8 us -> 76.9 us (0.79)
  blocking collectives: 45.1 us -> 17.9 us
  starting transfers between devices: 15.3 us -> 34 us
  waiting for transfers between devices: 23.5 us -> 11.8 us
  Pallas kernels: 9.56 us -> 12 us
  local copies, waits for them, and re-layouts: 2.46 us -> 0.07 us
    all_to_all x2 -> x1, blocking collectives: 45.1 us -> 17.9 us  [exchange(): lax.all_to_all(blocks, 'seq', split_axis=0, concat_axis=0, tiled=True)]
    ppermute x0 -> x8, starting transfers between devices: none -> 21.2 us  [the longest x2 12.5 us: across(): lax.ppermute(array, 'tensor', [(i, (i + RING) % GROUP) for i in range(GRO...]
    all_to_all x2, waiting for transfers between devices: 23.5 us -> 5.13 us  [exchange(): lax.all_to_all(blocks, 'seq', split_axis=0, concat_axis=0, tiled=True)]
    ppermute x0 -> x8, waiting for transfers between devices: none -> 6.64 us  [the longest x6 5.64 us: along_y(): received.append(lax.ppermute(array, 'tensor', pairs))]
    all_to_all x2, starting transfers between devices: 15.3 us -> 12.8 us  [exchange(): lax.all_to_all(blocks, 'seq', split_axis=0, concat_axis=0, tiled=True)]
    pallas_call x7 -> x9, Pallas kernels: 9.56 us -> 12 us  [call(): pl.pallas_call(kernel, out_shape=[jax.ShapeDtypeStruct(shape, dtype) for...]
    unnamed x25 -> x24, local copies, waits for them, and re-layouts: 2.29 us -> 0.07 us
  transfers between devices with their start and end apart: 2 -> 10, of which waited for: 2 -> 6; matrix products, arithmetic and copies ran while one was open for 0% -> 0% of each run, Pallas kernels for 3% -> 10%
where the time goes in v2:
time: 76.9 us; the launch traced here: 76.5 us
  starting transfers between devices  34 us (44%)
  blocking collectives  17.9 us (23%)
  Pallas kernels  12 us (16%)
  waiting for transfers between devices  11.8 us (15%)
  between operations  0.82 us (1%)
    all_to_all x1, blocking collectives, exchange(): lax.all_to_all(blocks, 'seq', split_axis=0, concat_axis=0, tiled=True)  17.9 us
    all_to_all x2, starting transfers between devices, exchange(): lax.all_to_all(blocks, 'seq', split_axis=0, concat_axis=0, tiled=True)  12.8 us
    ppermute x2, starting transfers between devices, across(): lax.ppermute(array, 'tensor', [(i, (i + RING) % GROUP) for i in range(GRO...  12.5 us
    pallas_call x9, Pallas kernels, call(): pl.pallas_call(kernel, out_shape=[jax.ShapeDtypeStruct(shape, dtype) for...  12 us
    ppermute x6, starting transfers between devices, along_y(): received.append(lax.ppermute(array, 'tensor', pairs))  8.72 us
    ppermute x6, waiting for transfers between devices, along_y(): received.append(lax.ppermute(array, 'tensor', pairs))  5.64 us
    all_to_all x2, waiting for transfers between devices, exchange(): lax.all_to_all(blocks, 'seq', split_axis=0, concat_axis=0, tiled=True)  5.13 us
  transfers between devices with their start and end apart: 10, of which 6 were waited for; matrix products, arithmetic and copies ran while one was open for 0% of the time, Pallas kernels for 10%

profile of v2, /device:TPU:1, one launch (start us, length us, event | category | flops | bytes accessed | tf_op | source)
XLA Modules:
  0.0 76.5 jit_solution(3352325336024387422)
XLA Ops:
  0.6 7.8 %collective-permute-start = (bf16[2,16384]{1,0:T(2,128)(2,1)}, bf16[2,16384]{1,0:T(2,128)(2,1)S(1)}, u32[]{:S(2)}, u32[]{:S(2)}) collective-permute-start(bf16[2,16384]{1,0:T(2,128)(2,1)} %near_ref.1), channel_id=1, source_target_pairs={{0,128},{32,160},{64,192},{96,224},{128,0},{160,32},{192,64},{224,... | collective-permute-start | bytes 196616 | tf_op jit(solution)/shard_map/ppermute | solution.py:317
  8.5 2.6 %shard_map.155 = (bf16[256,128]{1,0:T(8,128)(2,1)}, bf16[32,32,128]{2,1,0:T(8,128)(2,1)}) custom-call(bf16[2,16384]{1,0:T(2,128)(2,1)} %refs_3_.1, bf16[2,16384]{1,0:T(2,128)(2,1)} %refs_4_.1, bf16[2,16384]{1,0:T(2,128)(2,1)} %taps_hbm.1, bf16[512,256]{1,0:T(8,128)(2,1)} %constant.12.clone.first_hbm.first_ref, ...), custom_call_target="tpu_custom_call" | custom-call | tf_op jit(solution)/shard_map/pallas_call | solution.py:290
  11.1 0.0 copy-start
  11.1 0.0 copy-start.2
  11.1 8.1 %all-to-all-start = ((bf16[32,32,128]{2,1,0:T(8,128)(2,1)}), bf16[32,32,128]{2,1,0:T(8,128)(2,1)S(1)}, u32[]{:S(2)}, u32[]{:S(2)}) async-start(bf16[32,32,128]{2,1,0:T(8,128)(2,1)} %get-tuple-element.28), calls=%async_computation | async-start | bytes 524288 | tf_op jit(solution)/shard_map/all_to_all | solution.py:301
  19.3 0.0 copy-start.4
  19.3 0.9 %shard_map.156 = (f32[256,128]{1,0:T(8,128)S(1)}, bf16[256,128]{1,0:T(8,128)(2,1)S(1)}, bf16[256,128]{1,0:T(8,128)(2,1)S(1)}, bf16[256,128]{1,0:T(8,128)(2,1)S(1)}) custom-call(f32[17,16]{1,0:T(8,128)S(1)} %pad_maximum_fusion.weight_ref.skip_ref.refs_0_, bf16[2,16384]{1,0:T(2,128)(2,1)S(1)} %copy-done.9, bf16[2,16384]{1,0:T(2,128)(2,1)S(1)} %collective-permute-done.far_ref), custom_call_target="tpu_custom_call" | custom-call | tf_op jit(solution)/shard_map/pallas_call | solution.py:290
  20.2 1.4 %collective-permute-start.1 = (bf16[256,128]{1,0:T(8,128)(2,1)S(1)}, bf16[256,128]{1,0:T(8,128)(2,1)S(1)}, u32[]{:S(2)}, u32[]{:S(2)}) collective-permute-start(bf16[256,128]{1,0:T(8,128)(2,1)S(1)} %get-tuple-element.31), channel_id=1, source_target_pairs={{0,32},{32,64},{64,96},{96,0},{128,160},{160,192},{192,224},{224,1... | collective-permute-start | bytes 196616 | tf_op jit(solution)/shard_map/ppermute | solution.py:312
  21.6 2.6 %collective-permute-start.2 = (bf16[256,128]{1,0:T(8,128)(2,1)S(1)}, bf16[256,128]{1,0:T(8,128)(2,1)S(1)}, u32[]{:S(2)}, u32[]{:S(2)}) collective-permute-start(bf16[256,128]{1,0:T(8,128)(2,1)S(1)} %get-tuple-element.32), channel_id=1, source_target_pairs={{0,64},{32,96},{64,0},{96,32},{128,192},{160,224},{192,128},{224,1... | collective-permute-start | bytes 196616 | tf_op jit(solution)/shard_map/ppermute | solution.py:312
  24.2 1.1 %collective-permute-start.3 = (bf16[256,128]{1,0:T(8,128)(2,1)S(1)}, bf16[256,128]{1,0:T(8,128)(2,1)S(1)}, u32[]{:S(2)}, u32[]{:S(2)}) collective-permute-start(bf16[256,128]{1,0:T(8,128)(2,1)S(1)} %get-tuple-element.33), channel_id=1, source_target_pairs={{0,96},{32,0},{64,32},{96,64},{128,224},{160,128},{192,160},{224,1... | collective-permute-start | bytes 196616 | tf_op jit(solution)/shard_map/ppermute | solution.py:312
  25.3 2.3 %collective-permute-done.2.r2_ref = bf16[256,128]{1,0:T(8,128)(2,1)S(1)} collective-permute-done((bf16[256,128]{1,0:T(8,128)(2,1)S(1)}, bf16[256,128]{1,0:T(8,128)(2,1)S(1)}, u32[]{:S(2)}, u32[]{:S(2)}) %collective-permute-start.2) | collective-permute-done | bytes 65568 | tf_op jit(solution)/shard_map/ppermute | solution.py:312
  27.6 0.0 collective-permute-done.3.r3_ref
  27.7 0.4 shard_map.157
  28.1 2.4 %all-to-all-done.spec_ref = bf16[32,32,128]{2,1,0:T(8,128)(2,1)S(1)} async-done(((bf16[32,32,128]{2,1,0:T(8,128)(2,1)}), bf16[32,32,128]{2,1,0:T(8,128)(2,1)S(1)}, u32[]{:S(2)}, u32[]{:S(2)}) %all-to-all-start) | async-done | bytes 262176 | tf_op jit(solution)/shard_map/all_to_all | solution.py:301
  30.5 0.6 shard_map.158
  31.2 0.0 copy-start.1
  31.2 17.9 %all_to_all.15.rows_ref = bf16[32,32,128]{2,1,0:T(8,128)(2,1)S(1)} all-to-all(bf16[32,32,128]{2,1,0:T(8,128)(2,1)S(1)} %shard_map.158), channel_id=1, replica_groups=mesh['tensor'=8,'seq'=32] {'seq'}, dimensions={0} | all-to-all | bytes 524288 | tf_op jit(solution)/shard_map/all_to_all | solution.py:301
  49.1 1.9 %shard_map.159 = (bf16[256,128]{1,0:T(8,128)(2,1)S(1)}, bf16[2,16384]{1,0:T(2,128)(2,1)}) custom-call(f32[17,16]{1,0:T(8,128)S(1)} %pad_maximum_fusion.weight_ref.skip_ref.refs_0_, bf16[32,32,128]{2,1,0:T(8,128)(2,1)S(1)} %all_to_all.15.rows_ref, bf16[256,128]{1,0:T(8,128)(2,1)S(1)} %copy-done.8, bf16[2,16384]{1,0:T(2,128)(2,1)S(1)} %copy-done.5, ...), custom_call_target="tpu_custom_call" | custom-call | tf_op jit(solution)/shard_map/pallas_call | solution.py:290
  51.0 4.7 %collective-permute-start.4 = (bf16[256,128]{1,0:T(8,128)(2,1)S(1)}, bf16[256,128]{1,0:T(8,128)(2,1)S(1)}, u32[]{:S(2)}, u32[]{:S(2)}) collective-permute-start(bf16[256,128]{1,0:T(8,128)(2,1)S(1)} %get-tuple-element.37.near_ref), channel_id=1, source_target_pairs={{0,128},{32,160},{64,192},{96,224},{128,0},{160,32},{192,64},{224,... | collective-permute-start | bytes 196616 | tf_op jit(solution)/shard_map/ppermute | solution.py:317
  55.7 1.9 %shard_map.160 = bf16[32,32,128]{2,1,0:T(8,128)(2,1)} custom-call(bf16[32,32,128]{2,1,0:T(8,128)(2,1)S(1)} %all-to-all-done.spec_ref, bf16[32,32,128]{2,1,0:T(8,128)(2,1)S(1)} %all_to_all.15.rows_ref), custom_call_target="tpu_custom_call" | custom-call | tf_op jit(solution)/shard_map/pallas_call | solution.py:290
  57.5 1.0 %collective-permute-done.4.far_ref = bf16[256,128]{1,0:T(8,128)(2,1)S(1)} collective-permute-done((bf16[256,128]{1,0:T(8,128)(2,1)S(1)}, bf16[256,128]{1,0:T(8,128)(2,1)S(1)}, u32[]{:S(2)}, u32[]{:S(2)}) %collective-permute-start.4) | collective-permute-done | bytes 65568 | tf_op jit(solution)/shard_map/ppermute | solution.py:317
  58.6 4.6 %all-to-all-start.2 = ((bf16[32,32,128]{2,1,0:T(8,128)(2,1)}), bf16[32,32,128]{2,1,0:T(8,128)(2,1)S(1)}, u32[]{:S(2)}, u32[]{:S(2)}) async-start(bf16[32,32,128]{2,1,0:T(8,128)(2,1)} %shard_map.160), calls=%async_computation.2 | async-start | bytes 524288 | tf_op jit(solution)/shard_map/all_to_all | solution.py:301
  63.2 0.9 %shard_map.161 = (f32[256,128]{1,0:T(8,128)S(1)}, bf16[256,128]{1,0:T(8,128)(2,1)S(1)}, bf16[256,128]{1,0:T(8,128)(2,1)S(1)}, bf16[256,128]{1,0:T(8,128)(2,1)S(1)}) custom-call(f32[17,16]{1,0:T(8,128)S(1)} %pad_maximum_fusion.weight_ref.skip_ref.refs_0_, bf16[256,128]{1,0:T(8,128)(2,1)S(1)} %get-tuple-element.37.near_ref, ...), custom_call_target="tpu_custom_call" | custom-call | tf_op jit(solution)/shard_map/pallas_call | solution.py:290
  64.1 0.3 collective-permute-start.5
  64.4 3.2 %collective-permute-start.6 = (bf16[256,128]{1,0:T(8,128)(2,1)S(1)}, bf16[256,128]{1,0:T(8,128)(2,1)S(1)}, u32[]{:S(2)}, u32[]{:S(2)}) collective-permute-start(bf16[256,128]{1,0:T(8,128)(2,1)S(1)} %get-tuple-element.41), channel_id=1, source_target_pairs={{0,64},{32,96},{64,0},{96,32},{128,192},{160,224},{192,128},{224,1... | collective-permute-start | bytes 196616 | tf_op jit(solution)/shard_map/ppermute | solution.py:312
  67.6 0.1 collective-permute-start.7
  67.8 1.1 %collective-permute-done.5.r1_ref = bf16[256,128]{1,0:T(8,128)(2,1)S(1)} collective-permute-done((bf16[256,128]{1,0:T(8,128)(2,1)S(1)}, bf16[256,128]{1,0:T(8,128)(2,1)S(1)}, u32[]{:S(2)}, u32[]{:S(2)}) %collective-permute-start.5) | collective-permute-done | bytes 65568 | tf_op jit(solution)/shard_map/ppermute | solution.py:312
  68.8 2.2 %collective-permute-done.6.r2_ref = bf16[256,128]{1,0:T(8,128)(2,1)S(1)} collective-permute-done((bf16[256,128]{1,0:T(8,128)(2,1)S(1)}, bf16[256,128]{1,0:T(8,128)(2,1)S(1)}, u32[]{:S(2)}, u32[]{:S(2)}) %collective-permute-start.6) | collective-permute-done | bytes 65568 | tf_op jit(solution)/shard_map/ppermute | solution.py:312
  71.0 0.0 collective-permute-done.7.r3_ref
  71.1 0.7 shard_map.162
  71.8 2.7 %all-to-all-done.2.refs_1_ = bf16[32,32,128]{2,1,0:T(8,128)(2,1)S(1)} async-done(((bf16[32,32,128]{2,1,0:T(8,128)(2,1)}), bf16[32,32,128]{2,1,0:T(8,128)(2,1)S(1)}, u32[]{:S(2)}, u32[]{:S(2)}) %all-to-all-start.2) | async-done | bytes 262176 | tf_op jit(solution)/shard_map/all_to_all | solution.py:301
  74.5 2.0 %shard_map.163 = (bf16[2,16384]{1,0:T(2,128)(2,1)}, bf16[2,16384]{1,0:T(2,128)(2,1)}, f32[2,16384]{1,0:T(2,128)}) custom-call(f32[17,16]{1,0:T(8,128)S(1)} %pad_maximum_fusion.weight_ref.skip_ref.refs_0_, bf16[32,32,128]{2,1,0:T(8,128)(2,1)S(1)} %all-to-all-done.2.refs_1_, bf16[256,128]{1,0:T(8,128)(2,1)S(1)} %get-tuple-element.45.refs_2_, ...), custom_call_target="tpu_custom_call" | custom-call | tf_op jit(solution)/shard_map/pallas_call | solution.py:290
  (25 shorter events, 0.1 us)
Async XLA Ops:
  0.6 10.5 %collective-permute-start = (bf16[2,16384]{1,0:T(2,128)(2,1)}, bf16[2,16384]{1,0:T(2,128)(2,1)S(1)}, u32[]{:S(2)}, u32[]{:S(2)}) collective-permute-start(bf16[2,16384]{1,0:T(2,128)(2,1)} %near_ref.1), channel_id=1, source_target_pairs={{0,128},{32,160},{64,192},{96,224},{128,0},{160,32},{192,64},{224,... | collective-permute-start | bytes 196616 | tf_op jit(solution)/shard_map/ppermute | solution.py:317
  8.5 10.8 %copy-start.10 = (bf16[16,16]{1,0:T(8,128)(2,1)S(1)}, bf16[16,16]{1,0:T(8,128)(2,1)}, u32[]{:S(2)}) copy-start(bf16[16,16]{1,0:T(8,128)(2,1)} %param.17) | copy-start | bytes 1540
  8.5 10.9 %copy-start.9 = (bf16[2,16384]{1,0:T(2,128)(2,1)S(1)}, bf16[2,16384]{1,0:T(2,128)(2,1)}, u32[]{:S(2)}) copy-start(bf16[2,16384]{1,0:T(2,128)(2,1)} %near_ref.1) | copy-start | bytes 196612
  8.5 19.2 %copy-start.5 = (bf16[2,16384]{1,0:T(2,128)(2,1)S(1)}, bf16[2,16384]{1,0:T(2,128)(2,1)}, u32[]{:S(2)}) copy-start(bf16[2,16384]{1,0:T(2,128)(2,1)} %query_ref.3) | copy-start | bytes 196612
  11.1 8.2 %copy-start.11 = (f32[2]{0:T(128)S(1)}, f32[2]{0:T(128)}, u32[]{:S(2)}) copy-start(f32[2]{0:T(128)} %param.16) | copy-start | bytes 28
  11.1 16.5 %copy-start = (f32[2,256,128]{2,1,0:T(8,128)S(1)}, f32[2,256,128]{2,1,0:T(8,128)}, u32[]{:S(2)}) copy-start(f32[2,256,128]{2,1,0:T(8,128)} %constant.14.clone.turn_hbm.turn_ref.refs_6_) | copy-start | bytes 786436
  11.1 16.5 %copy-start.2 = (bf16[512,256]{1,0:T(8,128)(2,1)S(1)}, bf16[512,256]{1,0:T(8,128)(2,1)}, u32[]{:S(2)}) copy-start(bf16[512,256]{1,0:T(8,128)(2,1)} %constant.12.clone.first_hbm.first_ref) | copy-start | bytes 786436
  11.1 19.4 %all-to-all-start = ((bf16[32,32,128]{2,1,0:T(8,128)(2,1)}), bf16[32,32,128]{2,1,0:T(8,128)(2,1)S(1)}, u32[]{:S(2)}, u32[]{:S(2)}) async-start(bf16[32,32,128]{2,1,0:T(8,128)(2,1)} %get-tuple-element.28), calls=%async_computation | async-start | bytes 524288 | tf_op jit(solution)/shard_map/all_to_all | solution.py:301
  19.3 8.4 %copy-start.4 = (bf16[256,256]{1,0:T(8,128)(2,1)S(1)}, bf16[256,256]{1,0:T(8,128)(2,1)}, u32[]{:S(2)}) copy-start(bf16[256,256]{1,0:T(8,128)(2,1)} %constant.15.clone.second_hbm.second_ref) | copy-start | bytes 393220
  20.2 5.1 %collective-permute-start.1 = (bf16[256,128]{1,0:T(8,128)(2,1)S(1)}, bf16[256,128]{1,0:T(8,128)(2,1)S(1)}, u32[]{:S(2)}, u32[]{:S(2)}) collective-permute-start(bf16[256,128]{1,0:T(8,128)(2,1)S(1)} %get-tuple-element.31), channel_id=1, source_target_pairs={{0,32},{32,64},{64,96},{96,0},{128,160},{160,192},{192,224},{224,1... | collective-permute-start | bytes 196616 | tf_op jit(solution)/shard_map/ppermute | solution.py:312
  21.6 6.0 %collective-permute-start.2 = (bf16[256,128]{1,0:T(8,128)(2,1)S(1)}, bf16[256,128]{1,0:T(8,128)(2,1)S(1)}, u32[]{:S(2)}, u32[]{:S(2)}) collective-permute-start(bf16[256,128]{1,0:T(8,128)(2,1)S(1)} %get-tuple-element.32), channel_id=1, source_target_pairs={{0,64},{32,96},{64,0},{96,32},{128,192},{160,224},{192,128},{224,1... | collective-permute-start | bytes 196616 | tf_op jit(solution)/shard_map/ppermute | solution.py:312
  24.2 3.4 %collective-permute-start.3 = (bf16[256,128]{1,0:T(8,128)(2,1)S(1)}, bf16[256,128]{1,0:T(8,128)(2,1)S(1)}, u32[]{:S(2)}, u32[]{:S(2)}) collective-permute-start(bf16[256,128]{1,0:T(8,128)(2,1)S(1)} %get-tuple-element.33), channel_id=1, source_target_pairs={{0,96},{32,0},{64,32},{96,64},{128,224},{160,128},{192,160},{224,1... | collective-permute-start | bytes 196616 | tf_op jit(solution)/shard_map/ppermute | solution.py:312
  31.2 17.9 %copy-start.1 = (bf16[256,512]{1,0:T(8,128)(2,1)S(1)}, bf16[256,512]{1,0:T(8,128)(2,1)}, u32[]{:S(2)}) copy-start(bf16[256,512]{1,0:T(8,128)(2,1)} %constant.13.clone.first_ref.refs_5_) | copy-start | bytes 786436
  31.2 17.9 %copy-start.3 = (bf16[256,256]{1,0:T(8,128)(2,1)S(1)}, bf16[256,256]{1,0:T(8,128)(2,1)}, u32[]{:S(2)}) copy-start(bf16[256,256]{1,0:T(8,128)(2,1)} %constant.16.clone.second_ref.refs_7_) | copy-start | bytes 393220
  31.2 17.9 %copy-start.8 = (bf16[256,128]{1,0:T(8,128)(2,1)S(1)}, bf16[256,128]{1,0:T(8,128)(2,1)}, u32[]{:S(2)}) copy-start(bf16[256,128]{1,0:T(8,128)(2,1)} %get-tuple-element.35.kv_ref) | copy-start | bytes 196612
  51.0 7.6 %collective-permute-start.4 = (bf16[256,128]{1,0:T(8,128)(2,1)S(1)}, bf16[256,128]{1,0:T(8,128)(2,1)S(1)}, u32[]{:S(2)}, u32[]{:S(2)}) collective-permute-start(bf16[256,128]{1,0:T(8,128)(2,1)S(1)} %get-tuple-element.37.near_ref), channel_id=1, source_target_pairs={{0,128},{32,160},{64,192},{96,224},{128,0},{160,32},{192,64},{224,... | collective-permute-start | bytes 196616 | tf_op jit(solution)/shard_map/ppermute | solution.py:317
  58.6 15.9 %all-to-all-start.2 = ((bf16[32,32,128]{2,1,0:T(8,128)(2,1)}), bf16[32,32,128]{2,1,0:T(8,128)(2,1)S(1)}, u32[]{:S(2)}, u32[]{:S(2)}) async-start(bf16[32,32,128]{2,1,0:T(8,128)(2,1)} %shard_map.160), calls=%async_computation.2 | async-start | bytes 524288 | tf_op jit(solution)/shard_map/all_to_all | solution.py:301
  64.1 4.7 %collective-permute-start.5 = (bf16[256,128]{1,0:T(8,128)(2,1)S(1)}, bf16[256,128]{1,0:T(8,128)(2,1)S(1)}, u32[]{:S(2)}, u32[]{:S(2)}) collective-permute-start(bf16[256,128]{1,0:T(8,128)(2,1)S(1)} %get-tuple-element.40), channel_id=1, source_target_pairs={{0,32},{32,64},{64,96},{96,0},{128,160},{160,192},{192,224},{224,1... | collective-permute-start | bytes 196616 | tf_op jit(solution)/shard_map/ppermute | solution.py:312
  64.4 6.6 %collective-permute-start.6 = (bf16[256,128]{1,0:T(8,128)(2,1)S(1)}, bf16[256,128]{1,0:T(8,128)(2,1)S(1)}, u32[]{:S(2)}, u32[]{:S(2)}) collective-permute-start(bf16[256,128]{1,0:T(8,128)(2,1)S(1)} %get-tuple-element.41), channel_id=1, source_target_pairs={{0,64},{32,96},{64,0},{96,32},{128,192},{160,224},{192,128},{224,1... | collective-permute-start | bytes 196616 | tf_op jit(solution)/shard_map/ppermute | solution.py:312
  67.6 3.4 %collective-permute-start.7 = (bf16[256,128]{1,0:T(8,128)(2,1)S(1)}, bf16[256,128]{1,0:T(8,128)(2,1)S(1)}, u32[]{:S(2)}, u32[]{:S(2)}) collective-permute-start(bf16[256,128]{1,0:T(8,128)(2,1)S(1)} %get-tuple-element.42), channel_id=1, source_target_pairs={{0,96},{32,0},{64,32},{96,64},{128,224},{160,128},{192,160},{224,1... | collective-permute-start | bytes 196616 | tf_op jit(solution)/shard_map/ppermute | solution.py:312
  71.1 3.4 %copy-start.6 = (bf16[2,16384]{1,0:T(2,128)(2,1)S(1)}, bf16[2,16384]{1,0:T(2,128)(2,1)}, u32[]{:S(2)}) copy-start(bf16[2,16384]{1,0:T(2,128)(2,1)} %refs_3_.1) | copy-start | bytes 196612
  71.1 3.4 %copy-start.7 = (bf16[2,16384]{1,0:T(2,128)(2,1)S(1)}, bf16[2,16384]{1,0:T(2,128)(2,1)}, u32[]{:S(2)}) copy-start(bf16[2,16384]{1,0:T(2,128)(2,1)} %refs_4_.1) | copy-start | bytes 196612

commit v3 on v2

v3 whole, which is shorter than its diff:
```python
import math

import jax
import jax.numpy as jnp
import numpy as np
from jax import lax
from jax.experimental import pallas as pl
from jax.experimental.pallas import tpu as pltpu
from jax.sharding import PartitionSpec as P

F32 = jnp.float32
BF16 = jnp.bfloat16
CH = 2
GROUP = 8
RING = 4
CHUNK = 16
WEIGHTS = RING * CH * 2 * CH
TILE = 4
BLOCKS = 32
SIDE = 128
ROWS = CH * SIDE
BLOCK = SIDE * SIDE
LENGTH = 2 * BLOCK
PIECE = ROWS // BLOCKS
VMEM = pl.BlockSpec(memory_space=pltpu.VMEM)
COST = pl.CostEstimate(flops=10000000000, bytes_accessed=1000000, transcendentals=0)
SMEM = pl.BlockSpec(memory_space=pltpu.SMEM)
HBM = pl.BlockSpec(memory_space=pltpu.HBM)
ANY = pl.BlockSpec(memory_space=pl.ANY)


def tables():
    side = np.arange(SIDE)
    angle = 2 * np.pi * (side[:, None] + 0.5) * side[None, :] / (2 * SIDE)
    first = np.concatenate([np.cos(angle), -np.sin(angle)], axis=0)
    angle = 2 * np.pi * (side[:, None] + 0.5) * side[None, :] / LENGTH
    turn = np.stack([np.cos(angle), np.sin(angle)])
    angle = 2 * np.pi * side[:, None] * side[None, :] / SIDE
    second = np.stack([np.cos(angle), np.sin(angle)])
    return (
        jnp.asarray(first, BF16),
        jnp.asarray(first.T, BF16),
        jnp.asarray(turn, F32),
        jnp.asarray(second, BF16),
    )


def square(ref):
    return ref[...].astype(F32).reshape(ROWS, SIDE)


def second_stage(second, sign):
    cos, sin = second[0], second[1]
    top = [cos, sin] if sign > 0 else [cos, -sin]
    low = [-sin, cos] if sign > 0 else [sin, cos]
    return jnp.concatenate(
        [jnp.concatenate(top, axis=1), jnp.concatenate(low, axis=1)], axis=0
    )


def forward(signal, first, turn, second):
    both = jnp.concatenate([signal[:SIDE], signal[SIDE:]], axis=1)
    stage = jnp.dot(first, both, preferred_element_type=F32)
    cos, sin = turn[0], turn[1]
    turned = []
    for c in range(CH):
        real, imag = (stage[p * SIDE : (p + 1) * SIDE, c * SIDE : (c + 1) * SIDE] for p in (0, 1))
        turned.append(
            jnp.concatenate(
                [(real * cos + imag * sin).astype(BF16), (imag * cos - real * sin).astype(BF16)],
                axis=1,
            )
        )
    spec = jnp.dot(
        jnp.concatenate(turned, axis=0), second_stage(second, -1), preferred_element_type=F32
    )
    parts = [spec[:, p * SIDE : (p + 1) * SIDE].reshape(BLOCKS, PIECE, SIDE) for p in (0, 1)]
    return jnp.concatenate(parts, axis=1).astype(BF16)


def inverse(rows, first_t, turn, second):
    rows = rows.astype(F32)
    real = rows[:, :PIECE].reshape(ROWS, SIDE)
    imag = rows[:, PIECE:].reshape(ROWS, SIDE)
    spec = jnp.concatenate([real.astype(BF16), imag.astype(BF16)], axis=1)
    stage = jnp.dot(spec, second_stage(second, 1), preferred_element_type=F32)
    cos, sin = turn[0], turn[1]
    turned = []
    for c in range(CH):
        real, imag = (stage[c * SIDE : (c + 1) * SIDE, p * SIDE : (p + 1) * SIDE] for p in (0, 1))
        turned.append(
            jnp.concatenate(
                [(real * cos - imag * sin).astype(BF16), (imag * cos + real * sin).astype(BF16)],
                axis=0,
            )
        )
    both = jnp.dot(first_t, jnp.concatenate(turned, axis=1), preferred_element_type=F32)
    both = both * (2.0 / LENGTH)
    return jnp.concatenate([both[:, :SIDE], both[:, SIDE:]], axis=0)


def source_kernel(
    key_hbm, value_hbm, taps_hbm, weight_hbm, skip_hbm, first_hbm, turn_hbm, second_hbm,
    table_ref, kv_hbm, spec_hbm,
    key_ref, value_ref, taps_ref, weight_ref, skip_ref, first_ref, turn_ref, second_ref,
    kv_ref, spec_ref, sems,
):
    copies = []

    def send(src, dst):
        copy = pltpu.make_async_copy(src, dst, sems.at[len(copies)])
        copy.start()
        copies.append(copy)

    def part(sig):
        return spec_hbm.at[:, pl.ds(16 * sig, 16), :]

    send(taps_hbm, taps_ref)
    send(first_hbm, first_ref)
    send(turn_hbm, turn_ref)
    send(second_hbm, second_ref)
    send(key_hbm, key_ref)
    send(value_hbm, value_ref)
    send(weight_hbm, weight_ref)
    send(skip_hbm, skip_ref)
    for copy in copies:
        copy.wait()
    arrived = len(copies)
    tables_in = (first_ref[...], turn_ref[...], second_ref[...])
    spec_ref[1] = forward(square(taps_ref).astype(BF16), *tables_in)
    send(spec_ref.at[1], part(1))
    key_value = (square(key_ref) * square(value_ref)).astype(BF16)
    kv_ref[...] = key_value
    send(kv_ref, kv_hbm)
    spec_ref[0] = forward(key_value, *tables_in)
    send(spec_ref.at[0], part(0))
    table_ref[:WEIGHTS, :] = weight_rows(weight_ref[...], True)
    table_ref[WEIGHTS : 2 * WEIGHTS, :] = weight_rows(weight_ref[...], False)
    row = lax.broadcasted_iota(jnp.int32, (8, SIDE), 0)
    table_ref[2 * WEIGHTS :, :] = jnp.where(row == 0, skip_ref[0], skip_ref[1])
    for copy in copies[arrived:]:
        copy.wait()


def weight_rows(weight, by_row):
    place = lax.axis_index("tensor")
    near, line = place // RING, place % RING
    shape = (WEIGHTS, CH * GROUP)
    row = lax.broadcasted_iota(jnp.int32, shape, 0)
    column = lax.broadcasted_iota(jnp.int32, shape, 1)
    shift, chan, half, i = row // 8, row // 4 % 2, row // 2 % 2, row % 2
    to = (near * RING + (line + shift) % RING) * CH + chan
    of = ((near ^ half) * RING + line) * CH + i
    first, last = (to, of) if by_row else (of, to)
    pick = jnp.where(column == first, 1.0, 0.0).astype(BF16)
    picked = jnp.dot(pick, weight, preferred_element_type=F32)
    value = jnp.sum(jnp.where(column == last, picked, 0.0), axis=1, keepdims=True)
    return jnp.broadcast_to(value, (WEIGHTS, SIDE))


def mix_parts(table_ref, first_row, pieces, mine_ref, other_refs):
    for base in range(0, SIDE, CHUNK):
        loaded = [
            piece[i * SIDE + base : i * SIDE + base + CHUNK, :].astype(F32)
            for piece in pieces
            for i in range(CH)
        ]
        for shift in range(RING):
            for c in range(CH):
                total = None
                for i, value in enumerate(loaded):
                    row = first_row + (shift * CH + c) * 4 + i
                    part = table_ref[row : row + 1, :] * value
                    total = part if total is None else total + part
                place_rows = pl.ds(c * SIDE + base, CHUNK)
                if shift == 0:
                    mine_ref[place_rows, :] = total
                else:
                    other_refs[shift - 1][place_rows, :] = total.astype(BF16)


def grad_mix_kernel(table_ref, near_ref, far_ref, mine_ref, *rest):
    other_refs, squares = rest[: RING - 1], rest[RING - 1 :]
    for ref, buf in zip((near_ref, far_ref), squares):
        buf[...] = square(ref)
    mix_parts(table_ref, 0, squares, mine_ref, other_refs)


def out_mix_kernel(table_ref, near_ref, far_ref, mine_ref, *other_refs):
    mix_parts(table_ref, WEIGHTS, (near_ref, far_ref), mine_ref, other_refs)


def total_of(mine_ref, other_refs):
    total = mine_ref[...]
    for ref in other_refs:
        total = total + ref[...].astype(F32)
    return total


def load(spec_ref, sig, buf_ref, slot):
    both = spec_ref[:, 16 * sig : 16 * sig + 16, :].astype(F32)
    buf_ref[slot, 0] = both[:, :PIECE]
    buf_ref[slot, 1] = both[:, PIECE:]


def alternate():
    row = lax.broadcasted_iota(jnp.int32, (PIECE, SIDE), 0)
    return jnp.where(row % 2 == 0, 1.0, -1.0).astype(F32)


def put(out_ref, blk, sig, real, imag):
    both = jnp.concatenate([real, imag], axis=0)
    out_ref[blk, 16 * sig : 16 * sig + 16, :] = both.astype(BF16)


def add(total, parts):
    return parts if total is None else tuple(t + p for t, p in zip(total, parts))


def convolve(buf_ref, out_ref, sign):
    def at(slot, blk):
        return buf_ref[slot, 0, blk], buf_ref[slot, 1, blk]

    last = None
    for base in range(0, BLOCKS, TILE):
        sums = [None] * TILE
        window = {}
        for j in range(base + TILE):
            hr, hi = at(1, j)
            plus, minus = hr + hi, hi - hr
            for o in range(TILE):
                blk = base + o - j
                if blk < 0:
                    continue
                if blk not in window:
                    xr, xi = at(0, blk)
                    window[blk] = (xr, xi, xr + xi)
                xr, xi, both = window[blk]
                sums[o] = add(sums[o], (hr * both, xi * plus, xr * minus))
        for o in range(TILE):
            common, of_real, of_imag = sums[o]
            total = (common - of_real, common + of_imag)
            real, imag = total
            if last is not None:
                real, imag = real - sign * last[1], imag + sign * last[0]
            put(out_ref, base + o, 0, real, imag)
            last = total


def correlate(buf_ref, out_ref, sign, other, sig):
    def at(slot, blk):
        return buf_ref[slot, 0, blk], buf_ref[slot, 1, blk]

    after = None
    for base in range(BLOCKS - TILE, -1, -TILE):
        sums = [None] * TILE
        window = {}
        for j in range(BLOCKS - base):
            hr, hi = at(other, j)
            plus, minus = hr + hi, hr - hi
            for o in range(TILE):
                blk = base + o + j
                if blk >= BLOCKS:
                    continue
                if blk not in window:
                    gr, gi = at(2, blk)
                    window[blk] = (gr, gi, gr + gi)
                gr, gi, both = window[blk]
                sums[o] = add(sums[o], (hr * both, gi * minus, gr * plus))
        for o in range(TILE - 1, -1, -1):
            common, of_real, of_imag = sums[o]
            total = (common - of_real, common - of_imag)
            real, imag = total
            if after is not None:
                real, imag = real + sign * after[1], imag - sign * after[0]
            put(out_ref, base + o, sig, real, imag)
            after = total


def convolve_kernel(spec_ref, grad_ref, out_ref, buf_ref):
    out_ref[:, 16:, :] = grad_ref[...]
    load(spec_ref, 0, buf_ref, 0)
    load(spec_ref, 1, buf_ref, 1)
    convolve(buf_ref, out_ref, alternate())


def grad_kernel(
    mine_ref, r1_ref, r2_ref, r3_ref, query_ref, first_ref, turn_ref, second_ref,
    gated_ref, inner_ref, out_ref,
):
    grad_gated = total_of(mine_ref, (r1_ref, r2_ref, r3_ref))
    gated_ref[...] = grad_gated
    grad_inner = (grad_gated * square(query_ref)).astype(BF16)
    inner_ref[...] = grad_inner
    out_ref[...] = forward(grad_inner, first_ref[...], turn_ref[...], second_ref[...])


def correlate_kernel(
    spec_ref, rows_ref, inner_sum_ref, gated_ref, out_hbm, grad_query_hbm,
    buf_ref, out_ref, grad_query_ref, sems,
):
    grad_query_ref[...] = (gated_ref[...] * inner_sum_ref[...]).reshape(CH, BLOCK).astype(BF16)
    query_copy = pltpu.make_async_copy(grad_query_ref, grad_query_hbm, sems.at[0])
    query_copy.start()
    load(spec_ref, 0, buf_ref, 0)
    load(spec_ref, 1, buf_ref, 1)
    load(rows_ref, 1, buf_ref, 2)
    sign = alternate()
    copies = []
    for sig, other in ((0, 1), (1, 0)):
        correlate(buf_ref, out_ref.at[sig], sign, other, 0)
        copy = pltpu.make_async_copy(
            out_ref.at[sig], out_hbm.at[:, pl.ds(16 * sig, 16), :], sems.at[1 + sig]
        )
        copy.start()
        copies.append(copy)
    for copy in copies:
        copy.wait()
    query_copy.wait()


def gate_kernel(
    skip_ref, rows_ref, kv_ref, query_ref, first_ref, turn_ref, second_ref, out_ref, inner_sum_ref
):
    convolved = inverse(rows_ref[:, :16, :], first_ref[...], turn_ref[...], second_ref[...])
    inner_sum = convolved + skip_rows(skip_ref) * kv_ref[...].astype(F32)
    inner_sum_ref[...] = inner_sum
    out_ref[...] = (square(query_ref) * inner_sum).astype(BF16)


def skip_rows(table_ref):
    return jnp.concatenate(
        [
            jnp.broadcast_to(table_ref[2 * WEIGHTS + c : 2 * WEIGHTS + c + 1, :], (SIDE, SIDE))
            for c in range(CH)
        ],
        axis=0,
    )


def last_kernel(
    table_ref, rows_ref, inner_ref, key_ref, value_ref, first_ref, turn_ref, second_ref,
    mine_ref, r1_ref, r2_ref, r3_ref,
    out_hbm, grad_key_hbm, grad_value_hbm, grad_taps_hbm,
    out_ref, grad_key_ref, grad_value_ref, grad_taps_ref, sems, *, scale,
):
    copies = []

    def send(src, dst):
        copy = pltpu.make_async_copy(src, dst, sems.at[len(copies)])
        copy.start()
        copies.append(copy)

    both = total_of(mine_ref, (r1_ref, r2_ref, r3_ref))
    out_ref[...] = both.reshape(CH, BLOCK).astype(BF16)
    send(out_ref, out_hbm)
    tables_in = (first_ref[...], turn_ref[...], second_ref[...])
    taps = inverse(rows_ref[:, 16:, :], *tables_in) * scale
    grad_taps_ref[...] = taps.reshape(CH, BLOCK)
    send(grad_taps_ref, grad_taps_hbm)
    source = inverse(rows_ref[:, :16, :], *tables_in)
    source = source + skip_rows(table_ref) * inner_ref[...].astype(F32)
    source = source.reshape(CH, BLOCK)
    grad_key_ref[...] = (source * value_ref[...].astype(F32)).astype(BF16)
    send(grad_key_ref, grad_key_hbm)
    grad_value_ref[...] = (source * key_ref[...].astype(F32)).astype(BF16)
    send(grad_value_ref, grad_value_hbm)
    for copy in copies:
        copy.wait()


def call(kernel, outs, operands, smem=0, scratch=(), place=VMEM, limit=48, cost=None, out_place=VMEM):
    return pl.pallas_call(
        kernel,
        out_shape=[jax.ShapeDtypeStruct(shape, dtype) for shape, dtype in outs],
        in_specs=[SMEM] * smem + [place] * (len(operands) - smem),
        out_specs=out_place if isinstance(out_place, list) else [out_place] * len(outs),
        scratch_shapes=list(scratch),
        cost_estimate=cost,
        compiler_params=pltpu.CompilerParams(vmem_limit_bytes=limit * 1024 * 1024),
    )(*operands)


def exchange(blocks):
    return lax.all_to_all(blocks, "seq", split_axis=0, concat_axis=0, tiled=True)


def along_y(arrays):
    received = []
    for shift, array in enumerate(arrays, 1):
        pairs = [
            (near * RING + line, near * RING + (line + shift) % RING)
            for near in range(GROUP // RING)
            for line in range(RING)
        ]
        received.append(lax.ppermute(array, "tensor", pairs))
    return received


def across(array):
    return lax.ppermute(array, "tensor", [(i, (i + RING) % GROUP) for i in range(GROUP)])


def body(queries, key_feats, value_feats, filter_taps, skip_gain, out_weight, out_grad):
    first, first_t, turn, second = tables()
    forward_tables = (first, turn, second)
    inverse_tables = (first_t, turn, second)
    square_shape = (ROWS, SIDE)
    tokens = (CH, BLOCK)
    one, two = (BLOCKS, 16, SIDE), (BLOCKS, 32, SIDE)
    parts = [(square_shape, F32)] + [(square_shape, BF16)] * (RING - 1)

    first_inputs = (key_feats, value_feats, filter_taps, out_weight, skip_gain, *forward_tables)
    table, key_value, spec = call(
        source_kernel,
        [((2 * WEIGHTS + 8, SIDE), F32), (square_shape, BF16), (two, BF16)],
        [pltpu.with_memory_space_constraint(array, pltpu.HBM) for array in first_inputs],
        scratch=[
            *[pltpu.VMEM(tokens, BF16)] * 3,
            pltpu.VMEM(out_weight.shape, BF16),
            pltpu.SMEM((CH,), F32),
            *[pltpu.VMEM(array.shape, array.dtype) for array in forward_tables],
            pltpu.VMEM(square_shape, BF16),
            pltpu.VMEM((2, *one), BF16),
            pltpu.SemaphoreType.DMA((11,)),
        ],
        place=HBM,
        limit=32,
        out_place=[VMEM, ANY, ANY],
    )
    far = across(out_grad)
    spec = exchange(spec)
    mine, *others = call(
        grad_mix_kernel,
        parts,
        (table, out_grad, far),
        scratch=[pltpu.VMEM(square_shape, F32)] * 2,
        cost=COST,
    )
    others = along_y(others)
    grad_gated, grad_inner, grad_spec = call(
        grad_kernel,
        [(square_shape, F32), (square_shape, BF16), (one, BF16)],
        (mine, *others, queries, *forward_tables),
    )
    (rows,) = call(
        convolve_kernel,
        [(two, BF16)],
        (spec, grad_spec),
        scratch=[pltpu.VMEM((2, 2, BLOCKS, PIECE, SIDE), F32)],
    )
    rows = exchange(rows)
    gated, inner_sum = call(
        gate_kernel,
        [(square_shape, BF16), (square_shape, F32)],
        (table, rows, key_value, queries, *inverse_tables),
    )
    far = across(gated)
    rows, gated = lax.optimization_barrier((rows, gated))
    corr, grad_queries = call(
        correlate_kernel,
        [(two, BF16), (tokens, BF16)],
        (spec, rows, inner_sum, grad_gated),
        scratch=[
            pltpu.VMEM((3, 2, BLOCKS, PIECE, SIDE), F32),
            pltpu.VMEM((2, *one), BF16),
            pltpu.VMEM(tokens, BF16),
            pltpu.SemaphoreType.DMA((3,)),
        ],
        out_place=ANY,
    )
    corr = exchange(corr)
    mine, *others = call(out_mix_kernel, parts, (table, gated, far), cost=COST)
    others = along_y(others)

    def last(*refs):
        last_kernel(*refs, scale=(BLOCKS * BLOCK) ** -0.5)

    output, grad_keys, grad_values, grad_taps = call(
        last,
        [(tokens, BF16), (tokens, BF16), (tokens, BF16), (tokens, F32)],
        (table, corr, grad_inner, key_feats, value_feats, *inverse_tables, mine, *others),
        scratch=[
            *[pltpu.VMEM(tokens, BF16)] * 3,
            pltpu.VMEM(tokens, F32),
            pltpu.SemaphoreType.DMA((4,)),
        ],
        out_place=ANY,
    )
    return (output, grad_queries, grad_keys, grad_values, grad_taps)


def solution(mesh):
    assert dict(mesh.shape) == {"tensor": GROUP, "seq": BLOCKS}
    placed = P("tensor", "seq")
    return jax.shard_map(
        body,
        mesh=mesh,
        in_specs=(placed, placed, placed, placed, P("tensor"), P(), placed),
        out_specs=(placed,) * 5,
        check_vma=False,
    )
```

time: 76.9 us -> 67.6 us (0.88)
  starting transfers between devices: 34 us -> 28.6 us
  Pallas kernels: 12 us -> 7.57 us
  waiting for transfers between devices: 11.8 us -> 13.1 us
  blocking collectives: 17.9 us -> 17.1 us
    pallas_call x9 -> x8, Pallas kernels: 12 us -> 7.57 us  [call(): pl.pallas_call(kernel, out_shape=[jax.ShapeDtypeStruct(shape, dtype) for...]
    ppermute x2, starting transfers between devices: 12.5 us -> 9.07 us  [across(): lax.ppermute(array, 'tensor', [(i, (i + RING) % GROUP) for i in range(GRO...]
    all_to_all x2, starting transfers between devices: 12.8 us -> 10.8 us  [exchange(): lax.all_to_all(blocks, 'seq', split_axis=0, concat_axis=0, tiled=True)]
    all_to_all x1, blocking collectives: 17.9 us -> 17.1 us  [exchange(): lax.all_to_all(blocks, 'seq', split_axis=0, concat_axis=0, tiled=True)]
  transfers between devices with their start and end apart: 10 -> 10, of which waited for: 6 -> 7; matrix products, arithmetic and copies ran while one was open for 0% -> 0% of each run, Pallas kernels for 10% -> 8%
where the time goes in v3:
time: 67.6 us; the launch traced here: 67.2 us
  starting transfers between devices  28.6 us (42%)
  blocking collectives  17.1 us (25%)
  waiting for transfers between devices  13.1 us (19%)
  Pallas kernels  7.57 us (11%)
  between operations  0.79 us (1%)
    all_to_all x1, blocking collectives, exchange(): lax.all_to_all(blocks, 'seq', split_axis=0, concat_axis=0, tiled=True)  17.1 us
    all_to_all x2, starting transfers between devices, exchange(): lax.all_to_all(blocks, 'seq', split_axis=0, concat_axis=0, tiled=True)  10.8 us
    ppermute x2, starting transfers between devices, across(): lax.ppermute(array, 'tensor', [(i, (i + RING) % GROUP) for i in range(GRO...  9.07 us
    ppermute x6, starting transfers between devices, along_y(): received.append(lax.ppermute(array, 'tensor', pairs))  8.72 us
    pallas_call x8, Pallas kernels, call(): pl.pallas_call(kernel, out_shape=[jax.ShapeDtypeStruct(shape, dtype) for...  7.57 us
    ppermute x6, waiting for transfers between devices, along_y(): received.append(lax.ppermute(array, 'tensor', pairs))  5.92 us
    all_to_all x2, waiting for transfers between devices, exchange(): lax.all_to_all(blocks, 'seq', split_axis=0, concat_axis=0, tiled=True)  5.77 us
    ppermute x2, waiting for transfers between devices, across(): lax.ppermute(array, 'tensor', [(i, (i + RING) % GROUP) for i in range(GRO...  1.43 us
  transfers between devices with their start and end apart: 10, of which 7 were waited for; matrix products, arithmetic and copies ran while one was open for 0% of the time, Pallas kernels for 8%

profile of v3, /device:TPU:1, one launch (start us, length us, event | category | flops | bytes accessed | tf_op | source)
XLA Modules:
  0.0 67.2 jit_solution(856381796589454077)
XLA Ops:
  0.6 7.8 %collective-permute-start = (bf16[2,16384]{1,0:T(2,128)(2,1)}, bf16[2,16384]{1,0:T(2,128)(2,1)S(1)}, u32[]{:S(2)}, u32[]{:S(2)}) collective-permute-start(bf16[2,16384]{1,0:T(2,128)(2,1)} %near_ref.1), channel_id=1, source_target_pairs={{0,128},{32,160},{64,192},{96,224},{128,0},{160,32},{192,64},{224,... | collective-permute-start | bytes 196616 | tf_op jit(solution)/shard_map/ppermute | solution.py:401
  8.5 2.6 %shard_map.146 = (f32[72,128]{1,0:T(8,128)S(1)}, bf16[256,128]{1,0:T(8,128)(2,1)S(1)}, bf16[32,32,128]{2,1,0:T(8,128)(2,1)}) custom-call(bf16[2,16384]{1,0:T(2,128)(2,1)} %refs_3_.1, bf16[2,16384]{1,0:T(2,128)(2,1)} %refs_4_.1, bf16[2,16384]{1,0:T(2,128)(2,1)} %taps_hbm.1, bf16[16,16]{1,0:T(8,128)(2,1)} %weight_hbm.1, f32[2]{0:T(128)} %skip_hbm.1, ...), custom_call_target="tpu_custom_call" | custom-call | tf_op jit(solution)/shard_map/pallas_call | solution.py:373
  11.1 6.9 %all-to-all-start = ((bf16[32,32,128]{2,1,0:T(8,128)(2,1)}), bf16[32,32,128]{2,1,0:T(8,128)(2,1)S(1)}, u32[]{:S(2)}, u32[]{:S(2)}) async-start(bf16[32,32,128]{2,1,0:T(8,128)(2,1)} %get-tuple-element.30), calls=%async_computation | async-start | bytes 524288 | tf_op jit(solution)/shard_map/all_to_all | solution.py:385
  18.0 0.0 copy-start
  18.0 0.0 copy-start.1
  18.1 0.0 copy-start.4
  18.1 0.2 shard_map.147
  18.2 1.4 %collective-permute-start.1 = (bf16[256,128]{1,0:T(8,128)(2,1)S(1)}, bf16[256,128]{1,0:T(8,128)(2,1)S(1)}, u32[]{:S(2)}, u32[]{:S(2)}) collective-permute-start(bf16[256,128]{1,0:T(8,128)(2,1)S(1)} %get-tuple-element.32), channel_id=1, source_target_pairs={{0,32},{32,64},{64,96},{96,0},{128,160},{160,192},{192,224},{224,1... | collective-permute-start | bytes 196616 | tf_op jit(solution)/shard_map/ppermute | solution.py:396
  19.6 2.6 %collective-permute-start.2 = (bf16[256,128]{1,0:T(8,128)(2,1)S(1)}, bf16[256,128]{1,0:T(8,128)(2,1)S(1)}, u32[]{:S(2)}, u32[]{:S(2)}) collective-permute-start(bf16[256,128]{1,0:T(8,128)(2,1)S(1)} %get-tuple-element.33), channel_id=1, source_target_pairs={{0,64},{32,96},{64,0},{96,32},{128,192},{160,224},{192,128},{224,1... | collective-permute-start | bytes 196616 | tf_op jit(solution)/shard_map/ppermute | solution.py:396
  22.2 1.1 %collective-permute-start.3 = (bf16[256,128]{1,0:T(8,128)(2,1)S(1)}, bf16[256,128]{1,0:T(8,128)(2,1)S(1)}, u32[]{:S(2)}, u32[]{:S(2)}) collective-permute-start(bf16[256,128]{1,0:T(8,128)(2,1)S(1)} %get-tuple-element.34), channel_id=1, source_target_pairs={{0,96},{32,0},{64,32},{96,64},{128,224},{160,128},{192,160},{224,1... | collective-permute-start | bytes 196616 | tf_op jit(solution)/shard_map/ppermute | solution.py:396
  23.3 2.3 %collective-permute-done.2.r2_ref = bf16[256,128]{1,0:T(8,128)(2,1)S(1)} collective-permute-done((bf16[256,128]{1,0:T(8,128)(2,1)S(1)}, bf16[256,128]{1,0:T(8,128)(2,1)S(1)}, u32[]{:S(2)}, u32[]{:S(2)}) %collective-permute-start.2) | collective-permute-done | bytes 65568 | tf_op jit(solution)/shard_map/ppermute | solution.py:396
  25.6 0.0 collective-permute-done.3.r3_ref
  25.7 0.4 shard_map.148
  26.1 3.2 %all-to-all-done.spec_ref = bf16[32,32,128]{2,1,0:T(8,128)(2,1)S(1)} async-done(((bf16[32,32,128]{2,1,0:T(8,128)(2,1)}), bf16[32,32,128]{2,1,0:T(8,128)(2,1)S(1)}, u32[]{:S(2)}, u32[]{:S(2)}) %all-to-all-start) | async-done | bytes 262176 | tf_op jit(solution)/shard_map/all_to_all | solution.py:385
  29.3 0.5 shard_map.149
  29.8 0.0 copy-start.6
  29.8 17.1 %all_to_all.15.rows_ref = bf16[32,32,128]{2,1,0:T(8,128)(2,1)S(1)} all-to-all(bf16[32,32,128]{2,1,0:T(8,128)(2,1)S(1)} %shard_map.149), channel_id=1, replica_groups=mesh['tensor'=8,'seq'=32] {'seq'}, dimensions={0} | all-to-all | bytes 524288 | tf_op jit(solution)/shard_map/all_to_all | solution.py:385
  46.9 0.4 shard_map.150
  47.3 1.2 %collective-permute-start.4 = (bf16[256,128]{1,0:T(8,128)(2,1)S(1)}, bf16[256,128]{1,0:T(8,128)(2,1)S(1)}, u32[]{:S(2)}, u32[]{:S(2)}) collective-permute-start(bf16[256,128]{1,0:T(8,128)(2,1)S(1)} %get-tuple-element.43.near_ref), channel_id=1, source_target_pairs={{0,128},{32,160},{64,192},{96,224},{128,0},{160,32},{192,64},{224,... | collective-permute-start | bytes 196616 | tf_op jit(solution)/shard_map/ppermute | solution.py:401
  48.6 1.8 %shard_map.151 = (bf16[32,32,128]{2,1,0:T(8,128)(2,1)}, bf16[2,16384]{1,0:T(2,128)(2,1)}) custom-call(bf16[32,32,128]{2,1,0:T(8,128)(2,1)S(1)} %all-to-all-done.spec_ref, bf16[32,32,128]{2,1,0:T(8,128)(2,1)S(1)} %all_to_all.15.rows_ref, f32[256,128]{1,0:T(8,128)S(1)} %get-tuple-element.39.inner_sum_ref, f32[256,128]{1,0:T(8,128)S(1)} %get-tuple-element.40.gated_ref), custom_call_target="tpu_custom_call" | custom-call | tf_op jit(solution)/shard_map/pallas_call | solution.py:373
  50.4 3.9 %all-to-all-start.2 = ((bf16[32,32,128]{2,1,0:T(8,128)(2,1)}), bf16[32,32,128]{2,1,0:T(8,128)(2,1)S(1)}, u32[]{:S(2)}, u32[]{:S(2)}) async-start(bf16[32,32,128]{2,1,0:T(8,128)(2,1)} %get-tuple-element.41), calls=%async_computation.2 | async-start | bytes 524288 | tf_op jit(solution)/shard_map/all_to_all | solution.py:385
  54.3 0.0 copy-start.2
  54.3 1.4 %collective-permute-done.4.far_ref = bf16[256,128]{1,0:T(8,128)(2,1)S(1)} collective-permute-done((bf16[256,128]{1,0:T(8,128)(2,1)S(1)}, bf16[256,128]{1,0:T(8,128)(2,1)S(1)}, u32[]{:S(2)}, u32[]{:S(2)}) %collective-permute-start.4) | collective-permute-done | bytes 65568 | tf_op jit(solution)/shard_map/ppermute | solution.py:401
  55.7 0.1 shard_map.152
  55.9 0.3 collective-permute-start.5
  56.2 3.2 %collective-permute-start.6 = (bf16[256,128]{1,0:T(8,128)(2,1)S(1)}, bf16[256,128]{1,0:T(8,128)(2,1)S(1)}, u32[]{:S(2)}, u32[]{:S(2)}) collective-permute-start(bf16[256,128]{1,0:T(8,128)(2,1)S(1)} %get-tuple-element.46), channel_id=1, source_target_pairs={{0,64},{32,96},{64,0},{96,32},{128,192},{160,224},{192,128},{224,1... | collective-permute-start | bytes 196616 | tf_op jit(solution)/shard_map/ppermute | solution.py:396
  59.4 0.1 collective-permute-start.7
  59.5 1.0 %collective-permute-done.5.refs_9_ = bf16[256,128]{1,0:T(8,128)(2,1)S(1)} collective-permute-done((bf16[256,128]{1,0:T(8,128)(2,1)S(1)}, bf16[256,128]{1,0:T(8,128)(2,1)S(1)}, u32[]{:S(2)}, u32[]{:S(2)}) %collective-permute-start.5) | collective-permute-done | bytes 65568 | tf_op jit(solution)/shard_map/ppermute | solution.py:396
  60.6 1.7 %collective-permute-done.6.refs_10_ = bf16[256,128]{1,0:T(8,128)(2,1)S(1)} collective-permute-done((bf16[256,128]{1,0:T(8,128)(2,1)S(1)}, bf16[256,128]{1,0:T(8,128)(2,1)S(1)}, u32[]{:S(2)}, u32[]{:S(2)}) %collective-permute-start.6) | collective-permute-done | bytes 65568 | tf_op jit(solution)/shard_map/ppermute | solution.py:396
  62.3 0.8 %collective-permute-done.7.refs_11_ = bf16[256,128]{1,0:T(8,128)(2,1)S(1)} collective-permute-done((bf16[256,128]{1,0:T(8,128)(2,1)S(1)}, bf16[256,128]{1,0:T(8,128)(2,1)S(1)}, u32[]{:S(2)}, u32[]{:S(2)}) %collective-permute-start.7) | collective-permute-done | bytes 65568 | tf_op jit(solution)/shard_map/ppermute | solution.py:396
  63.1 2.6 %all-to-all-done.2.refs_1_ = bf16[32,32,128]{2,1,0:T(8,128)(2,1)S(1)} async-done(((bf16[32,32,128]{2,1,0:T(8,128)(2,1)}), bf16[32,32,128]{2,1,0:T(8,128)(2,1)S(1)}, u32[]{:S(2)}, u32[]{:S(2)}) %all-to-all-start.2) | async-done | bytes 262176 | tf_op jit(solution)/shard_map/all_to_all | solution.py:385
  65.7 1.6 %shard_map.153 = (bf16[2,16384]{1,0:T(2,128)(2,1)}, bf16[2,16384]{1,0:T(2,128)(2,1)}, bf16[2,16384]{1,0:T(2,128)(2,1)}, f32[2,16384]{1,0:T(2,128)}) custom-call(f32[72,128]{1,0:T(8,128)S(1)} %get-tuple-element.29.table_ref.skip_ref.refs_0_, bf16[32,32,128]{2,1,0:T(8,128)(2,1)S(1)} %all-to-all-done.2.refs_1_, bf16[256,128]{1,0:T(8,128)(2,1)S(1)} %get-tuple-element.42.refs_2_, ...), custom_call_target="tpu_custom_call" | custom-call | tf_op jit(solution)/shard_map/pallas_call | solution.py:373
  (13 shorter events, 0.0 us)
Async XLA Ops:
  0.6 17.4 %collective-permute-start = (bf16[2,16384]{1,0:T(2,128)(2,1)}, bf16[2,16384]{1,0:T(2,128)(2,1)S(1)}, u32[]{:S(2)}, u32[]{:S(2)}) collective-permute-start(bf16[2,16384]{1,0:T(2,128)(2,1)} %near_ref.1), channel_id=1, source_target_pairs={{0,128},{32,160},{64,192},{96,224},{128,0},{160,32},{192,64},{224,... | collective-permute-start | bytes 196616 | tf_op jit(solution)/shard_map/ppermute | solution.py:401
  11.1 6.9 %copy-start.7 = (bf16[2,16384]{1,0:T(2,128)(2,1)S(1)}, bf16[2,16384]{1,0:T(2,128)(2,1)}, u32[]{:S(2)}) copy-start(bf16[2,16384]{1,0:T(2,128)(2,1)} %near_ref.1) | copy-start | bytes 196612
  11.1 18.2 %all-to-all-start = ((bf16[32,32,128]{2,1,0:T(8,128)(2,1)}), bf16[32,32,128]{2,1,0:T(8,128)(2,1)S(1)}, u32[]{:S(2)}, u32[]{:S(2)}) async-start(bf16[32,32,128]{2,1,0:T(8,128)(2,1)} %get-tuple-element.30), calls=%async_computation | async-start | bytes 524288 | tf_op jit(solution)/shard_map/all_to_all | solution.py:385
  18.0 7.6 %copy-start = (f32[2,128,128]{2,1,0:T(8,128)S(1)}, f32[2,128,128]{2,1,0:T(8,128)}, u32[]{:S(2)}) copy-start(f32[2,128,128]{2,1,0:T(8,128)} %constant.10.clone.turn_hbm.turn_ref.refs_6_) | copy-start | bytes 393220
  18.0 7.6 %copy-start.1 = (bf16[2,128,128]{2,1,0:T(8,128)(2,1)S(1)}, bf16[2,128,128]{2,1,0:T(8,128)(2,1)}, u32[]{:S(2)}) copy-start(bf16[2,128,128]{2,1,0:T(8,128)(2,1)} %constant.11.clone.second_hbm.second_ref.refs_7_) | copy-start | bytes 196612
  18.1 7.6 %copy-start.4 = (bf16[256,128]{1,0:T(8,128)(2,1)S(1)}, bf16[256,128]{1,0:T(8,128)(2,1)}, u32[]{:S(2)}) copy-start(bf16[256,128]{1,0:T(8,128)(2,1)} %constant.8.clone.first_hbm.first_ref) | copy-start | bytes 196612
  18.1 7.6 %copy-start.5 = (bf16[2,16384]{1,0:T(2,128)(2,1)S(1)}, bf16[2,16384]{1,0:T(2,128)(2,1)}, u32[]{:S(2)}) copy-start(bf16[2,16384]{1,0:T(2,128)(2,1)} %query_ref.3) | copy-start | bytes 196612
  18.2 5.1 %collective-permute-start.1 = (bf16[256,128]{1,0:T(8,128)(2,1)S(1)}, bf16[256,128]{1,0:T(8,128)(2,1)S(1)}, u32[]{:S(2)}, u32[]{:S(2)}) collective-permute-start(bf16[256,128]{1,0:T(8,128)(2,1)S(1)} %get-tuple-element.32), channel_id=1, source_target_pairs={{0,32},{32,64},{64,96},{96,0},{128,160},{160,192},{192,224},{224,1... | collective-permute-start | bytes 196616 | tf_op jit(solution)/shard_map/ppermute | solution.py:396
  19.6 6.0 %collective-permute-start.2 = (bf16[256,128]{1,0:T(8,128)(2,1)S(1)}, bf16[256,128]{1,0:T(8,128)(2,1)S(1)}, u32[]{:S(2)}, u32[]{:S(2)}) collective-permute-start(bf16[256,128]{1,0:T(8,128)(2,1)S(1)} %get-tuple-element.33), channel_id=1, source_target_pairs={{0,64},{32,96},{64,0},{96,32},{128,192},{160,224},{192,128},{224,1... | collective-permute-start | bytes 196616 | tf_op jit(solution)/shard_map/ppermute | solution.py:396
  22.2 3.4 %collective-permute-start.3 = (bf16[256,128]{1,0:T(8,128)(2,1)S(1)}, bf16[256,128]{1,0:T(8,128)(2,1)S(1)}, u32[]{:S(2)}, u32[]{:S(2)}) collective-permute-start(bf16[256,128]{1,0:T(8,128)(2,1)S(1)} %get-tuple-element.34), channel_id=1, source_target_pairs={{0,96},{32,0},{64,32},{96,64},{128,224},{160,128},{192,160},{224,1... | collective-permute-start | bytes 196616 | tf_op jit(solution)/shard_map/ppermute | solution.py:396
  29.8 17.1 %copy-start.6 = (bf16[128,256]{1,0:T(8,128)(2,1)S(1)}, bf16[128,256]{1,0:T(8,128)(2,1)}, u32[]{:S(2)}) copy-start(bf16[128,256]{1,0:T(8,128)(2,1)} %constant.9.clone.first_ref.refs_5_) | copy-start | bytes 196612
  47.3 8.4 %collective-permute-start.4 = (bf16[256,128]{1,0:T(8,128)(2,1)S(1)}, bf16[256,128]{1,0:T(8,128)(2,1)S(1)}, u32[]{:S(2)}, u32[]{:S(2)}) collective-permute-start(bf16[256,128]{1,0:T(8,128)(2,1)S(1)} %get-tuple-element.43.near_ref), channel_id=1, source_target_pairs={{0,128},{32,160},{64,192},{96,224},{128,0},{160,32},{192,64},{224,... | collective-permute-start | bytes 196616 | tf_op jit(solution)/shard_map/ppermute | solution.py:401
  50.4 15.3 %all-to-all-start.2 = ((bf16[32,32,128]{2,1,0:T(8,128)(2,1)}), bf16[32,32,128]{2,1,0:T(8,128)(2,1)S(1)}, u32[]{:S(2)}, u32[]{:S(2)}) async-start(bf16[32,32,128]{2,1,0:T(8,128)(2,1)} %get-tuple-element.41), calls=%async_computation.2 | async-start | bytes 524288 | tf_op jit(solution)/shard_map/all_to_all | solution.py:385
  54.3 11.4 %copy-start.2 = (bf16[2,16384]{1,0:T(2,128)(2,1)S(1)}, bf16[2,16384]{1,0:T(2,128)(2,1)}, u32[]{:S(2)}) copy-start(bf16[2,16384]{1,0:T(2,128)(2,1)} %refs_3_.1) | copy-start | bytes 196612
  54.3 11.4 %copy-start.3 = (bf16[2,16384]{1,0:T(2,128)(2,1)S(1)}, bf16[2,16384]{1,0:T(2,128)(2,1)}, u32[]{:S(2)}) copy-start(bf16[2,16384]{1,0:T(2,128)(2,1)} %refs_4_.1) | copy-start | bytes 196612
  55.9 4.7 %collective-permute-start.5 = (bf16[256,128]{1,0:T(8,128)(2,1)S(1)}, bf16[256,128]{1,0:T(8,128)(2,1)S(1)}, u32[]{:S(2)}, u32[]{:S(2)}) collective-permute-start(bf16[256,128]{1,0:T(8,128)(2,1)S(1)} %get-tuple-element.45), channel_id=1, source_target_pairs={{0,32},{32,64},{64,96},{96,0},{128,160},{160,192},{192,224},{224,1... | collective-permute-start | bytes 196616 | tf_op jit(solution)/shard_map/ppermute | solution.py:396
  56.2 6.1 %collective-permute-start.6 = (bf16[256,128]{1,0:T(8,128)(2,1)S(1)}, bf16[256,128]{1,0:T(8,128)(2,1)S(1)}, u32[]{:S(2)}, u32[]{:S(2)}) collective-permute-start(bf16[256,128]{1,0:T(8,128)(2,1)S(1)} %get-tuple-element.46), channel_id=1, source_target_pairs={{0,64},{32,96},{64,0},{96,32},{128,192},{160,224},{192,128},{224,1... | collective-permute-start | bytes 196616 | tf_op jit(solution)/shard_map/ppermute | solution.py:396
  59.4 3.7 %collective-permute-start.7 = (bf16[256,128]{1,0:T(8,128)(2,1)S(1)}, bf16[256,128]{1,0:T(8,128)(2,1)S(1)}, u32[]{:S(2)}, u32[]{:S(2)}) collective-permute-start(bf16[256,128]{1,0:T(8,128)(2,1)S(1)} %get-tuple-element.47), channel_id=1, source_target_pairs={{0,96},{32,0},{64,32},{96,64},{128,224},{160,128},{192,160},{224,1... | collective-permute-start | bytes 196616 | tf_op jit(solution)/shard_map/ppermute | solution.py:396

commit v4 on v3

--- a/solution.py
+++ b/solution.py
@@ -1,4 +1,4 @@
-import math
+import functools
 
 import jax
 import jax.numpy as jnp
@@ -24,7 +24,6 @@
 PIECE = ROWS // BLOCKS
 VMEM = pl.BlockSpec(memory_space=pltpu.VMEM)
 COST = pl.CostEstimate(flops=10000000000, bytes_accessed=1000000, transcendentals=0)
-SMEM = pl.BlockSpec(memory_space=pltpu.SMEM)
 HBM = pl.BlockSpec(memory_space=pltpu.HBM)
 ANY = pl.BlockSpec(memory_space=pl.ANY)
 
@@ -58,13 +57,15 @@
     )
 
 
-def forward(signal, first, turn, second):
-    both = jnp.concatenate([signal[:SIDE], signal[SIDE:]], axis=1)
-    stage = jnp.dot(first, both, preferred_element_type=F32)
+def forward(signals, first, turn, second):
+    both = [jnp.concatenate([signal[:SIDE], signal[SIDE:]], axis=1) for signal in signals]
+    stages = jnp.dot(first, jnp.concatenate(both, axis=1), preferred_element_type=F32)
     cos, sin = turn[0], turn[1]
     turned = []
-    for c in range(CH):
-        real, imag = (stage[p * SIDE : (p + 1) * SIDE, c * SIDE : (c + 1) * SIDE] for p in (0, 1))
+    for c in range(CH * len(signals)):
+        real, imag = (
+            stages[p * SIDE : (p + 1) * SIDE, c * SIDE : (c + 1) * SIDE] for p in (0, 1)
+        )
         turned.append(
             jnp.concatenate(
                 [(real * cos + imag * sin).astype(BF16), (imag * cos - real * sin).astype(BF16)],
@@ -74,20 +75,30 @@
     spec = jnp.dot(
         jnp.concatenate(turned, axis=0), second_stage(second, -1), preferred_element_type=F32
     )
-    parts = [spec[:, p * SIDE : (p + 1) * SIDE].reshape(BLOCKS, PIECE, SIDE) for p in (0, 1)]
-    return jnp.concatenate(parts, axis=1).astype(BF16)
-
-
-def inverse(rows, first_t, turn, second):
-    rows = rows.astype(F32)
-    real = rows[:, :PIECE].reshape(ROWS, SIDE)
-    imag = rows[:, PIECE:].reshape(ROWS, SIDE)
-    spec = jnp.concatenate([real.astype(BF16), imag.astype(BF16)], axis=1)
-    stage = jnp.dot(spec, second_stage(second, 1), preferred_element_type=F32)
+    results = []
+    for i in range(len(signals)):
+        rows = spec[i * ROWS : (i + 1) * ROWS]
+        parts = [rows[:, p * SIDE : (p + 1) * SIDE].reshape(BLOCKS, PIECE, SIDE) for p in (0, 1)]
+        results.append(jnp.concatenate(parts, axis=1).astype(BF16))
+    return results
+
+
+def inverse(pieces, first_t, turn, second):
+    specs = []
+    for rows in pieces:
+        rows = rows.astype(F32)
+        real = rows[:, :PIECE].reshape(ROWS, SIDE)
+        imag = rows[:, PIECE:].reshape(ROWS, SIDE)
+        specs.append(jnp.concatenate([real.astype(BF16), imag.astype(BF16)], axis=1))
+    stages = jnp.dot(
+        jnp.concatenate(specs, axis=0), second_stage(second, 1), preferred_element_type=F32
+    )
     cos, sin = turn[0], turn[1]
     turned = []
-    for c in range(CH):
-        real, imag = (stage[c * SIDE : (c + 1) * SIDE, p * SIDE : (p + 1) * SIDE] for p in (0, 1))
+    for c in range(CH * len(pieces)):
+        real, imag = (
+            stages[c * SIDE : (c + 1) * SIDE, p * SIDE : (p + 1) * SIDE] for p in (0, 1)
+        )
         turned.append(
             jnp.concatenate(
                 [(real * cos - imag * sin).astype(BF16), (imag * cos + real * sin).astype(BF16)],
@@ -96,14 +107,17 @@
         )
     both = jnp.dot(first_t, jnp.concatenate(turned, axis=1), preferred_element_type=F32)
     both = both * (2.0 / LENGTH)
-    return jnp.concatenate([both[:, :SIDE], both[:, SIDE:]], axis=0)
+    columns = [both[:, c * SIDE : (c + 1) * SIDE] for c in range(CH * len(pieces))]
+    return [
+        jnp.concatenate(columns[CH * i : CH * i + CH], axis=0) for i in range(len(pieces))
+    ]
 
 
 def source_kernel(
     key_hbm, value_hbm, taps_hbm, weight_hbm, skip_hbm, first_hbm, turn_hbm, second_hbm,
-    table_ref, kv_hbm, spec_hbm,
+    table_ref, kv_ref, spec_hbm,
     key_ref, value_ref, taps_ref, weight_ref, skip_ref, first_ref, turn_ref, second_ref,
-    kv_ref, spec_ref, sems,
+    spec_ref, sems,
 ):
     copies = []
 
@@ -112,28 +126,27 @@
         copy.start()
         copies.append(copy)
 
-    def part(sig):
-        return spec_hbm.at[:, pl.ds(16 * sig, 16), :]
-
+    send(key_hbm, key_ref)
+    send(value_hbm, value_ref)
     send(taps_hbm, taps_ref)
     send(first_hbm, first_ref)
     send(turn_hbm, turn_ref)
     send(second_hbm, second_ref)
-    send(key_hbm, key_ref)
-    send(value_hbm, value_ref)
     send(weight_hbm, weight_ref)
     send(skip_hbm, skip_ref)
     for copy in copies:
         copy.wait()
     arrived = len(copies)
-    tables_in = (first_ref[...], turn_ref[...], second_ref[...])
-    spec_ref[1] = forward(square(taps_ref).astype(BF16), *tables_in)
-    send(spec_ref.at[1], part(1))
     key_value = (square(key_ref) * square(value_ref)).astype(BF16)
     kv_ref[...] = key_value
-    send(kv_ref, kv_hbm)
-    spec_ref[0] = forward(key_value, *tables_in)
-    send(spec_ref.at[0], part(0))
+    spec_ref[0], spec_ref[1] = forward(
+        [key_value, square(taps_ref).astype(BF16)],
+        first_ref[...],
+        turn_ref[...],
+        second_ref[...],
+    )
+    for sig in range(2):
+        send(spec_ref.at[sig], spec_hbm.at[:, pl.ds(16 * sig, 16), :])
     table_ref[:WEIGHTS, :] = weight_rows(weight_ref[...], True)
     table_ref[WEIGHTS : 2 * WEIGHTS, :] = weight_rows(weight_ref[...], False)
     row = lax.broadcasted_iota(jnp.int32, (8, SIDE), 0)
@@ -292,37 +305,42 @@
     gated_ref[...] = grad_gated
     grad_inner = (grad_gated * square(query_ref)).astype(BF16)
     inner_ref[...] = grad_inner
-    out_ref[...] = forward(grad_inner, first_ref[...], turn_ref[...], second_ref[...])
-
-
-def correlate_kernel(
-    spec_ref, rows_ref, inner_sum_ref, gated_ref, out_hbm, grad_query_hbm,
-    buf_ref, out_ref, grad_query_ref, sems,
-):
-    grad_query_ref[...] = (gated_ref[...] * inner_sum_ref[...]).reshape(CH, BLOCK).astype(BF16)
-    query_copy = pltpu.make_async_copy(grad_query_ref, grad_query_hbm, sems.at[0])
-    query_copy.start()
-    load(spec_ref, 0, buf_ref, 0)
-    load(spec_ref, 1, buf_ref, 1)
-    load(rows_ref, 1, buf_ref, 2)
-    sign = alternate()
-    copies = []
-    for sig, other in ((0, 1), (1, 0)):
-        correlate(buf_ref, out_ref.at[sig], sign, other, 0)
-        copy = pltpu.make_async_copy(
-            out_ref.at[sig], out_hbm.at[:, pl.ds(16 * sig, 16), :], sems.at[1 + sig]
+    (out_ref[...],) = forward([grad_inner], first_ref[...], turn_ref[...], second_ref[...])
+
+
+def correlate_kernel(half, spec_ref, rows_ref, inner_sum_ref, gated_ref, *refs):
+    out_hbm, grad_query_hbm, buf_ref, out_ref, grad_query_ref, sems = refs[2 * half :]
+
+    @pl.when(lax.axis_index("tensor") // RING == half)
+    def _():
+        grad_query_ref[...] = (
+            (gated_ref[...] * inner_sum_ref[...]).reshape(CH, BLOCK).astype(BF16)
         )
-        copy.start()
-        copies.append(copy)
-    for copy in copies:
-        copy.wait()
-    query_copy.wait()
+        query_copy = pltpu.make_async_copy(grad_query_ref, grad_query_hbm, sems.at[0])
+        query_copy.start()
+        load(spec_ref, 0, buf_ref, 0)
+        load(spec_ref, 1, buf_ref, 1)
+        load(rows_ref, 1, buf_ref, 2)
+        sign = alternate()
+        copies = []
+        for sig, other in ((0, 1), (1, 0)):
+            correlate(buf_ref, out_ref.at[sig], sign, other, 0)
+            copy = pltpu.make_async_copy(
+                out_ref.at[sig], out_hbm.at[:, pl.ds(16 * sig, 16), :], sems.at[1 + sig]
+            )
+            copy.start()
+            copies.append(copy)
+        for copy in copies:
+            copy.wait()
+        query_copy.wait()
 
 
 def gate_kernel(
     skip_ref, rows_ref, kv_ref, query_ref, first_ref, turn_ref, second_ref, out_ref, inner_sum_ref
 ):
-    convolved = inverse(rows_ref[:, :16, :], first_ref[...], turn_ref[...], second_ref[...])
+    (convolved,) = inverse(
+        [rows_ref[:, :16, :]], first_ref[...], turn_ref[...], second_ref[...]
+    )
     inner_sum = convolved + skip_rows(skip_ref) * kv_ref[...].astype(F32)
     inner_sum_ref[...] = inner_sum
     out_ref[...] = (square(query_ref) * inner_sum).astype(BF16)
@@ -355,10 +373,9 @@
     out_ref[...] = both.reshape(CH, BLOCK).astype(BF16)
     send(out_ref, out_hbm)
     tables_in = (first_ref[...], turn_ref[...], second_ref[...])
-    taps = inverse(rows_ref[:, 16:, :], *tables_in) * scale
-    grad_taps_ref[...] = taps.reshape(CH, BLOCK)
+    taps, source = inverse([rows_ref[:, 16:, :], rows_ref[:, :16, :]], *tables_in)
+    grad_taps_ref[...] = (taps * scale).reshape(CH, BLOCK)
     send(grad_taps_ref, grad_taps_hbm)
-    source = inverse(rows_ref[:, :16, :], *tables_in)
     source = source + skip_rows(table_ref) * inner_ref[...].astype(F32)
     source = source.reshape(CH, BLOCK)
     grad_key_ref[...] = (source * value_ref[...].astype(F32)).astype(BF16)
@@ -369,13 +386,14 @@
         copy.wait()
 
 
-def call(kernel, outs, operands, smem=0, scratch=(), place=VMEM, limit=48, cost=None, out_place=VMEM):
+def call(kernel, outs, operands, scratch=(), place=VMEM, limit=48, cost=None, out_place=VMEM, aliases=None):
     return pl.pallas_call(
         kernel,
         out_shape=[jax.ShapeDtypeStruct(shape, dtype) for shape, dtype in outs],
-        in_specs=[SMEM] * smem + [place] * (len(operands) - smem),
+        in_specs=place if isinstance(place, list) else [place] * len(operands),
         out_specs=out_place if isinstance(out_place, list) else [out_place] * len(outs),
         scratch_shapes=list(scratch),
+        input_output_aliases=aliases or {},
         cost_estimate=cost,
         compiler_params=pltpu.CompilerParams(vmem_limit_bytes=limit * 1024 * 1024),
     )(*operands)
@@ -411,24 +429,28 @@
     parts = [(square_shape, F32)] + [(square_shape, BF16)] * (RING - 1)
 
     first_inputs = (key_feats, value_feats, filter_taps, out_weight, skip_gain, *forward_tables)
+    first_inputs = [
+        pltpu.with_memory_space_constraint(array, pltpu.HBM) for array in first_inputs
+    ]
+
     table, key_value, spec = call(
         source_kernel,
         [((2 * WEIGHTS + 8, SIDE), F32), (square_shape, BF16), (two, BF16)],
-        [pltpu.with_memory_space_constraint(array, pltpu.HBM) for array in first_inputs],
+        first_inputs,
         scratch=[
             *[pltpu.VMEM(tokens, BF16)] * 3,
             pltpu.VMEM(out_weight.shape, BF16),
             pltpu.SMEM((CH,), F32),
             *[pltpu.VMEM(array.shape, array.dtype) for array in forward_tables],
-            pltpu.VMEM(square_shape, BF16),
             pltpu.VMEM((2, *one), BF16),
-            pltpu.SemaphoreType.DMA((11,)),
+            pltpu.SemaphoreType.DMA((len(first_inputs) + 2,)),
         ],
         place=HBM,
         limit=32,
-        out_place=[VMEM, ANY, ANY],
-    )
-    far = across(out_grad)
+        out_place=[VMEM, VMEM, ANY],
+    )
+    spec, far = lax.optimization_barrier((spec, out_grad))
+    far = across(far)
     spec = exchange(spec)
     mine, *others = call(
         grad_mix_kernel,
@@ -455,20 +477,26 @@
         [(square_shape, BF16), (square_shape, F32)],
         (table, rows, key_value, queries, *inverse_tables),
     )
+
+    def correlations(half, *given):
+        return call(
+            functools.partial(correlate_kernel, half),
+            [(two, BF16), (tokens, BF16)],
+            (spec, rows, inner_sum, grad_gated, *given),
+            scratch=[
+                pltpu.VMEM((3, 2, BLOCKS, PIECE, SIDE), F32),
+                pltpu.VMEM((2, *one), BF16),
+                pltpu.VMEM(tokens, BF16),
+                pltpu.SemaphoreType.DMA((3,)),
+            ],
+            place=[VMEM] * 4 + [ANY] * len(given),
+            out_place=ANY,
+            aliases={4 + i: i for i in range(len(given))},
+        )
+
+    *begun, gated = lax.optimization_barrier((*correlations(0), gated))
     far = across(gated)
-    rows, gated = lax.optimization_barrier((rows, gated))
-    corr, grad_queries = call(
-        correlate_kernel,
-        [(two, BF16), (tokens, BF16)],
-        (spec, rows, inner_sum, grad_gated),
-        scratch=[
-            pltpu.VMEM((3, 2, BLOCKS, PIECE, SIDE), F32),
-            pltpu.VMEM((2, *one), BF16),
-            pltpu.VMEM(tokens, BF16),
-            pltpu.SemaphoreType.DMA((3,)),
-        ],
-        out_place=ANY,
-    )
+    corr, grad_queries = correlations(1, *begun)
     corr = exchange(corr)
     mine, *others = call(out_mix_kernel, parts, (table, gated, far), cost=COST)
     others = along_y(others)

time: 67.6 us -> 65.8 us (0.973)
  starting transfers between devices: 28.6 us -> 27.1 us
    all_to_all x2, waiting for transfers between devices: 5.77 us -> 3.23 us  [exchange(): lax.all_to_all(blocks, 'seq', split_axis=0, concat_axis=0, tiled=True)]
    ppermute x2, waiting for transfers between devices: 1.43 us -> 3.8 us  [across(): lax.ppermute(array, 'tensor', [(i, (i + RING) % GROUP) for i in range(GRO...]
    ppermute x2, starting transfers between devices: 9.07 us -> 7.92 us  [across(): lax.ppermute(array, 'tensor', [(i, (i + RING) % GROUP) for i in range(GRO...]
    pallas_call x8 -> x9, Pallas kernels: 7.57 us -> 7.17 us  [call(): pl.pallas_call(kernel, out_shape=[jax.ShapeDtypeStruct(shape, dtype) for...]
  transfers between devices with their start and end apart: 10 -> 10, of which waited for: 7 -> 6; matrix products, arithmetic and copies ran while one was open for 0% -> 0% of each run, Pallas kernels for 8% -> 1%
where the time goes in v4:
time: 65.8 us; the launch traced here: 65.5 us
  starting transfers between devices  27.1 us (41%)
  blocking collectives  17.1 us (26%)
  waiting for transfers between devices  13.3 us (20%)
  Pallas kernels  7.17 us (11%)
  between operations  0.81 us (1%)
    all_to_all x1, blocking collectives, exchange(): lax.all_to_all(blocks, 'seq', split_axis=0, concat_axis=0, tiled=True)  17.1 us
    all_to_all x2, starting transfers between devices, exchange(): lax.all_to_all(blocks, 'seq', split_axis=0, concat_axis=0, tiled=True)  10.4 us
    ppermute x6, starting transfers between devices, along_y(): received.append(lax.ppermute(array, 'tensor', pairs))  8.72 us
    ppermute x2, starting transfers between devices, across(): lax.ppermute(array, 'tensor', [(i, (i + RING) % GROUP) for i in range(GRO...  7.92 us
    pallas_call x9, Pallas kernels, call(): pl.pallas_call(kernel, out_shape=[jax.ShapeDtypeStruct(shape, dtype) for...  7.17 us
    ppermute x6, waiting for transfers between devices, along_y(): received.append(lax.ppermute(array, 'tensor', pairs))  6.24 us
    ppermute x2, waiting for transfers between devices, across(): lax.ppermute(array, 'tensor', [(i, (i + RING) % GROUP) for i in range(GRO...  3.8 us
    all_to_all x2, waiting for transfers between devices, exchange(): lax.all_to_all(blocks, 'seq', split_axis=0, concat_axis=0, tiled=True)  3.23 us
  transfers between devices with their start and end apart: 10, of which 6 were waited for; matrix products, arithmetic and copies ran while one was open for 0% of the time, Pallas kernels for 1%

profile of v4, /device:TPU:1, one launch (start us, length us, event | category | flops | bytes accessed | tf_op | source)
XLA Modules:
  0.0 65.5 jit_solution(5171398141209610616)
XLA Ops:
  0.6 2.3 %shard_map.146 = (f32[72,128]{1,0:T(8,128)S(1)}, bf16[256,128]{1,0:T(8,128)(2,1)S(1)}, bf16[32,32,128]{2,1,0:T(8,128)(2,1)}) custom-call(bf16[2,16384]{1,0:T(2,128)(2,1)} %refs_3_.1, bf16[2,16384]{1,0:T(2,128)(2,1)} %refs_4_.1, bf16[2,16384]{1,0:T(2,128)(2,1)} %taps_hbm.1, bf16[16,16]{1,0:T(8,128)(2,1)} %weight_hbm.1, f32[2]{0:T(128)} %skip_hbm.1, ...), custom_call_target="tpu_custom_call" | custom-call | tf_op jit(solution)/shard_map/pallas_call | solution.py:390
  3.0 7.8 %collective-permute-start = (bf16[2,16384]{1,0:T(2,128)(2,1)S(1)}, bf16[2,16384]{1,0:T(2,128)(2,1)S(1)}, u32[]{:S(2)}, u32[]{:S(2)}) collective-permute-start(bf16[2,16384]{1,0:T(2,128)(2,1)S(1)} %copy-done.7), channel_id=1, source_target_pairs={{0,128},{32,160},{64,192},{96,224},{128,0},{160,32},{192,64},{224,... | collective-permute-start | bytes 196616 | tf_op jit(solution)/shard_map/ppermute | solution.py:419
  10.8 6.8 %all-to-all-start = ((bf16[32,32,128]{2,1,0:T(8,128)(2,1)}), bf16[32,32,128]{2,1,0:T(8,128)(2,1)S(1)}, u32[]{:S(2)}, u32[]{:S(2)}) async-start(bf16[32,32,128]{2,1,0:T(8,128)(2,1)} %get-tuple-element.36), calls=%async_computation | async-start | bytes 524288 | tf_op jit(solution)/shard_map/all_to_all | solution.py:403
  17.6 0.0 copy-start
  17.6 0.0 copy-start.1
  17.6 0.0 copy-start.4
  17.6 0.2 shard_map.147
  17.8 1.4 %collective-permute-start.1 = (bf16[256,128]{1,0:T(8,128)(2,1)S(1)}, bf16[256,128]{1,0:T(8,128)(2,1)S(1)}, u32[]{:S(2)}, u32[]{:S(2)}) collective-permute-start(bf16[256,128]{1,0:T(8,128)(2,1)S(1)} %get-tuple-element.39), channel_id=1, source_target_pairs={{0,32},{32,64},{64,96},{96,0},{128,160},{160,192},{192,224},{224,1... | collective-permute-start | bytes 196616 | tf_op jit(solution)/shard_map/ppermute | solution.py:414
  19.2 2.6 %collective-permute-start.2 = (bf16[256,128]{1,0:T(8,128)(2,1)S(1)}, bf16[256,128]{1,0:T(8,128)(2,1)S(1)}, u32[]{:S(2)}, u32[]{:S(2)}) collective-permute-start(bf16[256,128]{1,0:T(8,128)(2,1)S(1)} %get-tuple-element.40), channel_id=1, source_target_pairs={{0,64},{32,96},{64,0},{96,32},{128,192},{160,224},{192,128},{224,1... | collective-permute-start | bytes 196616 | tf_op jit(solution)/shard_map/ppermute | solution.py:414
  21.8 1.1 %collective-permute-start.3 = (bf16[256,128]{1,0:T(8,128)(2,1)S(1)}, bf16[256,128]{1,0:T(8,128)(2,1)S(1)}, u32[]{:S(2)}, u32[]{:S(2)}) collective-permute-start(bf16[256,128]{1,0:T(8,128)(2,1)S(1)} %get-tuple-element.41), channel_id=1, source_target_pairs={{0,96},{32,0},{64,32},{96,64},{128,224},{160,128},{192,160},{224,1... | collective-permute-start | bytes 196616 | tf_op jit(solution)/shard_map/ppermute | solution.py:414
  22.9 2.3 %collective-permute-done.2.r2_ref = bf16[256,128]{1,0:T(8,128)(2,1)S(1)} collective-permute-done((bf16[256,128]{1,0:T(8,128)(2,1)S(1)}, bf16[256,128]{1,0:T(8,128)(2,1)S(1)}, u32[]{:S(2)}, u32[]{:S(2)}) %collective-permute-start.2) | collective-permute-done | bytes 65568 | tf_op jit(solution)/shard_map/ppermute | solution.py:414
  25.2 0.0 collective-permute-done.3.r3_ref
  25.2 0.4 shard_map.148
  25.6 3.2 %all-to-all-done.spec_ref = bf16[32,32,128]{2,1,0:T(8,128)(2,1)S(1)} async-done(((bf16[32,32,128]{2,1,0:T(8,128)(2,1)}), bf16[32,32,128]{2,1,0:T(8,128)(2,1)S(1)}, u32[]{:S(2)}, u32[]{:S(2)}) %all-to-all-start) | async-done | bytes 262176 | tf_op jit(solution)/shard_map/all_to_all | solution.py:403
  28.9 0.5 shard_map.149
  29.4 0.0 copy-start.6
  29.4 17.1 %all_to_all.15.rows_ref = bf16[32,32,128]{2,1,0:T(8,128)(2,1)S(1)} all-to-all(bf16[32,32,128]{2,1,0:T(8,128)(2,1)S(1)} %shard_map.149), channel_id=1, replica_groups=mesh['tensor'=8,'seq'=32] {'seq'}, dimensions={0} | all-to-all | bytes 524288 | tf_op jit(solution)/shard_map/all_to_all | solution.py:403
  46.5 0.4 shard_map.150
  46.9 1.8 %shard_map.151 = (bf16[32,32,128]{2,1,0:T(8,128)(2,1)}, bf16[2,16384]{1,0:T(2,128)(2,1)}) custom-call(bf16[32,32,128]{2,1,0:T(8,128)(2,1)S(1)} %all-to-all-done.spec_ref, bf16[32,32,128]{2,1,0:T(8,128)(2,1)S(1)} %all_to_all.15.rows_ref, f32[256,128]{1,0:T(8,128)S(1)} %get-tuple-element.44.inner_sum_ref, f32[256,128]{1,0:T(8,128)S(1)} %get-tuple-element.45.gated_ref), custom_call_target="tpu_custom_call" | custom-call | tf_op jit(solution)/shard_map/pallas_call | solution.py:390
  48.7 0.1 collective-permute-start.4
  48.8 0.1 shard_map.152
  48.9 3.7 %all-to-all-start.2 = ((bf16[32,32,128]{2,1,0:T(8,128)(2,1)}), bf16[32,32,128]{2,1,0:T(8,128)(2,1)S(1)}, u32[]{:S(2)}, u32[]{:S(2)}) async-start(bf16[32,32,128]{2,1,0:T(8,128)(2,1)} %get-tuple-element.51), calls=%async_computation.2 | async-start | bytes 524288 | tf_op jit(solution)/shard_map/all_to_all | solution.py:403
  52.6 0.0 copy-start.3
  52.6 3.8 %collective-permute-done.4.far_ref = bf16[256,128]{1,0:T(8,128)(2,1)S(1)} collective-permute-done((bf16[256,128]{1,0:T(8,128)(2,1)S(1)}, bf16[256,128]{1,0:T(8,128)(2,1)S(1)}, u32[]{:S(2)}, u32[]{:S(2)}) %collective-permute-start.4) | collective-permute-done | bytes 65568 | tf_op jit(solution)/shard_map/ppermute | solution.py:419
  56.4 0.1 shard_map.153
  56.5 0.3 collective-permute-start.5
  56.8 3.2 %collective-permute-start.6 = (bf16[256,128]{1,0:T(8,128)(2,1)S(1)}, bf16[256,128]{1,0:T(8,128)(2,1)S(1)}, u32[]{:S(2)}, u32[]{:S(2)}) collective-permute-start(bf16[256,128]{1,0:T(8,128)(2,1)S(1)} %get-tuple-element.56), channel_id=1, source_target_pairs={{0,64},{32,96},{64,0},{96,32},{128,192},{160,224},{192,128},{224,1... | collective-permute-start | bytes 196616 | tf_op jit(solution)/shard_map/ppermute | solution.py:414
  60.1 0.1 collective-permute-start.7
  60.2 1.0 %collective-permute-done.5.refs_9_ = bf16[256,128]{1,0:T(8,128)(2,1)S(1)} collective-permute-done((bf16[256,128]{1,0:T(8,128)(2,1)S(1)}, bf16[256,128]{1,0:T(8,128)(2,1)S(1)}, u32[]{:S(2)}, u32[]{:S(2)}) %collective-permute-start.5) | collective-permute-done | bytes 65568 | tf_op jit(solution)/shard_map/ppermute | solution.py:414
  61.2 1.5 %collective-permute-done.6.refs_10_ = bf16[256,128]{1,0:T(8,128)(2,1)S(1)} collective-permute-done((bf16[256,128]{1,0:T(8,128)(2,1)S(1)}, bf16[256,128]{1,0:T(8,128)(2,1)S(1)}, u32[]{:S(2)}, u32[]{:S(2)}) %collective-permute-start.6) | collective-permute-done | bytes 65568 | tf_op jit(solution)/shard_map/ppermute | solution.py:414
  62.8 1.3 %collective-permute-done.7.refs_11_ = bf16[256,128]{1,0:T(8,128)(2,1)S(1)} collective-permute-done((bf16[256,128]{1,0:T(8,128)(2,1)S(1)}, bf16[256,128]{1,0:T(8,128)(2,1)S(1)}, u32[]{:S(2)}, u32[]{:S(2)}) %collective-permute-start.7) | collective-permute-done | bytes 65568 | tf_op jit(solution)/shard_map/ppermute | solution.py:414
  64.1 1.4 %shard_map.154 = (bf16[2,16384]{1,0:T(2,128)(2,1)}, bf16[2,16384]{1,0:T(2,128)(2,1)}, bf16[2,16384]{1,0:T(2,128)(2,1)}, f32[2,16384]{1,0:T(2,128)}) custom-call(f32[72,128]{1,0:T(8,128)S(1)} %get-tuple-element.34.table_ref.skip_ref.refs_0_, bf16[32,32,128]{2,1,0:T(8,128)(2,1)S(1)} %all-to-all-done.2.refs_1_, bf16[256,128]{1,0:T(8,128)(2,1)S(1)} %get-tuple-element.52.refs_2_, ...), custom_call_target="tpu_custom_call" | custom-call | tf_op jit(solution)/shard_map/pallas_call | solution.py:390
  (14 shorter events, 0.0 us)
Async XLA Ops:
  0.6 2.3 %copy-start.7 = (bf16[2,16384]{1,0:T(2,128)(2,1)S(1)}, bf16[2,16384]{1,0:T(2,128)(2,1)}, u32[]{:S(2)}) copy-start(bf16[2,16384]{1,0:T(2,128)(2,1)} %near_ref.1) | copy-start | bytes 196612
  3.0 14.6 %collective-permute-start = (bf16[2,16384]{1,0:T(2,128)(2,1)S(1)}, bf16[2,16384]{1,0:T(2,128)(2,1)S(1)}, u32[]{:S(2)}, u32[]{:S(2)}) collective-permute-start(bf16[2,16384]{1,0:T(2,128)(2,1)S(1)} %copy-done.7), channel_id=1, source_target_pairs={{0,128},{32,160},{64,192},{96,224},{128,0},{160,32},{192,64},{224,... | collective-permute-start | bytes 196616 | tf_op jit(solution)/shard_map/ppermute | solution.py:419
  10.8 18.1 %all-to-all-start = ((bf16[32,32,128]{2,1,0:T(8,128)(2,1)}), bf16[32,32,128]{2,1,0:T(8,128)(2,1)S(1)}, u32[]{:S(2)}, u32[]{:S(2)}) async-start(bf16[32,32,128]{2,1,0:T(8,128)(2,1)} %get-tuple-element.36), calls=%async_computation | async-start | bytes 524288 | tf_op jit(solution)/shard_map/all_to_all | solution.py:403
  17.6 7.6 %copy-start = (f32[2,128,128]{2,1,0:T(8,128)S(1)}, f32[2,128,128]{2,1,0:T(8,128)}, u32[]{:S(2)}) copy-start(f32[2,128,128]{2,1,0:T(8,128)} %constant.10.clone.turn_hbm.turn_ref.refs_6_) | copy-start | bytes 393220
  17.6 7.6 %copy-start.1 = (bf16[2,128,128]{2,1,0:T(8,128)(2,1)S(1)}, bf16[2,128,128]{2,1,0:T(8,128)(2,1)}, u32[]{:S(2)}) copy-start(bf16[2,128,128]{2,1,0:T(8,128)(2,1)} %constant.11.clone.second_hbm.second_ref.refs_7_) | copy-start | bytes 196612
  17.6 7.6 %copy-start.4 = (bf16[256,128]{1,0:T(8,128)(2,1)S(1)}, bf16[256,128]{1,0:T(8,128)(2,1)}, u32[]{:S(2)}) copy-start(bf16[256,128]{1,0:T(8,128)(2,1)} %constant.8.clone.first_hbm.first_ref) | copy-start | bytes 196612
  17.6 7.6 %copy-start.5 = (bf16[2,16384]{1,0:T(2,128)(2,1)S(1)}, bf16[2,16384]{1,0:T(2,128)(2,1)}, u32[]{:S(2)}) copy-start(bf16[2,16384]{1,0:T(2,128)(2,1)} %query_ref.3) | copy-start | bytes 196612
  17.8 5.1 %collective-permute-start.1 = (bf16[256,128]{1,0:T(8,128)(2,1)S(1)}, bf16[256,128]{1,0:T(8,128)(2,1)S(1)}, u32[]{:S(2)}, u32[]{:S(2)}) collective-permute-start(bf16[256,128]{1,0:T(8,128)(2,1)S(1)} %get-tuple-element.39), channel_id=1, source_target_pairs={{0,32},{32,64},{64,96},{96,0},{128,160},{160,192},{192,224},{224,1... | collective-permute-start | bytes 196616 | tf_op jit(solution)/shard_map/ppermute | solution.py:414
  19.2 6.0 %collective-permute-start.2 = (bf16[256,128]{1,0:T(8,128)(2,1)S(1)}, bf16[256,128]{1,0:T(8,128)(2,1)S(1)}, u32[]{:S(2)}, u32[]{:S(2)}) collective-permute-start(bf16[256,128]{1,0:T(8,128)(2,1)S(1)} %get-tuple-element.40), channel_id=1, source_target_pairs={{0,64},{32,96},{64,0},{96,32},{128,192},{160,224},{192,128},{224,1... | collective-permute-start | bytes 196616 | tf_op jit(solution)/shard_map/ppermute | solution.py:414
  21.8 3.4 %collective-permute-start.3 = (bf16[256,128]{1,0:T(8,128)(2,1)S(1)}, bf16[256,128]{1,0:T(8,128)(2,1)S(1)}, u32[]{:S(2)}, u32[]{:S(2)}) collective-permute-start(bf16[256,128]{1,0:T(8,128)(2,1)S(1)} %get-tuple-element.41), channel_id=1, source_target_pairs={{0,96},{32,0},{64,32},{96,64},{128,224},{160,128},{192,160},{224,1... | collective-permute-start | bytes 196616 | tf_op jit(solution)/shard_map/ppermute | solution.py:414
  29.4 17.1 %copy-start.6 = (bf16[128,256]{1,0:T(8,128)(2,1)S(1)}, bf16[128,256]{1,0:T(8,128)(2,1)}, u32[]{:S(2)}) copy-start(bf16[128,256]{1,0:T(8,128)(2,1)} %constant.9.clone.first_ref.refs_5_) | copy-start | bytes 196612
  48.7 7.7 %collective-permute-start.4 = (bf16[256,128]{1,0:T(8,128)(2,1)S(1)}, bf16[256,128]{1,0:T(8,128)(2,1)S(1)}, u32[]{:S(2)}, u32[]{:S(2)}) collective-permute-start(bf16[256,128]{1,0:T(8,128)(2,1)S(1)} %get-tuple-element.53.near_ref), channel_id=1, source_target_pairs={{0,128},{32,160},{64,192},{96,224},{128,0},{160,32},{192,64},{224,... | collective-permute-start | bytes 196616 | tf_op jit(solution)/shard_map/ppermute | solution.py:419
  48.9 15.2 %all-to-all-start.2 = ((bf16[32,32,128]{2,1,0:T(8,128)(2,1)}), bf16[32,32,128]{2,1,0:T(8,128)(2,1)S(1)}, u32[]{:S(2)}, u32[]{:S(2)}) async-start(bf16[32,32,128]{2,1,0:T(8,128)(2,1)} %get-tuple-element.51), calls=%async_computation.2 | async-start | bytes 524288 | tf_op jit(solution)/shard_map/all_to_all | solution.py:403
  52.5 11.5 %copy-start.2 = (bf16[2,16384]{1,0:T(2,128)(2,1)S(1)}, bf16[2,16384]{1,0:T(2,128)(2,1)}, u32[]{:S(2)}) copy-start(bf16[2,16384]{1,0:T(2,128)(2,1)} %refs_3_.1) | copy-start | bytes 196612
  52.6 11.5 %copy-start.3 = (bf16[2,16384]{1,0:T(2,128)(2,1)S(1)}, bf16[2,16384]{1,0:T(2,128)(2,1)}, u32[]{:S(2)}) copy-start(bf16[2,16384]{1,0:T(2,128)(2,1)} %refs_4_.1) | copy-start | bytes 196612
  56.5 4.7 %collective-permute-start.5 = (bf16[256,128]{1,0:T(8,128)(2,1)S(1)}, bf16[256,128]{1,0:T(8,128)(2,1)S(1)}, u32[]{:S(2)}, u32[]{:S(2)}) collective-permute-start(bf16[256,128]{1,0:T(8,128)(2,1)S(1)} %get-tuple-element.55), channel_id=1, source_target_pairs={{0,32},{32,64},{64,96},{96,0},{128,160},{160,192},{192,224},{224,1... | collective-permute-start | bytes 196616 | tf_op jit(solution)/shard_map/ppermute | solution.py:414
  56.8 5.9 %collective-permute-start.6 = (bf16[256,128]{1,0:T(8,128)(2,1)S(1)}, bf16[256,128]{1,0:T(8,128)(2,1)S(1)}, u32[]{:S(2)}, u32[]{:S(2)}) collective-permute-start(bf16[256,128]{1,0:T(8,128)(2,1)S(1)} %get-tuple-element.56), channel_id=1, source_target_pairs={{0,64},{32,96},{64,0},{96,32},{128,192},{160,224},{192,128},{224,1... | collective-permute-start | bytes 196616 | tf_op jit(solution)/shard_map/ppermute | solution.py:414
  60.1 4.0 %collective-permute-start.7 = (bf16[256,128]{1,0:T(8,128)(2,1)S(1)}, bf16[256,128]{1,0:T(8,128)(2,1)S(1)}, u32[]{:S(2)}, u32[]{:S(2)}) collective-permute-start(bf16[256,128]{1,0:T(8,128)(2,1)S(1)} %get-tuple-element.57), channel_id=1, source_target_pairs={{0,96},{32,0},{64,32},{96,64},{128,224},{160,128},{192,160},{224,1... | collective-permute-start | bytes 196616 | tf_op jit(solution)/shard_map/ppermute | solution.py:414

commit v5 on v3

--- a/solution.py
+++ b/solution.py
@@ -1,5 +1,3 @@
-import math
-
 import jax
 import jax.numpy as jnp
 import numpy as np
@@ -16,6 +14,11 @@
 CHUNK = 16
 WEIGHTS = RING * CH * 2 * CH
 TILE = 4
+ORDER = (
+    19, 23, 29, 26, 5, 17, 30, 10, 25, 16, 0, 3, 4, 14, 22, 6,
+    24, 8, 13, 21, 18, 27, 15, 31, 20, 12, 1, 2, 9, 11, 28, 7,
+)
+PLACE = tuple(ORDER.index(block) for block in range(len(ORDER)))
 BLOCKS = 32
 SIDE = 128
 ROWS = CH * SIDE
@@ -24,7 +27,6 @@
 PIECE = ROWS // BLOCKS
 VMEM = pl.BlockSpec(memory_space=pltpu.VMEM)
 COST = pl.CostEstimate(flops=10000000000, bytes_accessed=1000000, transcendentals=0)
-SMEM = pl.BlockSpec(memory_space=pltpu.SMEM)
 HBM = pl.BlockSpec(memory_space=pltpu.HBM)
 ANY = pl.BlockSpec(memory_space=pl.ANY)
 
@@ -58,52 +60,59 @@
     )
 
 
-def forward(signal, first, turn, second):
-    both = jnp.concatenate([signal[:SIDE], signal[SIDE:]], axis=1)
-    stage = jnp.dot(first, both, preferred_element_type=F32)
+def first_stage(signals, first):
+    both = [signal[c * SIDE : (c + 1) * SIDE] for signal in signals for c in range(CH)]
+    return jnp.dot(first, jnp.concatenate(both, axis=1), preferred_element_type=F32)
+
+
+def last_stage(stages, turn, matrix):
     cos, sin = turn[0], turn[1]
     turned = []
     for c in range(CH):
-        real, imag = (stage[p * SIDE : (p + 1) * SIDE, c * SIDE : (c + 1) * SIDE] for p in (0, 1))
+        real, imag = (
+            stages[p * SIDE : (p + 1) * SIDE, c * SIDE : (c + 1) * SIDE] for p in (0, 1)
+        )
         turned.append(
             jnp.concatenate(
                 [(real * cos + imag * sin).astype(BF16), (imag * cos - real * sin).astype(BF16)],
                 axis=1,
             )
         )
-    spec = jnp.dot(
-        jnp.concatenate(turned, axis=0), second_stage(second, -1), preferred_element_type=F32
-    )
+    spec = jnp.dot(jnp.concatenate(turned, axis=0), matrix, preferred_element_type=F32)
     parts = [spec[:, p * SIDE : (p + 1) * SIDE].reshape(BLOCKS, PIECE, SIDE) for p in (0, 1)]
     return jnp.concatenate(parts, axis=1).astype(BF16)
 
 
-def inverse(rows, first_t, turn, second):
-    rows = rows.astype(F32)
-    real = rows[:, :PIECE].reshape(ROWS, SIDE)
-    imag = rows[:, PIECE:].reshape(ROWS, SIDE)
-    spec = jnp.concatenate([real.astype(BF16), imag.astype(BF16)], axis=1)
-    stage = jnp.dot(spec, second_stage(second, 1), preferred_element_type=F32)
+def inverse(spec, count, first_t, turn, second):
+    stages = jnp.dot(spec, second_stage(second, 1), preferred_element_type=F32)
+    stages = stages.reshape(BLOCKS, count, PIECE, 2 * SIDE)
     cos, sin = turn[0], turn[1]
     turned = []
-    for c in range(CH):
-        real, imag = (stage[c * SIDE : (c + 1) * SIDE, p * SIDE : (p + 1) * SIDE] for p in (0, 1))
-        turned.append(
-            jnp.concatenate(
-                [(real * cos - imag * sin).astype(BF16), (imag * cos + real * sin).astype(BF16)],
-                axis=0,
+    for sig in range(count):
+        for c in range(CH):
+            owners = slice(c * BLOCKS // CH, (c + 1) * BLOCKS // CH)
+            rows = stages[owners, sig].reshape(SIDE, 2 * SIDE)
+            real, imag = rows[:, :SIDE], rows[:, SIDE:]
+            turned.append(
+                jnp.concatenate(
+                    [
+                        (real * cos - imag * sin).astype(BF16),
+                        (imag * cos + real * sin).astype(BF16),
+                    ],
+                    axis=0,
+                )
             )
-        )
     both = jnp.dot(first_t, jnp.concatenate(turned, axis=1), preferred_element_type=F32)
     both = both * (2.0 / LENGTH)
-    return jnp.concatenate([both[:, :SIDE], both[:, SIDE:]], axis=0)
+    columns = [both[:, c * SIDE : (c + 1) * SIDE] for c in range(CH * count)]
+    return [jnp.concatenate(columns[CH * i : CH * i + CH], axis=0) for i in range(count)]
 
 
 def source_kernel(
     key_hbm, value_hbm, taps_hbm, weight_hbm, skip_hbm, first_hbm, turn_hbm, second_hbm,
-    table_ref, kv_hbm, spec_hbm,
+    table_ref, kv_ref, spec_hbm,
     key_ref, value_ref, taps_ref, weight_ref, skip_ref, first_ref, turn_ref, second_ref,
-    kv_ref, spec_ref, sems,
+    spec_ref, sems,
 ):
     copies = []
 
@@ -112,33 +121,33 @@
         copy.start()
         copies.append(copy)
 
-    def part(sig):
-        return spec_hbm.at[:, pl.ds(16 * sig, 16), :]
-
+    send(weight_hbm, weight_ref)
+    send(skip_hbm, skip_ref)
+    send(key_hbm, key_ref)
+    send(value_hbm, value_ref)
     send(taps_hbm, taps_ref)
     send(first_hbm, first_ref)
     send(turn_hbm, turn_ref)
     send(second_hbm, second_ref)
-    send(key_hbm, key_ref)
-    send(value_hbm, value_ref)
-    send(weight_hbm, weight_ref)
-    send(skip_hbm, skip_ref)
-    for copy in copies:
+    for copy in copies[:2]:
         copy.wait()
-    arrived = len(copies)
-    tables_in = (first_ref[...], turn_ref[...], second_ref[...])
-    spec_ref[1] = forward(square(taps_ref).astype(BF16), *tables_in)
-    send(spec_ref.at[1], part(1))
-    key_value = (square(key_ref) * square(value_ref)).astype(BF16)
-    kv_ref[...] = key_value
-    send(kv_ref, kv_hbm)
-    spec_ref[0] = forward(key_value, *tables_in)
-    send(spec_ref.at[0], part(0))
     table_ref[:WEIGHTS, :] = weight_rows(weight_ref[...], True)
     table_ref[WEIGHTS : 2 * WEIGHTS, :] = weight_rows(weight_ref[...], False)
     row = lax.broadcasted_iota(jnp.int32, (8, SIDE), 0)
     table_ref[2 * WEIGHTS :, :] = jnp.where(row == 0, skip_ref[0], skip_ref[1])
-    for copy in copies[arrived:]:
+    for copy in copies[2:6]:
+        copy.wait()
+    key_value = (square(key_ref) * square(value_ref)).astype(BF16)
+    kv_ref[...] = key_value
+    stages = first_stage([key_value, square(taps_ref).astype(BF16)], first_ref[...])
+    for copy in copies[6:]:
+        copy.wait()
+    matrix = second_stage(second_ref[...], -1)
+    for sig in range(2):
+        columns = stages[:, sig * ROWS : (sig + 1) * ROWS]
+        spec_ref[:, 16 * sig : 16 * sig + 16, :] = last_stage(columns, turn_ref[...], matrix)
+    send(spec_ref, spec_hbm)
+    for copy in copies[8:]:
         copy.wait()
 
 
@@ -210,7 +219,7 @@
 
 def put(out_ref, blk, sig, real, imag):
     both = jnp.concatenate([real, imag], axis=0)
-    out_ref[blk, 16 * sig : 16 * sig + 16, :] = both.astype(BF16)
+    out_ref[PLACE[blk], 16 * sig : 16 * sig + 16, :] = both.astype(BF16)
 
 
 def add(total, parts):
@@ -219,7 +228,7 @@
 
 def convolve(buf_ref, out_ref, sign):
     def at(slot, blk):
-        return buf_ref[slot, 0, blk], buf_ref[slot, 1, blk]
+        return buf_ref[slot, 0, PLACE[blk]], buf_ref[slot, 1, PLACE[blk]]
 
     last = None
     for base in range(0, BLOCKS, TILE):
@@ -247,34 +256,39 @@
             last = total
 
 
-def correlate(buf_ref, out_ref, sign, other, sig):
-    def at(slot, blk):
-        return buf_ref[slot, 0, blk], buf_ref[slot, 1, blk]
-
-    after = None
+def correlate(buf_ref, loaded_ref, out_ref, sign):
+    def at(ref, slot, blk):
+        return ref[slot, 0, PLACE[blk]], ref[slot, 1, PLACE[blk]]
+
+    after = [None, None]
     for base in range(BLOCKS - TILE, -1, -TILE):
-        sums = [None] * TILE
-        window = {}
-        for j in range(BLOCKS - base):
-            hr, hi = at(other, j)
-            plus, minus = hr + hi, hr - hi
-            for o in range(TILE):
-                blk = base + o + j
-                if blk >= BLOCKS:
-                    continue
-                if blk not in window:
-                    gr, gi = at(2, blk)
-                    window[blk] = (gr, gi, gr + gi)
-                gr, gi, both = window[blk]
-                sums[o] = add(sums[o], (hr * both, gi * minus, gr * plus))
-        for o in range(TILE - 1, -1, -1):
-            common, of_real, of_imag = sums[o]
-            total = (common - of_real, common - of_imag)
-            real, imag = total
-            if after is not None:
-                real, imag = real + sign * after[1], imag - sign * after[0]
-            put(out_ref, base + o, sig, real, imag)
-            after = total
+        rows = [[None, None] for _ in range(TILE)]
+        for sig, other in ((0, 1), (1, 0)):
+            sums = [None] * TILE
+            window = {}
+            for j in range(BLOCKS - base):
+                hr, hi = at(loaded_ref, other, j)
+                plus, minus = hr + hi, hr - hi
+                for o in range(TILE):
+                    blk = base + o + j
+                    if blk >= BLOCKS:
+                        continue
+                    if blk not in window:
+                        gr, gi = at(buf_ref, 0, blk)
+                        window[blk] = (gr, gi, gr + gi)
+                    gr, gi, both = window[blk]
+                    sums[o] = add(sums[o], (hr * both, gi * minus, gr * plus))
+            for o in range(TILE - 1, -1, -1):
+                common, of_real, of_imag = sums[o]
+                total = (common - of_real, common - of_imag)
+                real, imag = total
+                if after[sig] is not None:
+                    real, imag = real + sign * after[sig][1], imag - sign * after[sig][0]
+                rows[o][sig] = (real, imag)
+                after[sig] = total
+        for o in range(TILE):
+            for p in range(2):
+                put(out_ref, base + o, p, rows[o][0][p], rows[o][1][p])
 
 
 def convolve_kernel(spec_ref, grad_ref, out_ref, buf_ref):
@@ -292,40 +306,66 @@
     gated_ref[...] = grad_gated
     grad_inner = (grad_gated * square(query_ref)).astype(BF16)
     inner_ref[...] = grad_inner
-    out_ref[...] = forward(grad_inner, first_ref[...], turn_ref[...], second_ref[...])
-
-
-def correlate_kernel(
-    spec_ref, rows_ref, inner_sum_ref, gated_ref, out_hbm, grad_query_hbm,
+    stages = first_stage([grad_inner], first_ref[...])
+    out_ref[...] = last_stage(stages, turn_ref[...], second_stage(second_ref[...], -1))
+
+
+def gate(table_ref, rows_ref, kv_ref, query_ref, first_ref, turn_ref, second_ref, out_ref):
+    rows = rows_ref[:, :16, :].astype(F32)
+    parts = [rows[:, p * PIECE : (p + 1) * PIECE].reshape(ROWS, SIDE).astype(BF16) for p in (0, 1)]
+    (convolved,) = inverse(
+        jnp.concatenate(parts, axis=1), 1, first_ref[...], turn_ref[...], second_ref[...]
+    )
+    inner_sum = convolved + skip_rows(table_ref) * kv_ref[...].astype(F32)
+    out_ref[...] = (square(query_ref) * inner_sum).astype(BF16)
+    return inner_sum
+
+
+def correlations(
+    loaded_ref, rows_ref, inner_sum, gated_ref, out_hbm, grad_query_hbm,
     buf_ref, out_ref, grad_query_ref, sems,
 ):
-    grad_query_ref[...] = (gated_ref[...] * inner_sum_ref[...]).reshape(CH, BLOCK).astype(BF16)
+    grad_query_ref[...] = (gated_ref[...] * inner_sum).reshape(CH, BLOCK).astype(BF16)
     query_copy = pltpu.make_async_copy(grad_query_ref, grad_query_hbm, sems.at[0])
     query_copy.start()
-    load(spec_ref, 0, buf_ref, 0)
-    load(spec_ref, 1, buf_ref, 1)
-    load(rows_ref, 1, buf_ref, 2)
+    load(rows_ref, 1, buf_ref, 0)
     sign = alternate()
-    copies = []
-    for sig, other in ((0, 1), (1, 0)):
-        correlate(buf_ref, out_ref.at[sig], sign, other, 0)
-        copy = pltpu.make_async_copy(
-            out_ref.at[sig], out_hbm.at[:, pl.ds(16 * sig, 16), :], sems.at[1 + sig]
+    correlate(buf_ref, loaded_ref, out_ref, sign)
+    copy = pltpu.make_async_copy(out_ref, out_hbm, sems.at[1])
+    copy.start()
+    copy.wait()
+    query_copy.wait()
+
+
+def near_kernel(
+    table_ref, rows_ref, kv_ref, query_ref, first_ref, turn_ref, second_ref, loaded_ref, gated_ref,
+    gated_out_ref, inner_sum_ref, out_hbm, grad_query_hbm, *scratch,
+):
+    gate_refs = (
+        table_ref, rows_ref, kv_ref, query_ref, first_ref, turn_ref, second_ref, gated_out_ref
+    )
+    near = lax.axis_index("tensor") // RING == 0
+
+    @pl.when(near)
+    def _():
+        inner_sum = gate(*gate_refs)
+        correlations(
+            loaded_ref, rows_ref, inner_sum, gated_ref, out_hbm, grad_query_hbm, *scratch
         )
-        copy.start()
-        copies.append(copy)
-    for copy in copies:
-        copy.wait()
-    query_copy.wait()
-
-
-def gate_kernel(
-    skip_ref, rows_ref, kv_ref, query_ref, first_ref, turn_ref, second_ref, out_ref, inner_sum_ref
+
+    @pl.when(jnp.logical_not(near))
+    def _():
+        inner_sum_ref[...] = gate(*gate_refs)
+
+
+def far_kernel(
+    loaded_ref, rows_ref, inner_sum_ref, gated_ref, _, __, out_hbm, grad_query_hbm, *scratch
 ):
-    convolved = inverse(rows_ref[:, :16, :], first_ref[...], turn_ref[...], second_ref[...])
-    inner_sum = convolved + skip_rows(skip_ref) * kv_ref[...].astype(F32)
-    inner_sum_ref[...] = inner_sum
-    out_ref[...] = (square(query_ref) * inner_sum).astype(BF16)
+    @pl.when(lax.axis_index("tensor") // RING == 1)
+    def _():
+        correlations(
+            loaded_ref, rows_ref, inner_sum_ref[...], gated_ref, out_hbm, grad_query_hbm, *scratch
+        )
 
 
 def skip_rows(table_ref):
@@ -355,10 +395,10 @@
     out_ref[...] = both.reshape(CH, BLOCK).astype(BF16)
     send(out_ref, out_hbm)
     tables_in = (first_ref[...], turn_ref[...], second_ref[...])
-    taps = inverse(rows_ref[:, 16:, :], *tables_in) * scale
-    grad_taps_ref[...] = taps.reshape(CH, BLOCK)
+    parts = [rows_ref[:, 16 * p : 16 * p + 16, :].reshape(2 * ROWS, SIDE) for p in (0, 1)]
+    source, taps = inverse(jnp.concatenate(parts, axis=1), 2, *tables_in)
+    grad_taps_ref[...] = (taps * scale).reshape(CH, BLOCK)
     send(grad_taps_ref, grad_taps_hbm)
-    source = inverse(rows_ref[:, :16, :], *tables_in)
     source = source + skip_rows(table_ref) * inner_ref[...].astype(F32)
     source = source.reshape(CH, BLOCK)
     grad_key_ref[...] = (source * value_ref[...].astype(F32)).astype(BF16)
@@ -369,20 +409,23 @@
         copy.wait()
 
 
-def call(kernel, outs, operands, smem=0, scratch=(), place=VMEM, limit=48, cost=None, out_place=VMEM):
+def call(kernel, outs, operands, scratch=(), place=VMEM, limit=48, cost=None, out_place=VMEM, aliases=None):
     return pl.pallas_call(
         kernel,
         out_shape=[jax.ShapeDtypeStruct(shape, dtype) for shape, dtype in outs],
-        in_specs=[SMEM] * smem + [place] * (len(operands) - smem),
+        in_specs=place if isinstance(place, list) else [place] * len(operands),
         out_specs=out_place if isinstance(out_place, list) else [out_place] * len(outs),
         scratch_shapes=list(scratch),
+        input_output_aliases=aliases or {},
         cost_estimate=cost,
         compiler_params=pltpu.CompilerParams(vmem_limit_bytes=limit * 1024 * 1024),
     )(*operands)
 
 
 def exchange(blocks):
-    return lax.all_to_all(blocks, "seq", split_axis=0, concat_axis=0, tiled=True)
+    return lax.all_to_all(
+        blocks, "seq", split_axis=0, concat_axis=0, tiled=True, axis_index_groups=[list(ORDER)]
+    )
 
 
 def along_y(arrays):
@@ -411,24 +454,28 @@
     parts = [(square_shape, F32)] + [(square_shape, BF16)] * (RING - 1)
 
     first_inputs = (key_feats, value_feats, filter_taps, out_weight, skip_gain, *forward_tables)
+    first_inputs = [
+        pltpu.with_memory_space_constraint(array, pltpu.HBM) for array in first_inputs
+    ]
+
     table, key_value, spec = call(
         source_kernel,
         [((2 * WEIGHTS + 8, SIDE), F32), (square_shape, BF16), (two, BF16)],
-        [pltpu.with_memory_space_constraint(array, pltpu.HBM) for array in first_inputs],
+        first_inputs,
         scratch=[
             *[pltpu.VMEM(tokens, BF16)] * 3,
             pltpu.VMEM(out_weight.shape, BF16),
             pltpu.SMEM((CH,), F32),
             *[pltpu.VMEM(array.shape, array.dtype) for array in forward_tables],
-            pltpu.VMEM(square_shape, BF16),
-            pltpu.VMEM((2, *one), BF16),
-            pltpu.SemaphoreType.DMA((11,)),
+            pltpu.VMEM(two, BF16),
+            pltpu.SemaphoreType.DMA((len(first_inputs) + 1,)),
         ],
         place=HBM,
         limit=32,
-        out_place=[VMEM, ANY, ANY],
-    )
-    far = across(out_grad)
+        out_place=[VMEM, VMEM, ANY],
+    )
+    spec, far = lax.optimization_barrier((spec, out_grad))
+    far = across(far)
     spec = exchange(spec)
     mine, *others = call(
         grad_mix_kernel,
@@ -443,31 +490,34 @@
         [(square_shape, F32), (square_shape, BF16), (one, BF16)],
         (mine, *others, queries, *forward_tables),
     )
-    (rows,) = call(
+    rows, loaded = call(
         convolve_kernel,
-        [(two, BF16)],
+        [(two, BF16), ((2, 2, BLOCKS, PIECE, SIDE), F32)],
         (spec, grad_spec),
-        scratch=[pltpu.VMEM((2, 2, BLOCKS, PIECE, SIDE), F32)],
     )
     rows = exchange(rows)
-    gated, inner_sum = call(
-        gate_kernel,
-        [(square_shape, BF16), (square_shape, F32)],
-        (table, rows, key_value, queries, *inverse_tables),
+    scratch = [
+        pltpu.VMEM((1, 2, BLOCKS, PIECE, SIDE), F32),
+        pltpu.VMEM(two, BF16),
+        pltpu.VMEM(tokens, BF16),
+        pltpu.SemaphoreType.DMA((2,)),
+    ]
+    gated, inner_sum, *begun = call(
+        near_kernel,
+        [(square_shape, BF16), (square_shape, F32), (two, BF16), (tokens, BF16)],
+        (table, rows, key_value, queries, *inverse_tables, loaded, grad_gated),
+        scratch=scratch,
+        out_place=[VMEM, VMEM, ANY, ANY],
     )
     far = across(gated)
-    rows, gated = lax.optimization_barrier((rows, gated))
     corr, grad_queries = call(
-        correlate_kernel,
+        far_kernel,
         [(two, BF16), (tokens, BF16)],
-        (spec, rows, inner_sum, grad_gated),
-        scratch=[
-            pltpu.VMEM((3, 2, BLOCKS, PIECE, SIDE), F32),
-            pltpu.VMEM((2, *one), BF16),
-            pltpu.VMEM(tokens, BF16),
-            pltpu.SemaphoreType.DMA((3,)),
-        ],
+        (loaded, rows, inner_sum, grad_gated, *begun),
+        scratch=scratch,
+        place=[VMEM] * 4 + [ANY] * 2,
         out_place=ANY,
+        aliases={4: 0, 5: 1},
     )
     corr = exchange(corr)
     mine, *others = call(out_mix_kernel, parts, (table, gated, far), cost=COST)

time: 67.6 us -> 62.1 us (0.919)
  the two profiles are of different devices: /device:TPU:1 before, /device:TPU:32 now
where the time goes in v5:
time: 62.1 us; the launch traced here: 61.8 us
  starting transfers between devices  29.1 us (47%)
  blocking collectives  14.4 us (23%)
  waiting for transfers between devices  10.3 us (17%)
  Pallas kernels  7.1 us (11%)
  between operations  0.81 us (1%)
    all_to_all x1, blocking collectives, exchange(): lax.all_to_all(blocks, 'seq', split_axis=0, concat_axis=0, tiled=True, ax...  14.4 us
    all_to_all x2, starting transfers between devices, exchange(): lax.all_to_all(blocks, 'seq', split_axis=0, concat_axis=0, tiled=True, ax...  12 us
    ppermute x6, starting transfers between devices, along_y(): received.append(lax.ppermute(array, 'tensor', pairs))  10.1 us
    pallas_call x8, Pallas kernels, call(): pl.pallas_call(kernel, out_shape=[jax.ShapeDtypeStruct(shape, dtype) for...  7.1 us
    ppermute x6, waiting for transfers between devices, along_y(): received.append(lax.ppermute(array, 'tensor', pairs))  7.05 us
    ppermute x2, starting transfers between devices, across(): lax.ppermute(array, 'tensor', [(i, (i + RING) % GROUP) for i in range(GRO...  6.95 us
    ppermute x2, waiting for transfers between devices, across(): lax.ppermute(array, 'tensor', [(i, (i + RING) % GROUP) for i in range(GRO...  3.26 us
  transfers between devices with their start and end apart: 10, of which 6 were waited for; matrix products, arithmetic and copies ran while one was open for 0% of the time, Pallas kernels for 1%

profile of v5, /device:TPU:32, one launch (start us, length us, event | category | flops | bytes accessed | tf_op | source)
XLA Modules:
  0.0 61.8 jit_solution(12924228911112815310)
XLA Ops:
  0.6 2.3 %shard_map.146 = (f32[72,128]{1,0:T(8,128)S(1)}, bf16[256,128]{1,0:T(8,128)(2,1)S(1)}, bf16[32,32,128]{2,1,0:T(8,128)(2,1)}) custom-call(bf16[2,16384]{1,0:T(2,128)(2,1)} %refs_3_.1, bf16[2,16384]{1,0:T(2,128)(2,1)} %refs_4_.1, bf16[2,16384]{1,0:T(2,128)(2,1)} %taps_hbm.1, bf16[16,16]{1,0:T(8,128)(2,1)} %weight_hbm.1, f32[2]{0:T(128)} %skip_hbm.1, ...), custom_call_target="tpu_custom_call" | custom-call | tf_op jit(solution)/shard_map/pallas_call | solution.py:413
  3.0 6.4 %collective-permute-start = (bf16[2,16384]{1,0:T(2,128)(2,1)S(1)}, bf16[2,16384]{1,0:T(2,128)(2,1)S(1)}, u32[]{:S(2)}, u32[]{:S(2)}) collective-permute-start(bf16[2,16384]{1,0:T(2,128)(2,1)S(1)} %copy-done.7), channel_id=1, source_target_pairs={{0,128},{32,160},{64,192},{96,224},{128,0},{160,32},{192,64},{224,... | collective-permute-start | bytes 196616 | tf_op jit(solution)/shard_map/ppermute | solution.py:444
  9.3 6.3 %all-to-all-start = ((bf16[32,32,128]{2,1,0:T(8,128)(2,1)}), bf16[32,32,128]{2,1,0:T(8,128)(2,1)S(1)}, u32[]{:S(2)}, u32[]{:S(2)}) async-start(bf16[32,32,128]{2,1,0:T(8,128)(2,1)} %get-tuple-element.35), calls=%async_computation | async-start | bytes 524288 | tf_op jit(solution)/shard_map/all_to_all | solution.py:426
  15.7 0.0 copy-start
  15.7 0.0 copy-start.1
  15.7 0.0 copy-start.4
  15.7 0.0 copy-start.5
  15.8 0.2 shard_map.147
  15.9 1.7 %collective-permute-start.1 = (bf16[256,128]{1,0:T(8,128)(2,1)S(1)}, bf16[256,128]{1,0:T(8,128)(2,1)S(1)}, u32[]{:S(2)}, u32[]{:S(2)}) collective-permute-start(bf16[256,128]{1,0:T(8,128)(2,1)S(1)} %get-tuple-element.38), channel_id=1, source_target_pairs={{0,32},{32,64},{64,96},{96,0},{128,160},{160,192},{192,224},{224,1... | collective-permute-start | bytes 196616 | tf_op jit(solution)/shard_map/ppermute | solution.py:439
  17.6 2.9 %collective-permute-start.2 = (bf16[256,128]{1,0:T(8,128)(2,1)S(1)}, bf16[256,128]{1,0:T(8,128)(2,1)S(1)}, u32[]{:S(2)}, u32[]{:S(2)}) collective-permute-start(bf16[256,128]{1,0:T(8,128)(2,1)S(1)} %get-tuple-element.39), channel_id=1, source_target_pairs={{0,64},{32,96},{64,0},{96,32},{128,192},{160,224},{192,128},{224,1... | collective-permute-start | bytes 196616 | tf_op jit(solution)/shard_map/ppermute | solution.py:439
  20.5 1.3 %collective-permute-start.3 = (bf16[256,128]{1,0:T(8,128)(2,1)S(1)}, bf16[256,128]{1,0:T(8,128)(2,1)S(1)}, u32[]{:S(2)}, u32[]{:S(2)}) collective-permute-start(bf16[256,128]{1,0:T(8,128)(2,1)S(1)} %get-tuple-element.40), channel_id=1, source_target_pairs={{0,96},{32,0},{64,32},{96,64},{128,224},{160,128},{192,160},{224,1... | collective-permute-start | bytes 196616 | tf_op jit(solution)/shard_map/ppermute | solution.py:439
  21.8 0.0 collective-permute-done.1.r1_ref
  21.8 2.1 %collective-permute-done.2.r2_ref = bf16[256,128]{1,0:T(8,128)(2,1)S(1)} collective-permute-done((bf16[256,128]{1,0:T(8,128)(2,1)S(1)}, bf16[256,128]{1,0:T(8,128)(2,1)S(1)}, u32[]{:S(2)}, u32[]{:S(2)}) %collective-permute-start.2) | collective-permute-done | bytes 65568 | tf_op jit(solution)/shard_map/ppermute | solution.py:439
  23.9 0.8 %collective-permute-done.3.r3_ref = bf16[256,128]{1,0:T(8,128)(2,1)S(1)} collective-permute-done((bf16[256,128]{1,0:T(8,128)(2,1)S(1)}, bf16[256,128]{1,0:T(8,128)(2,1)S(1)}, u32[]{:S(2)}, u32[]{:S(2)}) %collective-permute-start.3) | collective-permute-done | bytes 65568 | tf_op jit(solution)/shard_map/ppermute | solution.py:439
  24.8 0.4 shard_map.148
  25.2 0.5 shard_map.149
  25.7 0.0 copy-start.6
  25.7 14.4 %all_to_all.15.rows_ref = bf16[32,32,128]{2,1,0:T(8,128)(2,1)S(1)} all-to-all(bf16[32,32,128]{2,1,0:T(8,128)(2,1)S(1)} %get-tuple-element.43), channel_id=1, replica_groups={{19,23,29,26,5,17,30,10,25,16,0,3,4,14,22,6,24,8,13,21,18,27,15,31,20,1..., dimensions={0} | all-to-all | bytes 524288 | tf_op jit(solution)/shard_map/all_to_all | solution.py:426
  40.1 2.1 %shard_map.150 = (bf16[256,128]{1,0:T(8,128)(2,1)S(1)}, f32[256,128]{1,0:T(8,128)S(1)}, bf16[32,32,128]{2,1,0:T(8,128)(2,1)}, bf16[2,16384]{1,0:T(2,128)(2,1)}) custom-call(f32[72,128]{1,0:T(8,128)S(1)} %get-tuple-element.33.table_ref.refs_0_, bf16[32,32,128]{2,1,0:T(8,128)(2,1)S(1)} %all_to_all.15.rows_ref, bf16[256,128]{1,0:T(8,128)(2,1)S(1)} %get-tuple-element.44.kv_ref, ...), custom_call_target="tpu_custom_call" | custom-call | tf_op jit(solution)/shard_map/pallas_call | solution.py:413
  42.3 0.6 collective-permute-start.4
  42.9 5.6 %all-to-all-start.2 = ((bf16[32,32,128]{2,1,0:T(8,128)(2,1)}), bf16[32,32,128]{2,1,0:T(8,128)(2,1)S(1)}, u32[]{:S(2)}, u32[]{:S(2)}) async-start(bf16[32,32,128]{2,1,0:T(8,128)(2,1)} %get-tuple-element.49), calls=%async_computation.2 | async-start | bytes 524288 | tf_op jit(solution)/shard_map/all_to_all | solution.py:426
  48.5 0.0 copy-start.2
  48.6 0.0 copy-start.3
  48.6 3.3 %collective-permute-done.4.far_ref = bf16[256,128]{1,0:T(8,128)(2,1)S(1)} collective-permute-done((bf16[256,128]{1,0:T(8,128)(2,1)S(1)}, bf16[256,128]{1,0:T(8,128)(2,1)S(1)}, u32[]{:S(2)}, u32[]{:S(2)}) %collective-permute-start.4) | collective-permute-done | bytes 65568 | tf_op jit(solution)/shard_map/ppermute | solution.py:444
  51.8 0.1 shard_map.152
  52.0 0.4 collective-permute-start.5
  52.4 3.7 %collective-permute-start.6 = (bf16[256,128]{1,0:T(8,128)(2,1)S(1)}, bf16[256,128]{1,0:T(8,128)(2,1)S(1)}, u32[]{:S(2)}, u32[]{:S(2)}) collective-permute-start(bf16[256,128]{1,0:T(8,128)(2,1)S(1)} %get-tuple-element.54), channel_id=1, source_target_pairs={{0,64},{32,96},{64,0},{96,32},{128,192},{160,224},{192,128},{224,1... | collective-permute-start | bytes 196616 | tf_op jit(solution)/shard_map/ppermute | solution.py:439
  56.1 0.1 collective-permute-start.7
  56.2 2.0 %collective-permute-done.5.refs_9_ = bf16[256,128]{1,0:T(8,128)(2,1)S(1)} collective-permute-done((bf16[256,128]{1,0:T(8,128)(2,1)S(1)}, bf16[256,128]{1,0:T(8,128)(2,1)S(1)}, u32[]{:S(2)}, u32[]{:S(2)}) %collective-permute-start.5) | collective-permute-done | bytes 65568 | tf_op jit(solution)/shard_map/ppermute | solution.py:439
  58.2 0.8 %collective-permute-done.6.refs_10_ = bf16[256,128]{1,0:T(8,128)(2,1)S(1)} collective-permute-done((bf16[256,128]{1,0:T(8,128)(2,1)S(1)}, bf16[256,128]{1,0:T(8,128)(2,1)S(1)}, u32[]{:S(2)}, u32[]{:S(2)}) %collective-permute-start.6) | collective-permute-done | bytes 65568 | tf_op jit(solution)/shard_map/ppermute | solution.py:439
  59.1 1.3 %collective-permute-done.7.refs_11_ = bf16[256,128]{1,0:T(8,128)(2,1)S(1)} collective-permute-done((bf16[256,128]{1,0:T(8,128)(2,1)S(1)}, bf16[256,128]{1,0:T(8,128)(2,1)S(1)}, u32[]{:S(2)}, u32[]{:S(2)}) %collective-permute-start.7) | collective-permute-done | bytes 65568 | tf_op jit(solution)/shard_map/ppermute | solution.py:439
  60.3 1.4 %shard_map.153 = (bf16[2,16384]{1,0:T(2,128)(2,1)}, bf16[2,16384]{1,0:T(2,128)(2,1)}, bf16[2,16384]{1,0:T(2,128)(2,1)}, f32[2,16384]{1,0:T(2,128)}) custom-call(f32[72,128]{1,0:T(8,128)S(1)} %get-tuple-element.33.table_ref.refs_0_, bf16[32,32,128]{2,1,0:T(8,128)(2,1)S(1)} %all-to-all-done.2.refs_1_, bf16[256,128]{1,0:T(8,128)(2,1)S(1)} %get-tuple-element.50.refs_2_, ...), custom_call_target="tpu_custom_call" | custom-call | tf_op jit(solution)/shard_map/pallas_call | solution.py:413
  (13 shorter events, 0.0 us)
Async XLA Ops:
  0.6 2.3 %copy-start.7 = (bf16[2,16384]{1,0:T(2,128)(2,1)S(1)}, bf16[2,16384]{1,0:T(2,128)(2,1)}, u32[]{:S(2)}) copy-start(bf16[2,16384]{1,0:T(2,128)(2,1)} %near_ref.1) | copy-start | bytes 196612
  3.0 12.7 %collective-permute-start = (bf16[2,16384]{1,0:T(2,128)(2,1)S(1)}, bf16[2,16384]{1,0:T(2,128)(2,1)S(1)}, u32[]{:S(2)}, u32[]{:S(2)}) collective-permute-start(bf16[2,16384]{1,0:T(2,128)(2,1)S(1)} %copy-done.7), channel_id=1, source_target_pairs={{0,128},{32,160},{64,192},{96,224},{128,0},{160,32},{192,64},{224,... | collective-permute-start | bytes 196616 | tf_op jit(solution)/shard_map/ppermute | solution.py:444
  9.3 15.8 %all-to-all-start = ((bf16[32,32,128]{2,1,0:T(8,128)(2,1)}), bf16[32,32,128]{2,1,0:T(8,128)(2,1)S(1)}, u32[]{:S(2)}, u32[]{:S(2)}) async-start(bf16[32,32,128]{2,1,0:T(8,128)(2,1)} %get-tuple-element.35), calls=%async_computation | async-start | bytes 524288 | tf_op jit(solution)/shard_map/all_to_all | solution.py:426
  15.7 9.0 %copy-start = (f32[2,128,128]{2,1,0:T(8,128)S(1)}, f32[2,128,128]{2,1,0:T(8,128)}, u32[]{:S(2)}) copy-start(f32[2,128,128]{2,1,0:T(8,128)} %constant.10.clone.turn_hbm.turn_ref.refs_6_) | copy-start | bytes 393220
  15.7 9.0 %copy-start.1 = (bf16[2,128,128]{2,1,0:T(8,128)(2,1)S(1)}, bf16[2,128,128]{2,1,0:T(8,128)(2,1)}, u32[]{:S(2)}) copy-start(bf16[2,128,128]{2,1,0:T(8,128)(2,1)} %constant.11.clone.second_hbm.second_ref.refs_7_) | copy-start | bytes 196612
  15.7 9.0 %copy-start.4 = (bf16[256,128]{1,0:T(8,128)(2,1)S(1)}, bf16[256,128]{1,0:T(8,128)(2,1)}, u32[]{:S(2)}) copy-start(bf16[256,128]{1,0:T(8,128)(2,1)} %constant.8.clone.first_hbm.first_ref) | copy-start | bytes 196612
  15.7 9.0 %copy-start.5 = (bf16[2,16384]{1,0:T(2,128)(2,1)S(1)}, bf16[2,16384]{1,0:T(2,128)(2,1)}, u32[]{:S(2)}) copy-start(bf16[2,16384]{1,0:T(2,128)(2,1)} %query_ref.3) | copy-start | bytes 196612
  15.9 5.9 %collective-permute-start.1 = (bf16[256,128]{1,0:T(8,128)(2,1)S(1)}, bf16[256,128]{1,0:T(8,128)(2,1)S(1)}, u32[]{:S(2)}, u32[]{:S(2)}) collective-permute-start(bf16[256,128]{1,0:T(8,128)(2,1)S(1)} %get-tuple-element.38), channel_id=1, source_target_pairs={{0,32},{32,64},{64,96},{96,0},{128,160},{160,192},{192,224},{224,1... | collective-permute-start | bytes 196616 | tf_op jit(solution)/shard_map/ppermute | solution.py:439
  17.6 6.3 %collective-permute-start.2 = (bf16[256,128]{1,0:T(8,128)(2,1)S(1)}, bf16[256,128]{1,0:T(8,128)(2,1)S(1)}, u32[]{:S(2)}, u32[]{:S(2)}) collective-permute-start(bf16[256,128]{1,0:T(8,128)(2,1)S(1)} %get-tuple-element.39), channel_id=1, source_target_pairs={{0,64},{32,96},{64,0},{96,32},{128,192},{160,224},{192,128},{224,1... | collective-permute-start | bytes 196616 | tf_op jit(solution)/shard_map/ppermute | solution.py:439
  20.5 4.3 %collective-permute-start.3 = (bf16[256,128]{1,0:T(8,128)(2,1)S(1)}, bf16[256,128]{1,0:T(8,128)(2,1)S(1)}, u32[]{:S(2)}, u32[]{:S(2)}) collective-permute-start(bf16[256,128]{1,0:T(8,128)(2,1)S(1)} %get-tuple-element.40), channel_id=1, source_target_pairs={{0,96},{32,0},{64,32},{96,64},{128,224},{160,128},{192,160},{224,1... | collective-permute-start | bytes 196616 | tf_op jit(solution)/shard_map/ppermute | solution.py:439
  25.7 14.4 %copy-start.6 = (bf16[128,256]{1,0:T(8,128)(2,1)S(1)}, bf16[128,256]{1,0:T(8,128)(2,1)}, u32[]{:S(2)}) copy-start(bf16[128,256]{1,0:T(8,128)(2,1)} %constant.9.clone.first_ref.refs_5_) | copy-start | bytes 196612
  42.3 9.5 %collective-permute-start.4 = (bf16[256,128]{1,0:T(8,128)(2,1)S(1)}, bf16[256,128]{1,0:T(8,128)(2,1)S(1)}, u32[]{:S(2)}, u32[]{:S(2)}) collective-permute-start(bf16[256,128]{1,0:T(8,128)(2,1)S(1)} %get-tuple-element.51.near_ref), channel_id=1, source_target_pairs={{0,128},{32,160},{64,192},{96,224},{128,0},{160,32},{192,64},{224,... | collective-permute-start | bytes 196616 | tf_op jit(solution)/shard_map/ppermute | solution.py:444
  42.9 17.4 %all-to-all-start.2 = ((bf16[32,32,128]{2,1,0:T(8,128)(2,1)}), bf16[32,32,128]{2,1,0:T(8,128)(2,1)S(1)}, u32[]{:S(2)}, u32[]{:S(2)}) async-start(bf16[32,32,128]{2,1,0:T(8,128)(2,1)} %get-tuple-element.49), calls=%async_computation.2 | async-start | bytes 524288 | tf_op jit(solution)/shard_map/all_to_all | solution.py:426
  48.5 11.8 %copy-start.2 = (bf16[2,16384]{1,0:T(2,128)(2,1)S(1)}, bf16[2,16384]{1,0:T(2,128)(2,1)}, u32[]{:S(2)}) copy-start(bf16[2,16384]{1,0:T(2,128)(2,1)} %refs_3_.1) | copy-start | bytes 196612
  48.6 11.8 %copy-start.3 = (bf16[2,16384]{1,0:T(2,128)(2,1)S(1)}, bf16[2,16384]{1,0:T(2,128)(2,1)}, u32[]{:S(2)}) copy-start(bf16[2,16384]{1,0:T(2,128)(2,1)} %refs_4_.1) | copy-start | bytes 196612
  52.0 6.3 %collective-permute-start.5 = (bf16[256,128]{1,0:T(8,128)(2,1)S(1)}, bf16[256,128]{1,0:T(8,128)(2,1)S(1)}, u32[]{:S(2)}, u32[]{:S(2)}) collective-permute-start(bf16[256,128]{1,0:T(8,128)(2,1)S(1)} %get-tuple-element.53), channel_id=1, source_target_pairs={{0,32},{32,64},{64,96},{96,0},{128,160},{160,192},{192,224},{224,1... | collective-permute-start | bytes 196616 | tf_op jit(solution)/shard_map/ppermute | solution.py:439
  52.4 6.7 %collective-permute-start.6 = (bf16[256,128]{1,0:T(8,128)(2,1)S(1)}, bf16[256,128]{1,0:T(8,128)(2,1)S(1)}, u32[]{:S(2)}, u32[]{:S(2)}) collective-permute-start(bf16[256,128]{1,0:T(8,128)(2,1)S(1)} %get-tuple-element.54), channel_id=1, source_target_pairs={{0,64},{32,96},{64,0},{96,32},{128,192},{160,224},{192,128},{224,1... | collective-permute-start | bytes 196616 | tf_op jit(solution)/shard_map/ppermute | solution.py:439
  56.1 4.3 %collective-permute-start.7 = (bf16[256,128]{1,0:T(8,128)(2,1)S(1)}, bf16[256,128]{1,0:T(8,128)(2,1)S(1)}, u32[]{:S(2)}, u32[]{:S(2)}) collective-permute-start(bf16[256,128]{1,0:T(8,128)(2,1)S(1)} %get-tuple-element.55), channel_id=1, source_target_pairs={{0,96},{32,0},{64,32},{96,64},{128,224},{160,128},{192,160},{224,1... | collective-permute-start | bytes 196616 | tf_op jit(solution)/shard_map/ppermute | solution.py:439

commit v6 on v5

--- a/solution.py
+++ b/solution.py
@@ -321,25 +321,9 @@
     return inner_sum
 
 
-def correlations(
-    loaded_ref, rows_ref, inner_sum, gated_ref, out_hbm, grad_query_hbm,
-    buf_ref, out_ref, grad_query_ref, sems,
-):
-    grad_query_ref[...] = (gated_ref[...] * inner_sum).reshape(CH, BLOCK).astype(BF16)
-    query_copy = pltpu.make_async_copy(grad_query_ref, grad_query_hbm, sems.at[0])
-    query_copy.start()
-    load(rows_ref, 1, buf_ref, 0)
-    sign = alternate()
-    correlate(buf_ref, loaded_ref, out_ref, sign)
-    copy = pltpu.make_async_copy(out_ref, out_hbm, sems.at[1])
-    copy.start()
-    copy.wait()
-    query_copy.wait()
-
-
 def near_kernel(
     table_ref, rows_ref, kv_ref, query_ref, first_ref, turn_ref, second_ref, loaded_ref, gated_ref,
-    gated_out_ref, inner_sum_ref, out_hbm, grad_query_hbm, *scratch,
+    gated_out_ref, inner_sum_ref, out_ref, grad_query_ref, buf_ref,
 ):
     gate_refs = (
         table_ref, rows_ref, kv_ref, query_ref, first_ref, turn_ref, second_ref, gated_out_ref
@@ -349,9 +333,9 @@
     @pl.when(near)
     def _():
         inner_sum = gate(*gate_refs)
-        correlations(
-            loaded_ref, rows_ref, inner_sum, gated_ref, out_hbm, grad_query_hbm, *scratch
-        )
+        grad_query_ref[...] = (gated_ref[...] * inner_sum).reshape(CH, BLOCK).astype(BF16)
+        load(rows_ref, 1, buf_ref, 0)
+        correlate(buf_ref, loaded_ref, out_ref, alternate())
 
     @pl.when(jnp.logical_not(near))
     def _():
@@ -359,13 +343,35 @@
 
 
 def far_kernel(
-    loaded_ref, rows_ref, inner_sum_ref, gated_ref, _, __, out_hbm, grad_query_hbm, *scratch
+    loaded_ref, rows_ref, inner_sum_ref, gated_ref, near_ref, near_query_ref,
+    out_hbm, grad_query_hbm, buf_ref, out_ref, grad_query_ref, sems,
 ):
-    @pl.when(lax.axis_index("tensor") // RING == 1)
+    near = lax.axis_index("tensor") // RING == 0
+
+    @pl.when(near)
     def _():
-        correlations(
-            loaded_ref, rows_ref, inner_sum_ref[...], gated_ref, out_hbm, grad_query_hbm, *scratch
+        copies = [
+            pltpu.make_async_copy(near_ref, out_hbm, sems.at[0]),
+            pltpu.make_async_copy(near_query_ref, grad_query_hbm, sems.at[1]),
+        ]
+        for copy in copies:
+            copy.start()
+        for copy in copies:
+            copy.wait()
+
+    @pl.when(jnp.logical_not(near))
+    def _():
+        grad_query_ref[...] = (
+            (gated_ref[...] * inner_sum_ref[...]).reshape(CH, BLOCK).astype(BF16)
         )
+        copies = [pltpu.make_async_copy(grad_query_ref, grad_query_hbm, sems.at[0])]
+        copies[0].start()
+        load(rows_ref, 1, buf_ref, 0)
+        correlate(buf_ref, loaded_ref, out_ref, alternate())
+        copies.append(pltpu.make_async_copy(out_ref, out_hbm, sems.at[1]))
+        copies[1].start()
+        for copy in copies:
+            copy.wait()
 
 
 def skip_rows(table_ref):
@@ -409,14 +415,13 @@
         copy.wait()
 
 
-def call(kernel, outs, operands, scratch=(), place=VMEM, limit=48, cost=None, out_place=VMEM, aliases=None):
+def call(kernel, outs, operands, scratch=(), place=VMEM, limit=48, cost=None, out_place=VMEM):
     return pl.pallas_call(
         kernel,
         out_shape=[jax.ShapeDtypeStruct(shape, dtype) for shape, dtype in outs],
         in_specs=place if isinstance(place, list) else [place] * len(operands),
         out_specs=out_place if isinstance(out_place, list) else [out_place] * len(outs),
         scratch_shapes=list(scratch),
-        input_output_aliases=aliases or {},
         cost_estimate=cost,
         compiler_params=pltpu.CompilerParams(vmem_limit_bytes=limit * 1024 * 1024),
     )(*operands)
@@ -496,28 +501,24 @@
         (spec, grad_spec),
     )
     rows = exchange(rows)
-    scratch = [
-        pltpu.VMEM((1, 2, BLOCKS, PIECE, SIDE), F32),
-        pltpu.VMEM(two, BF16),
-        pltpu.VMEM(tokens, BF16),
-        pltpu.SemaphoreType.DMA((2,)),
-    ]
     gated, inner_sum, *begun = call(
         near_kernel,
         [(square_shape, BF16), (square_shape, F32), (two, BF16), (tokens, BF16)],
         (table, rows, key_value, queries, *inverse_tables, loaded, grad_gated),
-        scratch=scratch,
-        out_place=[VMEM, VMEM, ANY, ANY],
+        scratch=[pltpu.VMEM((1, 2, BLOCKS, PIECE, SIDE), F32)],
     )
     far = across(gated)
     corr, grad_queries = call(
         far_kernel,
         [(two, BF16), (tokens, BF16)],
         (loaded, rows, inner_sum, grad_gated, *begun),
-        scratch=scratch,
-        place=[VMEM] * 4 + [ANY] * 2,
+        scratch=[
+            pltpu.VMEM((1, 2, BLOCKS, PIECE, SIDE), F32),
+            pltpu.VMEM(two, BF16),
+            pltpu.VMEM(tokens, BF16),
+            pltpu.SemaphoreType.DMA((2,)),
+        ],
         out_place=ANY,
-        aliases={4: 0, 5: 1},
     )
     corr = exchange(corr)
     mine, *others = call(out_mix_kernel, parts, (table, gated, far), cost=COST)

time: 62.1 us -> 61.6 us (level)
  the two profiles are of different devices: /device:TPU:32 before, /device:TPU:1 now
where the time goes in v6:
time: 61.6 us; the launch traced here: 61.3 us
  starting transfers between devices  31.4 us (51%)
  blocking collectives  15.1 us (25%)
  Pallas kernels  7.06 us (11%)
  waiting for transfers between devices  6.81 us (11%)
  between operations  0.81 us (1%)
    all_to_all x1, blocking collectives, exchange(): lax.all_to_all(blocks, 'seq', split_axis=0, concat_axis=0, tiled=True, ax...  15.1 us
    all_to_all x2, starting transfers between devices, exchange(): lax.all_to_all(blocks, 'seq', split_axis=0, concat_axis=0, tiled=True, ax...  14 us
    ppermute x2, starting transfers between devices, across(): lax.ppermute(array, 'tensor', [(i, (i + RING) % GROUP) for i in range(GRO...  8.84 us
    ppermute x6, starting transfers between devices, along_y(): received.append(lax.ppermute(array, 'tensor', pairs))  8.6 us
    pallas_call x8, Pallas kernels, call(): pl.pallas_call(kernel, out_shape=[jax.ShapeDtypeStruct(shape, dtype) for...  7.06 us
    ppermute x6, waiting for transfers between devices, along_y(): received.append(lax.ppermute(array, 'tensor', pairs))  6.18 us
  transfers between devices with their start and end apart: 10, of which 6 were waited for; matrix products, arithmetic and copies ran while one was open for 0% of the time, Pallas kernels for 2%

profile of v6, /device:TPU:1, one launch (start us, length us, event | category | flops | bytes accessed | tf_op | source)
XLA Modules:
  0.0 61.3 jit_solution(1599360331836671405)
XLA Ops:
  0.6 2.3 %shard_map.146 = (f32[72,128]{1,0:T(8,128)S(1)}, bf16[256,128]{1,0:T(8,128)(2,1)S(1)}, bf16[32,32,128]{2,1,0:T(8,128)(2,1)}) custom-call(bf16[2,16384]{1,0:T(2,128)(2,1)} %refs_3_.1, bf16[2,16384]{1,0:T(2,128)(2,1)} %refs_4_.1, bf16[2,16384]{1,0:T(2,128)(2,1)} %taps_hbm.1, bf16[16,16]{1,0:T(8,128)(2,1)} %weight_hbm.1, f32[2]{0:T(128)} %skip_hbm.1, ...), custom_call_target="tpu_custom_call" | custom-call | tf_op jit(solution)/shard_map/pallas_call | solution.py:419
  3.0 7.8 %collective-permute-start = (bf16[2,16384]{1,0:T(2,128)(2,1)S(1)}, bf16[2,16384]{1,0:T(2,128)(2,1)S(1)}, u32[]{:S(2)}, u32[]{:S(2)}) collective-permute-start(bf16[2,16384]{1,0:T(2,128)(2,1)S(1)} %copy-done.7), channel_id=1, source_target_pairs={{0,128},{32,160},{64,192},{96,224},{128,0},{160,32},{192,64},{224,... | collective-permute-start | bytes 196616 | tf_op jit(solution)/shard_map/ppermute | solution.py:449
  10.8 7.4 %all-to-all-start = ((bf16[32,32,128]{2,1,0:T(8,128)(2,1)}), bf16[32,32,128]{2,1,0:T(8,128)(2,1)S(1)}, u32[]{:S(2)}, u32[]{:S(2)}) async-start(bf16[32,32,128]{2,1,0:T(8,128)(2,1)} %get-tuple-element.35), calls=%async_computation | async-start | bytes 524288 | tf_op jit(solution)/shard_map/all_to_all | solution.py:431
  18.2 0.0 copy-start
  18.2 0.0 copy-start.1
  18.2 0.0 copy-start.4
  18.2 0.0 copy-start.5
  18.2 0.2 shard_map.147
  18.4 1.4 %collective-permute-start.1 = (bf16[256,128]{1,0:T(8,128)(2,1)S(1)}, bf16[256,128]{1,0:T(8,128)(2,1)S(1)}, u32[]{:S(2)}, u32[]{:S(2)}) collective-permute-start(bf16[256,128]{1,0:T(8,128)(2,1)S(1)} %get-tuple-element.38), channel_id=1, source_target_pairs={{0,32},{32,64},{64,96},{96,0},{128,160},{160,192},{192,224},{224,1... | collective-permute-start | bytes 196616 | tf_op jit(solution)/shard_map/ppermute | solution.py:444
  19.7 2.6 %collective-permute-start.2 = (bf16[256,128]{1,0:T(8,128)(2,1)S(1)}, bf16[256,128]{1,0:T(8,128)(2,1)S(1)}, u32[]{:S(2)}, u32[]{:S(2)}) collective-permute-start(bf16[256,128]{1,0:T(8,128)(2,1)S(1)} %get-tuple-element.39), channel_id=1, source_target_pairs={{0,64},{32,96},{64,0},{96,32},{128,192},{160,224},{192,128},{224,1... | collective-permute-start | bytes 196616 | tf_op jit(solution)/shard_map/ppermute | solution.py:444
  22.4 1.1 %collective-permute-start.3 = (bf16[256,128]{1,0:T(8,128)(2,1)S(1)}, bf16[256,128]{1,0:T(8,128)(2,1)S(1)}, u32[]{:S(2)}, u32[]{:S(2)}) collective-permute-start(bf16[256,128]{1,0:T(8,128)(2,1)S(1)} %get-tuple-element.40), channel_id=1, source_target_pairs={{0,96},{32,0},{64,32},{96,64},{128,224},{160,128},{192,160},{224,1... | collective-permute-start | bytes 196616 | tf_op jit(solution)/shard_map/ppermute | solution.py:444
  23.4 0.0 collective-permute-done.1.r1_ref
  23.4 2.2 %collective-permute-done.2.r2_ref = bf16[256,128]{1,0:T(8,128)(2,1)S(1)} collective-permute-done((bf16[256,128]{1,0:T(8,128)(2,1)S(1)}, bf16[256,128]{1,0:T(8,128)(2,1)S(1)}, u32[]{:S(2)}, u32[]{:S(2)}) %collective-permute-start.2) | collective-permute-done | bytes 65568 | tf_op jit(solution)/shard_map/ppermute | solution.py:444
  25.7 0.1 collective-permute-done.3.r3_ref
  25.8 0.4 shard_map.148
  26.2 0.5 shard_map.149
  26.7 0.0 copy-start.6
  26.8 15.1 %all_to_all.15.rows_ref = bf16[32,32,128]{2,1,0:T(8,128)(2,1)S(1)} all-to-all(bf16[32,32,128]{2,1,0:T(8,128)(2,1)S(1)} %get-tuple-element.43), channel_id=1, replica_groups={{19,23,29,26,5,17,30,10,25,16,0,3,4,14,22,6,24,8,13,21,18,27,15,31,20,1..., dimensions={0} | all-to-all | bytes 524288 | tf_op jit(solution)/shard_map/all_to_all | solution.py:431
  41.9 1.4 %shard_map.150 = (bf16[256,128]{1,0:T(8,128)(2,1)S(1)}, f32[256,128]{1,0:T(8,128)S(1)}, bf16[32,32,128]{2,1,0:T(8,128)(2,1)S(1)}, bf16[2,16384]{1,0:T(2,128)(2,1)S(1)}) custom-call(f32[72,128]{1,0:T(8,128)S(1)} %get-tuple-element.33.table_ref.refs_0_, bf16[32,32,128]{2,1,0:T(8,128)(2,1)S(1)} %all_to_all.15.rows_ref, ...), custom_call_target="tpu_custom_call" | custom-call | tf_op jit(solution)/shard_map/pallas_call | solution.py:419
  43.3 1.0 %collective-permute-start.4 = (bf16[256,128]{1,0:T(8,128)(2,1)S(1)}, bf16[256,128]{1,0:T(8,128)(2,1)S(1)}, u32[]{:S(2)}, u32[]{:S(2)}) collective-permute-start(bf16[256,128]{1,0:T(8,128)(2,1)S(1)} %get-tuple-element.51.near_ref), channel_id=1, source_target_pairs={{0,128},{32,160},{64,192},{96,224},{128,0},{160,32},{192,64},{224,... | collective-permute-start | bytes 196616 | tf_op jit(solution)/shard_map/ppermute | solution.py:449
  44.3 0.7 %shard_map.151 = (bf16[32,32,128]{2,1,0:T(8,128)(2,1)}, bf16[2,16384]{1,0:T(2,128)(2,1)}) custom-call(f32[2,2,32,8,128]{4,3,2,1,0:T(8,128)S(1)} %get-tuple-element.42.loaded_ref, bf16[32,32,128]{2,1,0:T(8,128)(2,1)S(1)} %all_to_all.15.rows_ref, f32[256,128]{1,0:T(8,128)S(1)} %get-tuple-element.46.inner_sum_ref, f32[256,128]{1,0:T(8,128)S(1)} %get-tuple-element.45.gated_ref, ...), custom_call_target="tpu_custom_call" | custom-call | tf_op jit(solution)/shard_map/pallas_call | solution.py:419
  45.0 6.6 %all-to-all-start.2 = ((bf16[32,32,128]{2,1,0:T(8,128)(2,1)}), bf16[32,32,128]{2,1,0:T(8,128)(2,1)S(1)}, u32[]{:S(2)}, u32[]{:S(2)}) async-start(bf16[32,32,128]{2,1,0:T(8,128)(2,1)} %get-tuple-element.49), calls=%async_computation.2 | async-start | bytes 524288 | tf_op jit(solution)/shard_map/all_to_all | solution.py:431
  51.7 0.0 copy-start.2
  51.7 0.0 copy-start.3
  51.7 0.1 shard_map.152
  51.9 0.1 collective-permute-start.5
  52.0 3.4 %collective-permute-start.6 = (bf16[256,128]{1,0:T(8,128)(2,1)S(1)}, bf16[256,128]{1,0:T(8,128)(2,1)S(1)}, u32[]{:S(2)}, u32[]{:S(2)}) collective-permute-start(bf16[256,128]{1,0:T(8,128)(2,1)S(1)} %get-tuple-element.54), channel_id=1, source_target_pairs={{0,64},{32,96},{64,0},{96,32},{128,192},{160,224},{192,128},{224,1... | collective-permute-start | bytes 196616 | tf_op jit(solution)/shard_map/ppermute | solution.py:444
  55.4 1.2 %collective-permute-done.5.refs_9_ = bf16[256,128]{1,0:T(8,128)(2,1)S(1)} collective-permute-done((bf16[256,128]{1,0:T(8,128)(2,1)S(1)}, bf16[256,128]{1,0:T(8,128)(2,1)S(1)}, u32[]{:S(2)}, u32[]{:S(2)}) %collective-permute-start.5) | collective-permute-done | bytes 65568 | tf_op jit(solution)/shard_map/ppermute | solution.py:444
  56.6 1.7 %collective-permute-done.6.refs_10_ = bf16[256,128]{1,0:T(8,128)(2,1)S(1)} collective-permute-done((bf16[256,128]{1,0:T(8,128)(2,1)S(1)}, bf16[256,128]{1,0:T(8,128)(2,1)S(1)}, u32[]{:S(2)}, u32[]{:S(2)}) %collective-permute-start.6) | collective-permute-done | bytes 65568 | tf_op jit(solution)/shard_map/ppermute | solution.py:444
  58.3 1.0 %collective-permute-done.7.refs_11_ = bf16[256,128]{1,0:T(8,128)(2,1)S(1)} collective-permute-done((bf16[256,128]{1,0:T(8,128)(2,1)S(1)}, bf16[256,128]{1,0:T(8,128)(2,1)S(1)}, u32[]{:S(2)}, u32[]{:S(2)}) %collective-permute-start.7) | collective-permute-done | bytes 65568 | tf_op jit(solution)/shard_map/ppermute | solution.py:444
  59.3 0.6 %all-to-all-done.2.refs_1_ = bf16[32,32,128]{2,1,0:T(8,128)(2,1)S(1)} async-done(((bf16[32,32,128]{2,1,0:T(8,128)(2,1)}), bf16[32,32,128]{2,1,0:T(8,128)(2,1)S(1)}, u32[]{:S(2)}, u32[]{:S(2)}) %all-to-all-start.2) | async-done | bytes 262176 | tf_op jit(solution)/shard_map/all_to_all | solution.py:431
  59.9 1.4 %shard_map.153 = (bf16[2,16384]{1,0:T(2,128)(2,1)}, bf16[2,16384]{1,0:T(2,128)(2,1)}, bf16[2,16384]{1,0:T(2,128)(2,1)}, f32[2,16384]{1,0:T(2,128)}) custom-call(f32[72,128]{1,0:T(8,128)S(1)} %get-tuple-element.33.table_ref.refs_0_, bf16[32,32,128]{2,1,0:T(8,128)(2,1)S(1)} %all-to-all-done.2.refs_1_, bf16[256,128]{1,0:T(8,128)(2,1)S(1)} %get-tuple-element.50.refs_2_, ...), custom_call_target="tpu_custom_call" | custom-call | tf_op jit(solution)/shard_map/pallas_call | solution.py:419
  (13 shorter events, 0.0 us)
Async XLA Ops:
  0.6 2.3 %copy-start.7 = (bf16[2,16384]{1,0:T(2,128)(2,1)S(1)}, bf16[2,16384]{1,0:T(2,128)(2,1)}, u32[]{:S(2)}) copy-start(bf16[2,16384]{1,0:T(2,128)(2,1)} %near_ref.1) | copy-start | bytes 196612
  3.0 15.2 %collective-permute-start = (bf16[2,16384]{1,0:T(2,128)(2,1)S(1)}, bf16[2,16384]{1,0:T(2,128)(2,1)S(1)}, u32[]{:S(2)}, u32[]{:S(2)}) collective-permute-start(bf16[2,16384]{1,0:T(2,128)(2,1)S(1)} %copy-done.7), channel_id=1, source_target_pairs={{0,128},{32,160},{64,192},{96,224},{128,0},{160,32},{192,64},{224,... | collective-permute-start | bytes 196616 | tf_op jit(solution)/shard_map/ppermute | solution.py:449
  10.8 15.4 %all-to-all-start = ((bf16[32,32,128]{2,1,0:T(8,128)(2,1)}), bf16[32,32,128]{2,1,0:T(8,128)(2,1)S(1)}, u32[]{:S(2)}, u32[]{:S(2)}) async-start(bf16[32,32,128]{2,1,0:T(8,128)(2,1)} %get-tuple-element.35), calls=%async_computation | async-start | bytes 524288 | tf_op jit(solution)/shard_map/all_to_all | solution.py:431
  18.2 7.6 %copy-start = (f32[2,128,128]{2,1,0:T(8,128)S(1)}, f32[2,128,128]{2,1,0:T(8,128)}, u32[]{:S(2)}) copy-start(f32[2,128,128]{2,1,0:T(8,128)} %constant.10.clone.turn_hbm.turn_ref.refs_6_) | copy-start | bytes 393220
  18.2 7.6 %copy-start.1 = (bf16[2,128,128]{2,1,0:T(8,128)(2,1)S(1)}, bf16[2,128,128]{2,1,0:T(8,128)(2,1)}, u32[]{:S(2)}) copy-start(bf16[2,128,128]{2,1,0:T(8,128)(2,1)} %constant.11.clone.second_hbm.second_ref.refs_7_) | copy-start | bytes 196612
  18.2 7.6 %copy-start.4 = (bf16[256,128]{1,0:T(8,128)(2,1)S(1)}, bf16[256,128]{1,0:T(8,128)(2,1)}, u32[]{:S(2)}) copy-start(bf16[256,128]{1,0:T(8,128)(2,1)} %constant.8.clone.first_hbm.first_ref) | copy-start | bytes 196612
  18.2 7.6 %copy-start.5 = (bf16[2,16384]{1,0:T(2,128)(2,1)S(1)}, bf16[2,16384]{1,0:T(2,128)(2,1)}, u32[]{:S(2)}) copy-start(bf16[2,16384]{1,0:T(2,128)(2,1)} %query_ref.3) | copy-start | bytes 196612
  18.4 5.1 %collective-permute-start.1 = (bf16[256,128]{1,0:T(8,128)(2,1)S(1)}, bf16[256,128]{1,0:T(8,128)(2,1)S(1)}, u32[]{:S(2)}, u32[]{:S(2)}) collective-permute-start(bf16[256,128]{1,0:T(8,128)(2,1)S(1)} %get-tuple-element.38), channel_id=1, source_target_pairs={{0,32},{32,64},{64,96},{96,0},{128,160},{160,192},{192,224},{224,1... | collective-permute-start | bytes 196616 | tf_op jit(solution)/shard_map/ppermute | solution.py:444
  19.7 5.9 %collective-permute-start.2 = (bf16[256,128]{1,0:T(8,128)(2,1)S(1)}, bf16[256,128]{1,0:T(8,128)(2,1)S(1)}, u32[]{:S(2)}, u32[]{:S(2)}) collective-permute-start(bf16[256,128]{1,0:T(8,128)(2,1)S(1)} %get-tuple-element.39), channel_id=1, source_target_pairs={{0,64},{32,96},{64,0},{96,32},{128,192},{160,224},{192,128},{224,1... | collective-permute-start | bytes 196616 | tf_op jit(solution)/shard_map/ppermute | solution.py:444
  22.4 3.4 %collective-permute-start.3 = (bf16[256,128]{1,0:T(8,128)(2,1)S(1)}, bf16[256,128]{1,0:T(8,128)(2,1)S(1)}, u32[]{:S(2)}, u32[]{:S(2)}) collective-permute-start(bf16[256,128]{1,0:T(8,128)(2,1)S(1)} %get-tuple-element.40), channel_id=1, source_target_pairs={{0,96},{32,0},{64,32},{96,64},{128,224},{160,128},{192,160},{224,1... | collective-permute-start | bytes 196616 | tf_op jit(solution)/shard_map/ppermute | solution.py:444
  26.7 15.1 %copy-start.6 = (bf16[128,256]{1,0:T(8,128)(2,1)S(1)}, bf16[128,256]{1,0:T(8,128)(2,1)}, u32[]{:S(2)}) copy-start(bf16[128,256]{1,0:T(8,128)(2,1)} %constant.9.clone.first_ref.refs_5_) | copy-start | bytes 196612
  43.3 8.4 %collective-permute-start.4 = (bf16[256,128]{1,0:T(8,128)(2,1)S(1)}, bf16[256,128]{1,0:T(8,128)(2,1)S(1)}, u32[]{:S(2)}, u32[]{:S(2)}) collective-permute-start(bf16[256,128]{1,0:T(8,128)(2,1)S(1)} %get-tuple-element.51.near_ref), channel_id=1, source_target_pairs={{0,128},{32,160},{64,192},{96,224},{128,0},{160,32},{192,64},{224,... | collective-permute-start | bytes 196616 | tf_op jit(solution)/shard_map/ppermute | solution.py:449
  45.0 14.8 %all-to-all-start.2 = ((bf16[32,32,128]{2,1,0:T(8,128)(2,1)}), bf16[32,32,128]{2,1,0:T(8,128)(2,1)S(1)}, u32[]{:S(2)}, u32[]{:S(2)}) async-start(bf16[32,32,128]{2,1,0:T(8,128)(2,1)} %get-tuple-element.49), calls=%async_computation.2 | async-start | bytes 524288 | tf_op jit(solution)/shard_map/all_to_all | solution.py:431
  51.7 8.2 %copy-start.2 = (bf16[2,16384]{1,0:T(2,128)(2,1)S(1)}, bf16[2,16384]{1,0:T(2,128)(2,1)}, u32[]{:S(2)}) copy-start(bf16[2,16384]{1,0:T(2,128)(2,1)} %refs_3_.1) | copy-start | bytes 196612
  51.7 8.2 %copy-start.3 = (bf16[2,16384]{1,0:T(2,128)(2,1)S(1)}, bf16[2,16384]{1,0:T(2,128)(2,1)}, u32[]{:S(2)}) copy-start(bf16[2,16384]{1,0:T(2,128)(2,1)} %refs_4_.1) | copy-start | bytes 196612
  51.9 4.7 %collective-permute-start.5 = (bf16[256,128]{1,0:T(8,128)(2,1)S(1)}, bf16[256,128]{1,0:T(8,128)(2,1)S(1)}, u32[]{:S(2)}, u32[]{:S(2)}) collective-permute-start(bf16[256,128]{1,0:T(8,128)(2,1)S(1)} %get-tuple-element.53), channel_id=1, source_target_pairs={{0,32},{32,64},{64,96},{96,0},{128,160},{160,192},{192,224},{224,1... | collective-permute-start | bytes 196616 | tf_op jit(solution)/shard_map/ppermute | solution.py:444
  52.0 6.3 %collective-permute-start.6 = (bf16[256,128]{1,0:T(8,128)(2,1)S(1)}, bf16[256,128]{1,0:T(8,128)(2,1)S(1)}, u32[]{:S(2)}, u32[]{:S(2)}) collective-permute-start(bf16[256,128]{1,0:T(8,128)(2,1)S(1)} %get-tuple-element.54), channel_id=1, source_target_pairs={{0,64},{32,96},{64,0},{96,32},{128,192},{160,224},{192,128},{224,1... | collective-permute-start | bytes 196616 | tf_op jit(solution)/shard_map/ppermute | solution.py:444
  55.4 3.8 %collective-permute-start.7 = (bf16[256,128]{1,0:T(8,128)(2,1)S(1)}, bf16[256,128]{1,0:T(8,128)(2,1)S(1)}, u32[]{:S(2)}, u32[]{:S(2)}) collective-permute-start(bf16[256,128]{1,0:T(8,128)(2,1)S(1)} %get-tuple-element.55), channel_id=1, source_target_pairs={{0,96},{32,0},{64,32},{96,64},{128,224},{160,128},{192,160},{224,1... | collective-permute-start | bytes 196616 | tf_op jit(solution)/shard_map/ppermute | solution.py:444

commit v7 on v6

--- a/solution.py
+++ b/solution.py
@@ -300,11 +300,13 @@
 
 def grad_kernel(
     mine_ref, r1_ref, r2_ref, r3_ref, query_ref, first_ref, turn_ref, second_ref,
-    gated_ref, inner_ref, out_ref,
+    gated_ref, inner_ref, square_ref, out_ref,
 ):
     grad_gated = total_of(mine_ref, (r1_ref, r2_ref, r3_ref))
     gated_ref[...] = grad_gated
-    grad_inner = (grad_gated * square(query_ref)).astype(BF16)
+    query = square(query_ref)
+    square_ref[...] = query
+    grad_inner = (grad_gated * query).astype(BF16)
     inner_ref[...] = grad_inner
     stages = first_stage([grad_inner], first_ref[...])
     out_ref[...] = last_stage(stages, turn_ref[...], second_stage(second_ref[...], -1))
@@ -317,7 +319,7 @@
         jnp.concatenate(parts, axis=1), 1, first_ref[...], turn_ref[...], second_ref[...]
     )
     inner_sum = convolved + skip_rows(table_ref) * kv_ref[...].astype(F32)
-    out_ref[...] = (square(query_ref) * inner_sum).astype(BF16)
+    out_ref[...] = (query_ref[...] * inner_sum).astype(BF16)
     return inner_sum
 
 
@@ -490,9 +492,9 @@
         cost=COST,
     )
     others = along_y(others)
-    grad_gated, grad_inner, grad_spec = call(
+    grad_gated, grad_inner, query, grad_spec = call(
         grad_kernel,
-        [(square_shape, F32), (square_shape, BF16), (one, BF16)],
+        [(square_shape, F32), (square_shape, BF16), (square_shape, F32), (one, BF16)],
         (mine, *others, queries, *forward_tables),
     )
     rows, loaded = call(
@@ -504,7 +506,7 @@
     gated, inner_sum, *begun = call(
         near_kernel,
         [(square_shape, BF16), (square_shape, F32), (two, BF16), (tokens, BF16)],
-        (table, rows, key_value, queries, *inverse_tables, loaded, grad_gated),
+        (table, rows, key_value, query, *inverse_tables, loaded, grad_gated),
         scratch=[pltpu.VMEM((1, 2, BLOCKS, PIECE, SIDE), F32)],
     )
     far = across(gated)

time: 61.6 us -> 61.6 us (level)
  no operation moved by 1% of the time
where the time goes in v7:
time: 61.6 us; the launch traced here: 61.3 us
  starting transfers between devices  31.5 us (51%)
  blocking collectives  15.1 us (25%)
  Pallas kernels  7.04 us (11%)
  waiting for transfers between devices  6.8 us (11%)
  between operations  0.81 us (1%)
    all_to_all x1, blocking collectives, exchange(): lax.all_to_all(blocks, 'seq', split_axis=0, concat_axis=0, tiled=True, ax...  15.1 us
    all_to_all x2, starting transfers between devices, exchange(): lax.all_to_all(blocks, 'seq', split_axis=0, concat_axis=0, tiled=True, ax...  14 us
    ppermute x2, starting transfers between devices, across(): lax.ppermute(array, 'tensor', [(i, (i + RING) % GROUP) for i in range(GRO...  8.86 us
    ppermute x6, starting transfers between devices, along_y(): received.append(lax.ppermute(array, 'tensor', pairs))  8.6 us
    pallas_call x8, Pallas kernels, call(): pl.pallas_call(kernel, out_shape=[jax.ShapeDtypeStruct(shape, dtype) for...  7.04 us
    ppermute x6, waiting for transfers between devices, along_y(): received.append(lax.ppermute(array, 'tensor', pairs))  6.19 us
  transfers between devices with their start and end apart: 10, of which 6 were waited for; matrix products, arithmetic and copies ran while one was open for 0% of the time, Pallas kernels for 2%

profile of v7, /device:TPU:1, one launch (start us, length us, event | category | flops | bytes accessed | tf_op | source)
XLA Modules:
  0.0 61.3 jit_solution(7197034301848484390)
XLA Ops:
  0.6 2.3 %shard_map.146 = (f32[72,128]{1,0:T(8,128)S(1)}, bf16[256,128]{1,0:T(8,128)(2,1)S(1)}, bf16[32,32,128]{2,1,0:T(8,128)(2,1)}) custom-call(bf16[2,16384]{1,0:T(2,128)(2,1)} %refs_3_.1, bf16[2,16384]{1,0:T(2,128)(2,1)} %refs_4_.1, bf16[2,16384]{1,0:T(2,128)(2,1)} %taps_hbm.1, bf16[16,16]{1,0:T(8,128)(2,1)} %weight_hbm.1, f32[2]{0:T(128)} %skip_hbm.1, ...), custom_call_target="tpu_custom_call" | custom-call | tf_op jit(solution)/shard_map/pallas_call | solution.py:421
  3.0 7.8 %collective-permute-start = (bf16[2,16384]{1,0:T(2,128)(2,1)S(1)}, bf16[2,16384]{1,0:T(2,128)(2,1)S(1)}, u32[]{:S(2)}, u32[]{:S(2)}) collective-permute-start(bf16[2,16384]{1,0:T(2,128)(2,1)S(1)} %copy-done.7), channel_id=1, source_target_pairs={{0,128},{32,160},{64,192},{96,224},{128,0},{160,32},{192,64},{224,... | collective-permute-start | bytes 196616 | tf_op jit(solution)/shard_map/ppermute | solution.py:451
  10.8 7.4 %all-to-all-start = ((bf16[32,32,128]{2,1,0:T(8,128)(2,1)}), bf16[32,32,128]{2,1,0:T(8,128)(2,1)S(1)}, u32[]{:S(2)}, u32[]{:S(2)}) async-start(bf16[32,32,128]{2,1,0:T(8,128)(2,1)} %get-tuple-element.36), calls=%async_computation | async-start | bytes 524288 | tf_op jit(solution)/shard_map/all_to_all | solution.py:433
  18.2 0.0 copy-start
  18.2 0.0 copy-start.1
  18.2 0.0 copy-start.5
  18.2 0.0 copy-start.6
  18.2 0.2 shard_map.147
  18.4 1.4 %collective-permute-start.1 = (bf16[256,128]{1,0:T(8,128)(2,1)S(1)}, bf16[256,128]{1,0:T(8,128)(2,1)S(1)}, u32[]{:S(2)}, u32[]{:S(2)}) collective-permute-start(bf16[256,128]{1,0:T(8,128)(2,1)S(1)} %get-tuple-element.39), channel_id=1, source_target_pairs={{0,32},{32,64},{64,96},{96,0},{128,160},{160,192},{192,224},{224,1... | collective-permute-start | bytes 196616 | tf_op jit(solution)/shard_map/ppermute | solution.py:446
  19.7 2.6 %collective-permute-start.2 = (bf16[256,128]{1,0:T(8,128)(2,1)S(1)}, bf16[256,128]{1,0:T(8,128)(2,1)S(1)}, u32[]{:S(2)}, u32[]{:S(2)}) collective-permute-start(bf16[256,128]{1,0:T(8,128)(2,1)S(1)} %get-tuple-element.40), channel_id=1, source_target_pairs={{0,64},{32,96},{64,0},{96,32},{128,192},{160,224},{192,128},{224,1... | collective-permute-start | bytes 196616 | tf_op jit(solution)/shard_map/ppermute | solution.py:446
  22.4 1.1 %collective-permute-start.3 = (bf16[256,128]{1,0:T(8,128)(2,1)S(1)}, bf16[256,128]{1,0:T(8,128)(2,1)S(1)}, u32[]{:S(2)}, u32[]{:S(2)}) collective-permute-start(bf16[256,128]{1,0:T(8,128)(2,1)S(1)} %get-tuple-element.41), channel_id=1, source_target_pairs={{0,96},{32,0},{64,32},{96,64},{128,224},{160,128},{192,160},{224,1... | collective-permute-start | bytes 196616 | tf_op jit(solution)/shard_map/ppermute | solution.py:446
  23.4 0.0 collective-permute-done.1.r1_ref
  23.4 2.2 %collective-permute-done.2.r2_ref = bf16[256,128]{1,0:T(8,128)(2,1)S(1)} collective-permute-done((bf16[256,128]{1,0:T(8,128)(2,1)S(1)}, bf16[256,128]{1,0:T(8,128)(2,1)S(1)}, u32[]{:S(2)}, u32[]{:S(2)}) %collective-permute-start.2) | collective-permute-done | bytes 65568 | tf_op jit(solution)/shard_map/ppermute | solution.py:446
  25.7 0.1 collective-permute-done.3.r3_ref
  25.8 0.4 shard_map.148
  26.2 0.5 shard_map.149
  26.7 0.0 copy-start.2
  26.8 15.1 %all_to_all.15.rows_ref = bf16[32,32,128]{2,1,0:T(8,128)(2,1)S(1)} all-to-all(bf16[32,32,128]{2,1,0:T(8,128)(2,1)S(1)} %get-tuple-element.44), channel_id=1, replica_groups={{19,23,29,26,5,17,30,10,25,16,0,3,4,14,22,6,24,8,13,21,18,27,15,31,20,1..., dimensions={0} | all-to-all | bytes 524288 | tf_op jit(solution)/shard_map/all_to_all | solution.py:433
  41.9 1.4 %shard_map.150 = (bf16[256,128]{1,0:T(8,128)(2,1)S(1)}, f32[256,128]{1,0:T(8,128)S(1)}, bf16[32,32,128]{2,1,0:T(8,128)(2,1)S(1)}, bf16[2,16384]{1,0:T(2,128)(2,1)S(1)}) custom-call(f32[72,128]{1,0:T(8,128)S(1)} %get-tuple-element.34.table_ref.refs_0_, bf16[32,32,128]{2,1,0:T(8,128)(2,1)S(1)} %all_to_all.15.rows_ref, ...), custom_call_target="tpu_custom_call" | custom-call | tf_op jit(solution)/shard_map/pallas_call | solution.py:421
  43.3 1.0 %collective-permute-start.4 = (bf16[256,128]{1,0:T(8,128)(2,1)S(1)}, bf16[256,128]{1,0:T(8,128)(2,1)S(1)}, u32[]{:S(2)}, u32[]{:S(2)}) collective-permute-start(bf16[256,128]{1,0:T(8,128)(2,1)S(1)} %get-tuple-element.53.near_ref), channel_id=1, source_target_pairs={{0,128},{32,160},{64,192},{96,224},{128,0},{160,32},{192,64},{224,... | collective-permute-start | bytes 196616 | tf_op jit(solution)/shard_map/ppermute | solution.py:451
  44.3 0.7 %shard_map.151 = (bf16[32,32,128]{2,1,0:T(8,128)(2,1)}, bf16[2,16384]{1,0:T(2,128)(2,1)}) custom-call(f32[2,2,32,8,128]{4,3,2,1,0:T(8,128)S(1)} %get-tuple-element.43.loaded_ref, bf16[32,32,128]{2,1,0:T(8,128)(2,1)S(1)} %all_to_all.15.rows_ref, f32[256,128]{1,0:T(8,128)S(1)} %get-tuple-element.48.inner_sum_ref, f32[256,128]{1,0:T(8,128)S(1)} %get-tuple-element.47.gated_ref, ...), custom_call_target="tpu_custom_call" | custom-call | tf_op jit(solution)/shard_map/pallas_call | solution.py:421
  45.0 6.6 %all-to-all-start.2 = ((bf16[32,32,128]{2,1,0:T(8,128)(2,1)}), bf16[32,32,128]{2,1,0:T(8,128)(2,1)S(1)}, u32[]{:S(2)}, u32[]{:S(2)}) async-start(bf16[32,32,128]{2,1,0:T(8,128)(2,1)} %get-tuple-element.51), calls=%async_computation.2 | async-start | bytes 524288 | tf_op jit(solution)/shard_map/all_to_all | solution.py:433
  51.7 0.0 copy-start.3
  51.7 0.0 copy-start.4
  51.7 0.1 shard_map.152
  51.9 0.1 collective-permute-start.5
  52.0 3.4 %collective-permute-start.6 = (bf16[256,128]{1,0:T(8,128)(2,1)S(1)}, bf16[256,128]{1,0:T(8,128)(2,1)S(1)}, u32[]{:S(2)}, u32[]{:S(2)}) collective-permute-start(bf16[256,128]{1,0:T(8,128)(2,1)S(1)} %get-tuple-element.56), channel_id=1, source_target_pairs={{0,64},{32,96},{64,0},{96,32},{128,192},{160,224},{192,128},{224,1... | collective-permute-start | bytes 196616 | tf_op jit(solution)/shard_map/ppermute | solution.py:446
  55.4 1.2 %collective-permute-done.5.refs_9_ = bf16[256,128]{1,0:T(8,128)(2,1)S(1)} collective-permute-done((bf16[256,128]{1,0:T(8,128)(2,1)S(1)}, bf16[256,128]{1,0:T(8,128)(2,1)S(1)}, u32[]{:S(2)}, u32[]{:S(2)}) %collective-permute-start.5) | collective-permute-done | bytes 65568 | tf_op jit(solution)/shard_map/ppermute | solution.py:446
  56.6 1.7 %collective-permute-done.6.refs_10_ = bf16[256,128]{1,0:T(8,128)(2,1)S(1)} collective-permute-done((bf16[256,128]{1,0:T(8,128)(2,1)S(1)}, bf16[256,128]{1,0:T(8,128)(2,1)S(1)}, u32[]{:S(2)}, u32[]{:S(2)}) %collective-permute-start.6) | collective-permute-done | bytes 65568 | tf_op jit(solution)/shard_map/ppermute | solution.py:446
  58.3 1.0 %collective-permute-done.7.refs_11_ = bf16[256,128]{1,0:T(8,128)(2,1)S(1)} collective-permute-done((bf16[256,128]{1,0:T(8,128)(2,1)S(1)}, bf16[256,128]{1,0:T(8,128)(2,1)S(1)}, u32[]{:S(2)}, u32[]{:S(2)}) %collective-permute-start.7) | collective-permute-done | bytes 65568 | tf_op jit(solution)/shard_map/ppermute | solution.py:446
  59.3 0.6 all-to-all-done.2.refs_1_
  59.9 1.4 %shard_map.153 = (bf16[2,16384]{1,0:T(2,128)(2,1)}, bf16[2,16384]{1,0:T(2,128)(2,1)}, bf16[2,16384]{1,0:T(2,128)(2,1)}, f32[2,16384]{1,0:T(2,128)}) custom-call(f32[72,128]{1,0:T(8,128)S(1)} %get-tuple-element.34.table_ref.refs_0_, bf16[32,32,128]{2,1,0:T(8,128)(2,1)S(1)} %all-to-all-done.2.refs_1_, bf16[256,128]{1,0:T(8,128)(2,1)S(1)} %get-tuple-element.52.refs_2_, ...), custom_call_target="tpu_custom_call" | custom-call | tf_op jit(solution)/shard_map/pallas_call | solution.py:421
  (13 shorter events, 0.0 us)
Async XLA Ops:
  0.6 2.3 %copy-start.7 = (bf16[2,16384]{1,0:T(2,128)(2,1)S(1)}, bf16[2,16384]{1,0:T(2,128)(2,1)}, u32[]{:S(2)}) copy-start(bf16[2,16384]{1,0:T(2,128)(2,1)} %near_ref.1) | copy-start | bytes 196612
  3.0 15.2 %collective-permute-start = (bf16[2,16384]{1,0:T(2,128)(2,1)S(1)}, bf16[2,16384]{1,0:T(2,128)(2,1)S(1)}, u32[]{:S(2)}, u32[]{:S(2)}) collective-permute-start(bf16[2,16384]{1,0:T(2,128)(2,1)S(1)} %copy-done.7), channel_id=1, source_target_pairs={{0,128},{32,160},{64,192},{96,224},{128,0},{160,32},{192,64},{224,... | collective-permute-start | bytes 196616 | tf_op jit(solution)/shard_map/ppermute | solution.py:451
  10.8 15.4 %all-to-all-start = ((bf16[32,32,128]{2,1,0:T(8,128)(2,1)}), bf16[32,32,128]{2,1,0:T(8,128)(2,1)S(1)}, u32[]{:S(2)}, u32[]{:S(2)}) async-start(bf16[32,32,128]{2,1,0:T(8,128)(2,1)} %get-tuple-element.36), calls=%async_computation | async-start | bytes 524288 | tf_op jit(solution)/shard_map/all_to_all | solution.py:433
  18.2 7.6 %copy-start = (f32[2,128,128]{2,1,0:T(8,128)S(1)}, f32[2,128,128]{2,1,0:T(8,128)}, u32[]{:S(2)}) copy-start(f32[2,128,128]{2,1,0:T(8,128)} %constant.10.clone.turn_hbm.turn_ref.refs_6_) | copy-start | bytes 393220
  18.2 7.6 %copy-start.1 = (bf16[2,128,128]{2,1,0:T(8,128)(2,1)S(1)}, bf16[2,128,128]{2,1,0:T(8,128)(2,1)}, u32[]{:S(2)}) copy-start(bf16[2,128,128]{2,1,0:T(8,128)(2,1)} %constant.11.clone.second_hbm.second_ref.refs_7_) | copy-start | bytes 196612
  18.2 7.6 %copy-start.5 = (bf16[256,128]{1,0:T(8,128)(2,1)S(1)}, bf16[256,128]{1,0:T(8,128)(2,1)}, u32[]{:S(2)}) copy-start(bf16[256,128]{1,0:T(8,128)(2,1)} %constant.8.clone.first_hbm.first_ref) | copy-start | bytes 196612
  18.2 7.6 %copy-start.6 = (bf16[2,16384]{1,0:T(2,128)(2,1)S(1)}, bf16[2,16384]{1,0:T(2,128)(2,1)}, u32[]{:S(2)}) copy-start(bf16[2,16384]{1,0:T(2,128)(2,1)} %query_ref.1) | copy-start | bytes 196612
  18.4 5.1 %collective-permute-start.1 = (bf16[256,128]{1,0:T(8,128)(2,1)S(1)}, bf16[256,128]{1,0:T(8,128)(2,1)S(1)}, u32[]{:S(2)}, u32[]{:S(2)}) collective-permute-start(bf16[256,128]{1,0:T(8,128)(2,1)S(1)} %get-tuple-element.39), channel_id=1, source_target_pairs={{0,32},{32,64},{64,96},{96,0},{128,160},{160,192},{192,224},{224,1... | collective-permute-start | bytes 196616 | tf_op jit(solution)/shard_map/ppermute | solution.py:446
  19.7 5.9 %collective-permute-start.2 = (bf16[256,128]{1,0:T(8,128)(2,1)S(1)}, bf16[256,128]{1,0:T(8,128)(2,1)S(1)}, u32[]{:S(2)}, u32[]{:S(2)}) collective-permute-start(bf16[256,128]{1,0:T(8,128)(2,1)S(1)} %get-tuple-element.40), channel_id=1, source_target_pairs={{0,64},{32,96},{64,0},{96,32},{128,192},{160,224},{192,128},{224,1... | collective-permute-start | bytes 196616 | tf_op jit(solution)/shard_map/ppermute | solution.py:446
  22.4 3.4 %collective-permute-start.3 = (bf16[256,128]{1,0:T(8,128)(2,1)S(1)}, bf16[256,128]{1,0:T(8,128)(2,1)S(1)}, u32[]{:S(2)}, u32[]{:S(2)}) collective-permute-start(bf16[256,128]{1,0:T(8,128)(2,1)S(1)} %get-tuple-element.41), channel_id=1, source_target_pairs={{0,96},{32,0},{64,32},{96,64},{128,224},{160,128},{192,160},{224,1... | collective-permute-start | bytes 196616 | tf_op jit(solution)/shard_map/ppermute | solution.py:446
  26.7 15.1 %copy-start.2 = (bf16[128,256]{1,0:T(8,128)(2,1)S(1)}, bf16[128,256]{1,0:T(8,128)(2,1)}, u32[]{:S(2)}) copy-start(bf16[128,256]{1,0:T(8,128)(2,1)} %constant.9.clone.first_ref.refs_5_) | copy-start | bytes 196612
  43.3 8.5 %collective-permute-start.4 = (bf16[256,128]{1,0:T(8,128)(2,1)S(1)}, bf16[256,128]{1,0:T(8,128)(2,1)S(1)}, u32[]{:S(2)}, u32[]{:S(2)}) collective-permute-start(bf16[256,128]{1,0:T(8,128)(2,1)S(1)} %get-tuple-element.53.near_ref), channel_id=1, source_target_pairs={{0,128},{32,160},{64,192},{96,224},{128,0},{160,32},{192,64},{224,... | collective-permute-start | bytes 196616 | tf_op jit(solution)/shard_map/ppermute | solution.py:451
  45.0 14.8 %all-to-all-start.2 = ((bf16[32,32,128]{2,1,0:T(8,128)(2,1)}), bf16[32,32,128]{2,1,0:T(8,128)(2,1)S(1)}, u32[]{:S(2)}, u32[]{:S(2)}) async-start(bf16[32,32,128]{2,1,0:T(8,128)(2,1)} %get-tuple-element.51), calls=%async_computation.2 | async-start | bytes 524288 | tf_op jit(solution)/shard_map/all_to_all | solution.py:433
  51.7 8.2 %copy-start.3 = (bf16[2,16384]{1,0:T(2,128)(2,1)S(1)}, bf16[2,16384]{1,0:T(2,128)(2,1)}, u32[]{:S(2)}) copy-start(bf16[2,16384]{1,0:T(2,128)(2,1)} %refs_3_.1) | copy-start | bytes 196612
  51.7 8.2 %copy-start.4 = (bf16[2,16384]{1,0:T(2,128)(2,1)S(1)}, bf16[2,16384]{1,0:T(2,128)(2,1)}, u32[]{:S(2)}) copy-start(bf16[2,16384]{1,0:T(2,128)(2,1)} %refs_4_.1) | copy-start | bytes 196612
  51.9 4.7 %collective-permute-start.5 = (bf16[256,128]{1,0:T(8,128)(2,1)S(1)}, bf16[256,128]{1,0:T(8,128)(2,1)S(1)}, u32[]{:S(2)}, u32[]{:S(2)}) collective-permute-start(bf16[256,128]{1,0:T(8,128)(2,1)S(1)} %get-tuple-element.55), channel_id=1, source_target_pairs={{0,32},{32,64},{64,96},{96,0},{128,160},{160,192},{192,224},{224,1... | collective-permute-start | bytes 196616 | tf_op jit(solution)/shard_map/ppermute | solution.py:446
  52.0 6.3 %collective-permute-start.6 = (bf16[256,128]{1,0:T(8,128)(2,1)S(1)}, bf16[256,128]{1,0:T(8,128)(2,1)S(1)}, u32[]{:S(2)}, u32[]{:S(2)}) collective-permute-start(bf16[256,128]{1,0:T(8,128)(2,1)S(1)} %get-tuple-element.56), channel_id=1, source_target_pairs={{0,64},{32,96},{64,0},{96,32},{128,192},{160,224},{192,128},{224,1... | collective-permute-start | bytes 196616 | tf_op jit(solution)/shard_map/ppermute | solution.py:446
  55.4 3.8 %collective-permute-start.7 = (bf16[256,128]{1,0:T(8,128)(2,1)S(1)}, bf16[256,128]{1,0:T(8,128)(2,1)S(1)}, u32[]{:S(2)}, u32[]{:S(2)}) collective-permute-start(bf16[256,128]{1,0:T(8,128)(2,1)S(1)} %get-tuple-element.57), channel_id=1, source_target_pairs={{0,96},{32,0},{64,32},{96,64},{128,224},{160,128},{192,160},{224,1... | collective-permute-start | bytes 196616 | tf_op jit(solution)/shard_map/ppermute | solution.py:446

commit v8 on v6

--- a/solution.py
+++ b/solution.py
@@ -15,8 +15,8 @@
 WEIGHTS = RING * CH * 2 * CH
 TILE = 4
 ORDER = (
-    19, 23, 29, 26, 5, 17, 30, 10, 25, 16, 0, 3, 4, 14, 22, 6,
-    24, 8, 13, 21, 18, 27, 15, 31, 20, 12, 1, 2, 9, 11, 28, 7,
+    19, 23, 2, 26, 27, 5, 25, 10, 3, 16, 4, 6, 30, 14, 22, 0,
+    24, 8, 13, 21, 12, 17, 15, 31, 20, 29, 1, 18, 9, 11, 28, 7,
 )
 PLACE = tuple(ORDER.index(block) for block in range(len(ORDER)))
 BLOCKS = 32

time: 61.6 us -> 61.6 us (level)
  transfers between devices with their start and end apart: 10 -> 10, of which waited for: 6 -> 7; matrix products, arithmetic and copies ran while one was open for 0% -> 0% of each run, Pallas kernels for 2% -> 2%
where the time goes in v8:
time: 61.6 us; the launch traced here: 61.3 us
  starting transfers between devices  31 us (50%)
  blocking collectives  15.6 us (25%)
  Pallas kernels  7.04 us (11%)
  waiting for transfers between devices  6.74 us (11%)
  between operations  0.8 us (1%)
    all_to_all x1, blocking collectives, exchange(): lax.all_to_all(blocks, 'seq', split_axis=0, concat_axis=0, tiled=True, ax...  15.6 us
    all_to_all x2, starting transfers between devices, exchange(): lax.all_to_all(blocks, 'seq', split_axis=0, concat_axis=0, tiled=True, ax...  13.5 us
    ppermute x2, starting transfers between devices, across(): lax.ppermute(array, 'tensor', [(i, (i + RING) % GROUP) for i in range(GRO...  8.94 us
    ppermute x6, starting transfers between devices, along_y(): received.append(lax.ppermute(array, 'tensor', pairs))  8.6 us
    pallas_call x8, Pallas kernels, call(): pl.pallas_call(kernel, out_shape=[jax.ShapeDtypeStruct(shape, dtype) for...  7.04 us
    ppermute x6, waiting for transfers between devices, along_y(): received.append(lax.ppermute(array, 'tensor', pairs))  6.15 us
  transfers between devices with their start and end apart: 10, of which 7 were waited for; matrix products, arithmetic and copies ran while one was open for 0% of the time, Pallas kernels for 2%

profile of v8, /device:TPU:1, one launch (start us, length us, event | category | flops | bytes accessed | tf_op | source)
XLA Modules:
  0.0 61.3 jit_solution(14974308105842116040)
XLA Ops:
  0.6 2.3 %shard_map.146 = (f32[72,128]{1,0:T(8,128)S(1)}, bf16[256,128]{1,0:T(8,128)(2,1)S(1)}, bf16[32,32,128]{2,1,0:T(8,128)(2,1)}) custom-call(bf16[2,16384]{1,0:T(2,128)(2,1)} %refs_3_.1, bf16[2,16384]{1,0:T(2,128)(2,1)} %refs_4_.1, bf16[2,16384]{1,0:T(2,128)(2,1)} %taps_hbm.1, bf16[16,16]{1,0:T(8,128)(2,1)} %weight_hbm.1, f32[2]{0:T(128)} %skip_hbm.1, ...), custom_call_target="tpu_custom_call" | custom-call | tf_op jit(solution)/shard_map/pallas_call | solution.py:419
  3.0 7.8 %collective-permute-start = (bf16[2,16384]{1,0:T(2,128)(2,1)S(1)}, bf16[2,16384]{1,0:T(2,128)(2,1)S(1)}, u32[]{:S(2)}, u32[]{:S(2)}) collective-permute-start(bf16[2,16384]{1,0:T(2,128)(2,1)S(1)} %copy-done.7), channel_id=1, source_target_pairs={{0,128},{32,160},{64,192},{96,224},{128,0},{160,32},{192,64},{224,... | collective-permute-start | bytes 196616 | tf_op jit(solution)/shard_map/ppermute | solution.py:449
  10.8 7.4 %all-to-all-start = ((bf16[32,32,128]{2,1,0:T(8,128)(2,1)}), bf16[32,32,128]{2,1,0:T(8,128)(2,1)S(1)}, u32[]{:S(2)}, u32[]{:S(2)}) async-start(bf16[32,32,128]{2,1,0:T(8,128)(2,1)} %get-tuple-element.35), calls=%async_computation | async-start | bytes 524288 | tf_op jit(solution)/shard_map/all_to_all | solution.py:431
  18.2 0.0 copy-start
  18.2 0.0 copy-start.1
  18.2 0.0 copy-start.4
  18.2 0.0 copy-start.5
  18.2 0.2 shard_map.147
  18.4 1.4 %collective-permute-start.1 = (bf16[256,128]{1,0:T(8,128)(2,1)S(1)}, bf16[256,128]{1,0:T(8,128)(2,1)S(1)}, u32[]{:S(2)}, u32[]{:S(2)}) collective-permute-start(bf16[256,128]{1,0:T(8,128)(2,1)S(1)} %get-tuple-element.38), channel_id=1, source_target_pairs={{0,32},{32,64},{64,96},{96,0},{128,160},{160,192},{192,224},{224,1... | collective-permute-start | bytes 196616 | tf_op jit(solution)/shard_map/ppermute | solution.py:444
  19.7 2.6 %collective-permute-start.2 = (bf16[256,128]{1,0:T(8,128)(2,1)S(1)}, bf16[256,128]{1,0:T(8,128)(2,1)S(1)}, u32[]{:S(2)}, u32[]{:S(2)}) collective-permute-start(bf16[256,128]{1,0:T(8,128)(2,1)S(1)} %get-tuple-element.39), channel_id=1, source_target_pairs={{0,64},{32,96},{64,0},{96,32},{128,192},{160,224},{192,128},{224,1... | collective-permute-start | bytes 196616 | tf_op jit(solution)/shard_map/ppermute | solution.py:444
  22.4 1.1 %collective-permute-start.3 = (bf16[256,128]{1,0:T(8,128)(2,1)S(1)}, bf16[256,128]{1,0:T(8,128)(2,1)S(1)}, u32[]{:S(2)}, u32[]{:S(2)}) collective-permute-start(bf16[256,128]{1,0:T(8,128)(2,1)S(1)} %get-tuple-element.40), channel_id=1, source_target_pairs={{0,96},{32,0},{64,32},{96,64},{128,224},{160,128},{192,160},{224,1... | collective-permute-start | bytes 196616 | tf_op jit(solution)/shard_map/ppermute | solution.py:444
  23.4 2.2 %collective-permute-done.2.r2_ref = bf16[256,128]{1,0:T(8,128)(2,1)S(1)} collective-permute-done((bf16[256,128]{1,0:T(8,128)(2,1)S(1)}, bf16[256,128]{1,0:T(8,128)(2,1)S(1)}, u32[]{:S(2)}, u32[]{:S(2)}) %collective-permute-start.2) | collective-permute-done | bytes 65568 | tf_op jit(solution)/shard_map/ppermute | solution.py:444
  25.6 0.1 collective-permute-done.3.r3_ref
  25.8 0.4 shard_map.148
  26.2 0.0 all-to-all-done.spec_ref
  26.2 0.5 shard_map.149
  26.8 0.0 copy-start.6
  26.8 15.6 %all_to_all.15.rows_ref = bf16[32,32,128]{2,1,0:T(8,128)(2,1)S(1)} all-to-all(bf16[32,32,128]{2,1,0:T(8,128)(2,1)S(1)} %get-tuple-element.43), channel_id=1, replica_groups={{19,23,2,26,27,5,25,10,3,16,4,6,30,14,22,0,24,8,13,21,12,17,15,31,20,29..., dimensions={0} | all-to-all | bytes 524288 | tf_op jit(solution)/shard_map/all_to_all | solution.py:431
  42.4 1.4 %shard_map.150 = (bf16[256,128]{1,0:T(8,128)(2,1)S(1)}, f32[256,128]{1,0:T(8,128)S(1)}, bf16[32,32,128]{2,1,0:T(8,128)(2,1)S(1)}, bf16[2,16384]{1,0:T(2,128)(2,1)S(1)}) custom-call(f32[72,128]{1,0:T(8,128)S(1)} %get-tuple-element.33.table_ref.refs_0_, bf16[32,32,128]{2,1,0:T(8,128)(2,1)S(1)} %all_to_all.15.rows_ref, ...), custom_call_target="tpu_custom_call" | custom-call | tf_op jit(solution)/shard_map/pallas_call | solution.py:419
  43.8 1.1 %collective-permute-start.4 = (bf16[256,128]{1,0:T(8,128)(2,1)S(1)}, bf16[256,128]{1,0:T(8,128)(2,1)S(1)}, u32[]{:S(2)}, u32[]{:S(2)}) collective-permute-start(bf16[256,128]{1,0:T(8,128)(2,1)S(1)} %get-tuple-element.51.near_ref), channel_id=1, source_target_pairs={{0,128},{32,160},{64,192},{96,224},{128,0},{160,32},{192,64},{224,... | collective-permute-start | bytes 196616 | tf_op jit(solution)/shard_map/ppermute | solution.py:449
  44.9 0.7 %shard_map.151 = (bf16[32,32,128]{2,1,0:T(8,128)(2,1)}, bf16[2,16384]{1,0:T(2,128)(2,1)}) custom-call(f32[2,2,32,8,128]{4,3,2,1,0:T(8,128)S(1)} %get-tuple-element.42.loaded_ref, bf16[32,32,128]{2,1,0:T(8,128)(2,1)S(1)} %all_to_all.15.rows_ref, f32[256,128]{1,0:T(8,128)S(1)} %get-tuple-element.46.inner_sum_ref, f32[256,128]{1,0:T(8,128)S(1)} %get-tuple-element.45.gated_ref, ...), custom_call_target="tpu_custom_call" | custom-call | tf_op jit(solution)/shard_map/pallas_call | solution.py:419
  45.6 6.1 %all-to-all-start.2 = ((bf16[32,32,128]{2,1,0:T(8,128)(2,1)}), bf16[32,32,128]{2,1,0:T(8,128)(2,1)S(1)}, u32[]{:S(2)}, u32[]{:S(2)}) async-start(bf16[32,32,128]{2,1,0:T(8,128)(2,1)} %get-tuple-element.49), calls=%async_computation.2 | async-start | bytes 524288 | tf_op jit(solution)/shard_map/all_to_all | solution.py:431
  51.8 0.0 copy-start.2
  51.8 0.4 collective-permute-done.4.far_ref
  52.2 0.1 shard_map.152
  52.3 0.1 collective-permute-start.5
  52.4 3.4 %collective-permute-start.6 = (bf16[256,128]{1,0:T(8,128)(2,1)S(1)}, bf16[256,128]{1,0:T(8,128)(2,1)S(1)}, u32[]{:S(2)}, u32[]{:S(2)}) collective-permute-start(bf16[256,128]{1,0:T(8,128)(2,1)S(1)} %get-tuple-element.54), channel_id=1, source_target_pairs={{0,64},{32,96},{64,0},{96,32},{128,192},{160,224},{192,128},{224,1... | collective-permute-start | bytes 196616 | tf_op jit(solution)/shard_map/ppermute | solution.py:444
  55.9 1.2 %collective-permute-done.5.refs_9_ = bf16[256,128]{1,0:T(8,128)(2,1)S(1)} collective-permute-done((bf16[256,128]{1,0:T(8,128)(2,1)S(1)}, bf16[256,128]{1,0:T(8,128)(2,1)S(1)}, u32[]{:S(2)}, u32[]{:S(2)}) %collective-permute-start.5) | collective-permute-done | bytes 65568 | tf_op jit(solution)/shard_map/ppermute | solution.py:444
  57.0 1.8 %collective-permute-done.6.refs_10_ = bf16[256,128]{1,0:T(8,128)(2,1)S(1)} collective-permute-done((bf16[256,128]{1,0:T(8,128)(2,1)S(1)}, bf16[256,128]{1,0:T(8,128)(2,1)S(1)}, u32[]{:S(2)}, u32[]{:S(2)}) %collective-permute-start.6) | collective-permute-done | bytes 65568 | tf_op jit(solution)/shard_map/ppermute | solution.py:444
  58.8 0.9 %collective-permute-done.7.refs_11_ = bf16[256,128]{1,0:T(8,128)(2,1)S(1)} collective-permute-done((bf16[256,128]{1,0:T(8,128)(2,1)S(1)}, bf16[256,128]{1,0:T(8,128)(2,1)S(1)}, u32[]{:S(2)}, u32[]{:S(2)}) %collective-permute-start.7) | collective-permute-done | bytes 65568 | tf_op jit(solution)/shard_map/ppermute | solution.py:444
  59.7 0.2 all-to-all-done.2.refs_1_
  59.9 1.4 %shard_map.153 = (bf16[2,16384]{1,0:T(2,128)(2,1)}, bf16[2,16384]{1,0:T(2,128)(2,1)}, bf16[2,16384]{1,0:T(2,128)(2,1)}, f32[2,16384]{1,0:T(2,128)}) custom-call(f32[72,128]{1,0:T(8,128)S(1)} %get-tuple-element.33.table_ref.refs_0_, bf16[32,32,128]{2,1,0:T(8,128)(2,1)S(1)} %all-to-all-done.2.refs_1_, bf16[256,128]{1,0:T(8,128)(2,1)S(1)} %get-tuple-element.50.refs_2_, ...), custom_call_target="tpu_custom_call" | custom-call | tf_op jit(solution)/shard_map/pallas_call | solution.py:419
  (13 shorter events, 0.0 us)
Async XLA Ops:
  0.6 2.3 %copy-start.7 = (bf16[2,16384]{1,0:T(2,128)(2,1)S(1)}, bf16[2,16384]{1,0:T(2,128)(2,1)}, u32[]{:S(2)}) copy-start(bf16[2,16384]{1,0:T(2,128)(2,1)} %near_ref.1) | copy-start | bytes 196612
  3.0 15.2 %collective-permute-start = (bf16[2,16384]{1,0:T(2,128)(2,1)S(1)}, bf16[2,16384]{1,0:T(2,128)(2,1)S(1)}, u32[]{:S(2)}, u32[]{:S(2)}) collective-permute-start(bf16[2,16384]{1,0:T(2,128)(2,1)S(1)} %copy-done.7), channel_id=1, source_target_pairs={{0,128},{32,160},{64,192},{96,224},{128,0},{160,32},{192,64},{224,... | collective-permute-start | bytes 196616 | tf_op jit(solution)/shard_map/ppermute | solution.py:449
  10.8 15.4 %all-to-all-start = ((bf16[32,32,128]{2,1,0:T(8,128)(2,1)}), bf16[32,32,128]{2,1,0:T(8,128)(2,1)S(1)}, u32[]{:S(2)}, u32[]{:S(2)}) async-start(bf16[32,32,128]{2,1,0:T(8,128)(2,1)} %get-tuple-element.35), calls=%async_computation | async-start | bytes 524288 | tf_op jit(solution)/shard_map/all_to_all | solution.py:431
  18.2 7.6 %copy-start = (f32[2,128,128]{2,1,0:T(8,128)S(1)}, f32[2,128,128]{2,1,0:T(8,128)}, u32[]{:S(2)}) copy-start(f32[2,128,128]{2,1,0:T(8,128)} %constant.10.clone.turn_hbm.turn_ref.refs_6_) | copy-start | bytes 393220
  18.2 7.6 %copy-start.1 = (bf16[2,128,128]{2,1,0:T(8,128)(2,1)S(1)}, bf16[2,128,128]{2,1,0:T(8,128)(2,1)}, u32[]{:S(2)}) copy-start(bf16[2,128,128]{2,1,0:T(8,128)(2,1)} %constant.11.clone.second_hbm.second_ref.refs_7_) | copy-start | bytes 196612
  18.2 7.6 %copy-start.4 = (bf16[256,128]{1,0:T(8,128)(2,1)S(1)}, bf16[256,128]{1,0:T(8,128)(2,1)}, u32[]{:S(2)}) copy-start(bf16[256,128]{1,0:T(8,128)(2,1)} %constant.8.clone.first_hbm.first_ref) | copy-start | bytes 196612
  18.2 7.6 %copy-start.5 = (bf16[2,16384]{1,0:T(2,128)(2,1)S(1)}, bf16[2,16384]{1,0:T(2,128)(2,1)}, u32[]{:S(2)}) copy-start(bf16[2,16384]{1,0:T(2,128)(2,1)} %query_ref.3) | copy-start | bytes 196612
  18.4 5.1 %collective-permute-start.1 = (bf16[256,128]{1,0:T(8,128)(2,1)S(1)}, bf16[256,128]{1,0:T(8,128)(2,1)S(1)}, u32[]{:S(2)}, u32[]{:S(2)}) collective-permute-start(bf16[256,128]{1,0:T(8,128)(2,1)S(1)} %get-tuple-element.38), channel_id=1, source_target_pairs={{0,32},{32,64},{64,96},{96,0},{128,160},{160,192},{192,224},{224,1... | collective-permute-start | bytes 196616 | tf_op jit(solution)/shard_map/ppermute | solution.py:444
  19.7 5.9 %collective-permute-start.2 = (bf16[256,128]{1,0:T(8,128)(2,1)S(1)}, bf16[256,128]{1,0:T(8,128)(2,1)S(1)}, u32[]{:S(2)}, u32[]{:S(2)}) collective-permute-start(bf16[256,128]{1,0:T(8,128)(2,1)S(1)} %get-tuple-element.39), channel_id=1, source_target_pairs={{0,64},{32,96},{64,0},{96,32},{128,192},{160,224},{192,128},{224,1... | collective-permute-start | bytes 196616 | tf_op jit(solution)/shard_map/ppermute | solution.py:444
  22.4 3.4 %collective-permute-start.3 = (bf16[256,128]{1,0:T(8,128)(2,1)S(1)}, bf16[256,128]{1,0:T(8,128)(2,1)S(1)}, u32[]{:S(2)}, u32[]{:S(2)}) collective-permute-start(bf16[256,128]{1,0:T(8,128)(2,1)S(1)} %get-tuple-element.40), channel_id=1, source_target_pairs={{0,96},{32,0},{64,32},{96,64},{128,224},{160,128},{192,160},{224,1... | collective-permute-start | bytes 196616 | tf_op jit(solution)/shard_map/ppermute | solution.py:444
  26.8 15.6 %copy-start.6 = (bf16[128,256]{1,0:T(8,128)(2,1)S(1)}, bf16[128,256]{1,0:T(8,128)(2,1)}, u32[]{:S(2)}) copy-start(bf16[128,256]{1,0:T(8,128)(2,1)} %constant.9.clone.first_ref.refs_5_) | copy-start | bytes 196612
  43.8 8.4 %collective-permute-start.4 = (bf16[256,128]{1,0:T(8,128)(2,1)S(1)}, bf16[256,128]{1,0:T(8,128)(2,1)S(1)}, u32[]{:S(2)}, u32[]{:S(2)}) collective-permute-start(bf16[256,128]{1,0:T(8,128)(2,1)S(1)} %get-tuple-element.51.near_ref), channel_id=1, source_target_pairs={{0,128},{32,160},{64,192},{96,224},{128,0},{160,32},{192,64},{224,... | collective-permute-start | bytes 196616 | tf_op jit(solution)/shard_map/ppermute | solution.py:449
  45.6 14.2 %all-to-all-start.2 = ((bf16[32,32,128]{2,1,0:T(8,128)(2,1)}), bf16[32,32,128]{2,1,0:T(8,128)(2,1)S(1)}, u32[]{:S(2)}, u32[]{:S(2)}) async-start(bf16[32,32,128]{2,1,0:T(8,128)(2,1)} %get-tuple-element.49), calls=%async_computation.2 | async-start | bytes 524288 | tf_op jit(solution)/shard_map/all_to_all | solution.py:431
  51.8 8.1 %copy-start.2 = (bf16[2,16384]{1,0:T(2,128)(2,1)S(1)}, bf16[2,16384]{1,0:T(2,128)(2,1)}, u32[]{:S(2)}) copy-start(bf16[2,16384]{1,0:T(2,128)(2,1)} %refs_3_.1) | copy-start | bytes 196612
  51.8 8.1 %copy-start.3 = (bf16[2,16384]{1,0:T(2,128)(2,1)S(1)}, bf16[2,16384]{1,0:T(2,128)(2,1)}, u32[]{:S(2)}) copy-start(bf16[2,16384]{1,0:T(2,128)(2,1)} %refs_4_.1) | copy-start | bytes 196612
  52.3 4.7 %collective-permute-start.5 = (bf16[256,128]{1,0:T(8,128)(2,1)S(1)}, bf16[256,128]{1,0:T(8,128)(2,1)S(1)}, u32[]{:S(2)}, u32[]{:S(2)}) collective-permute-start(bf16[256,128]{1,0:T(8,128)(2,1)S(1)} %get-tuple-element.53), channel_id=1, source_target_pairs={{0,32},{32,64},{64,96},{96,0},{128,160},{160,192},{192,224},{224,1... | collective-permute-start | bytes 196616 | tf_op jit(solution)/shard_map/ppermute | solution.py:444
  52.4 6.4 %collective-permute-start.6 = (bf16[256,128]{1,0:T(8,128)(2,1)S(1)}, bf16[256,128]{1,0:T(8,128)(2,1)S(1)}, u32[]{:S(2)}, u32[]{:S(2)}) collective-permute-start(bf16[256,128]{1,0:T(8,128)(2,1)S(1)} %get-tuple-element.54), channel_id=1, source_target_pairs={{0,64},{32,96},{64,0},{96,32},{128,192},{160,224},{192,128},{224,1... | collective-permute-start | bytes 196616 | tf_op jit(solution)/shard_map/ppermute | solution.py:444
  55.9 3.8 %collective-permute-start.7 = (bf16[256,128]{1,0:T(8,128)(2,1)S(1)}, bf16[256,128]{1,0:T(8,128)(2,1)S(1)}, u32[]{:S(2)}, u32[]{:S(2)}) collective-permute-start(bf16[256,128]{1,0:T(8,128)(2,1)S(1)} %get-tuple-element.55), channel_id=1, source_target_pairs={{0,96},{32,0},{64,32},{96,64},{128,224},{160,128},{192,160},{224,1... | collective-permute-start | bytes 196616 | tf_op jit(solution)/shard_map/ppermute | solution.py:444
